TPU v7x, 128 devices: a whole 4x4x4 slice. The times are simulated.
128 devices in a mesh: facet: 32 (over x, z, core), col: 4 (over y).
Axes of the slice: x: 4, y: 4, z: 4, core: 2. Of those that a mesh axis runs over, the one named last changes fastest.
Arguments:
- facets: bfloat16 [2, 32768, 1024], P(None, ('facet', 'col')), may hold values from -6 to 6
- observed: float32 [2, 128, 1024], P(None, 'col'), may hold values from -6 to 6
- uv_cells: int32 [2, 128, 1024], P(None, 'col'), may hold values from 0 to 511
- counts: int32 [128], P('col'), may hold values from 64 to 1024, as said below
Outputs:
- facet_residual: float32 [2, 32768, 1024], P(None, ('facet', 'col'))
Inputs may be any that keep to these rules, and one draw needn't show every extreme that they name: Live slots of a subgrid are its first counts[s] slots; in every column some subgrid has all 1024 slots live.
All inputs are finite; a program needn't handle non-finite values.
Results may differ from a plain program's by a relative error of at most 0.008.
Values may be sent and summed in bfloat16 or wider, within the bound.
No kernel may reach another device: no remote copies, remote signals or barrier semaphores. Data moves between devices by JAX's collectives and lax.ppermute only.
A program may use at most 64 MiB of HBM per device.

v0:
```python
import math

import jax
import jax.numpy as jnp
import ml_dtypes
import numpy as np
from jax import lax
from jax.experimental import pallas as pl
from jax.experimental.pallas import tpu as pltpu
from jax.sharding import Mesh
from jax.sharding import PartitionSpec as P

F = 1024
S = 512
IMAGE = 65536
VIS = 1024
W = 64
SUBCOL = 32
N_COL = 4
FACET = ("facet_0", "facet_1", "facet_2")
FACET_COL = ("facet_0", "facet_1", "facet_2", "col")
BF = jnp.bfloat16
F32 = jnp.float32


def unit(ticks, modulus):
    angle = (ticks % modulus).astype(np.float64) * (-2.0 * math.pi / modulus)
    return np.cos(angle), np.sin(angle)


def taper():
    return 0.6 + 0.4 * np.sin(math.pi * (np.arange(F) + 0.5) / F) ** 2


def bf(values):
    return np.asarray(values, np.float32).astype(ml_dtypes.bfloat16)


def hi_lo(values):
    high = bf(values)
    return high, bf(values - high.astype(np.float64))


def column_rows():
    c, l, q = np.arange(N_COL), np.arange(W), np.arange(F)
    vc = c * (IMAGE // 4) + (29 * c + 3) % 64
    ticks = q[None, None, :] * (vc[:, None, None] + 64 * l[None, :, None])
    real, imag = unit(ticks, IMAGE)
    weights = taper() / math.sqrt(F)
    return bf(np.stack([real * weights, imag * weights], axis=1).reshape(N_COL * 2 * W, F))


def window_rows():
    j, k, p = np.arange(SUBCOL), np.arange(W), np.arange(F)
    freqs = 1024 * (k[None, :] + j[:, None]) + ((37 * j + 5) % 1024)[:, None]
    real, imag = unit(p[None, :] * freqs.reshape(-1, 1), IMAGE)
    weights = taper() / math.sqrt(F)
    return bf(np.stack([real * weights, imag * weights]))


def left_rows():
    real, imag = unit(np.arange(256)[:, None] * np.arange(S)[None, :], S)
    return bf(np.concatenate([real, imag]))


def right_rows():
    base = hi_lo(np.concatenate(unit(np.arange(W)[:, None] * np.arange(S)[None, :], S)))
    eighth = hi_lo(np.concatenate(unit(W * np.arange(8)[:, None] * np.arange(S)[None, :], S)))
    return np.concatenate([base[0], base[1], eighth[0], eighth[1]])


def facet_tables():
    return np.stack(unit(np.arange(W), W)).astype(np.float32)


def dot(a, b):
    return jnp.dot(a, b, preferred_element_type=F32)


def half_sign(shape):
    lane = lax.broadcasted_iota(jnp.int32, shape, len(shape) - 1)
    return jnp.where(lane % 128 < W, -1.0, 1.0).astype(F32)


def swap(values):
    return pltpu.roll(values, W, 1)


def scalar_phase(units, facet_row, facet_col, subgrid, column):
    shift = (37 * subgrid + 5) & 1023
    anchor = (29 * column + 3) & 63
    tick = (facet_row * shift + facet_col * anchor) & 63
    return units[0, tick], units[1, tick]


def strip_kernel(pixels, table, out):
    real = dot(pixels[0], table[...])
    imag = dot(pixels[1], table[...])
    sign = half_sign((256, 128))
    for c in range(N_COL):
        at = slice(c * 128, (c + 1) * 128)
        out[c] = (real[:, at] + sign * swap(imag[:, at])).astype(BF)


def window_kernel(units, table, strip, out):
    facet = lax.axis_index(FACET)
    column = lax.axis_index("col")
    step = pl.program_id(0)
    group = out.shape[0]
    rows = group * W
    both = dot(table[...].reshape(2 * rows, F), strip[...].reshape(F, 128))
    sign = half_sign((W, 128))
    for g in range(group):
        at = slice(g * W, (g + 1) * W)
        block = both[:rows][at] + sign * swap(both[rows:][at])
        real, imag = scalar_phase(units, facet // 8, facet % 8, step * group + g, column)
        out[g] = (block * real + sign * swap(block) * imag).astype(BF)


def subgrid_kernel(units, counts, windows, observed, cells, left_tab, right_tab, out, left, weighted):
    subgrid = lax.axis_index(FACET)
    column = lax.axis_index("col")
    count = counts[subgrid]
    turned = []
    for y in range(8):
        block = jnp.concatenate([windows[x * 8 + y] for x in range(4)], axis=0)
        block = block.astype(F32).T
        other = jnp.concatenate([-block[W:], block[:W]], axis=0)
        turned.append(jnp.concatenate([block, other], axis=1).astype(BF))
    chunk = 256
    for begin in range(0, VIS, chunk):
        at = slice(begin, begin + chunk)
        first = cells[0, pl.ds(subgrid, 1), at]
        second = cells[1, pl.ds(subgrid, 1), at]
        cell = lax.broadcasted_iota(jnp.int32, (S, chunk), 0)
        left_part = dot(left_tab[...], jnp.where(cell == first, 1.0, 0.0).astype(BF)).astype(BF)
        left[:, at] = left_part
        right = dot(right_tab[...], jnp.where(cell == second, 1.0, 0.0).astype(BF))
        base_real = right[0:64] + right[128:192]
        base_imag = right[64:128] + right[192:256]
        eighth_real = right[256:264] + right[272:280]
        eighth_imag = right[264:272] + right[280:288]
        pred_real = jnp.zeros((1, chunk), F32)
        pred_imag = jnp.zeros((1, chunk), F32)
        for y in range(8):
            inner = dot(turned[y], left_part)
            inner_real, inner_imag = inner[:W], inner[W:]
            part_real = jnp.sum(inner_real * base_real - inner_imag * base_imag, axis=0, keepdims=True)
            part_imag = jnp.sum(inner_real * base_imag + inner_imag * base_real, axis=0, keepdims=True)
            er, ei = eighth_real[y : y + 1], eighth_imag[y : y + 1]
            pred_real += part_real * er - part_imag * ei
            pred_imag += part_real * ei + part_imag * er
        slot = begin + lax.broadcasted_iota(jnp.int32, (1, chunk), 1)
        live = slot < count
        resid_real = jnp.where(live, observed[0, pl.ds(subgrid, 1), at] - pred_real / S, 0.0)
        resid_imag = jnp.where(live, observed[1, pl.ds(subgrid, 1), at] - pred_imag / S, 0.0)
        for y in range(8):
            er, ei = eighth_real[y : y + 1], eighth_imag[y : y + 1]
            turned_real = resid_real * er + resid_imag * ei
            turned_imag = resid_imag * er - resid_real * ei
            weighted[y * 128 : y * 128 + W, at] = (
                turned_real * base_real + turned_imag * base_imag
            ).astype(BF)
            weighted[y * 128 + W : (y + 1) * 128, at] = (
                turned_imag * base_real - turned_real * base_imag
            ).astype(BF)
    sign = half_sign((W, 128))
    for y in range(8):
        both = lax.dot_general(
            left[...],
            weighted[y * 128 : (y + 1) * 128],
            (((1,), (1,)), ((), ())),
            preferred_element_type=F32,
        )
        for x in range(4):
            block = both[x * W : (x + 1) * W] - sign * swap(both[256 + x * W : 256 + (x + 1) * W])
            real, imag = scalar_phase(units, x, y, subgrid, column)
            scale = 1.0 / math.sqrt(VIS)
            out[x * 8 + y] = (
                block * (real * scale) - sign * swap(block) * (imag * scale)
            ).astype(BF)


def back_kernel(table, returned, out, turned):
    @pl.when(pl.program_id(0) == 0)
    def _():
        for g in range(8):
            block = returned[g * 4 : (g + 1) * 4].reshape(256, 128)
            turned[:, g * 256 : (g + 1) * 256] = block.astype(F32).T.astype(BF)

    real = dot(turned[...], table[0])
    imag = dot(turned[...], table[1])
    out[0, :W] = (real[:W] + imag[W:]).astype(BF)
    out[0, W:] = (real[W:] - imag[:W]).astype(BF)


def image_kernel(strips, table, out):
    rows, others = [], []
    for c in range(N_COL):
        block = strips[c].astype(F32)
        other = jnp.concatenate([block[W:], -block[:W]], axis=0)
        rows.append(block.T.astype(BF))
        others.append(other.T.astype(BF))
    out[0] = dot(jnp.concatenate(rows, axis=1), table[...])
    out[1] = dot(jnp.concatenate(others, axis=1), table[...])


VMEM = pl.BlockSpec(memory_space=pltpu.VMEM)
SMEM = pl.BlockSpec(memory_space=pltpu.SMEM)


def params():
    return pltpu.CompilerParams(vmem_limit_bytes=48 * 1024 * 1024)


def on_device(facets, observed, uv_cells, counts):
    units = jnp.asarray(facet_tables())
    by_column = column_rows()
    row_tab = jnp.asarray(window_rows())
    strips = pl.pallas_call(
        strip_kernel,
        out_shape=jax.ShapeDtypeStruct((N_COL, 256, 128), BF),
        in_specs=[VMEM, VMEM],
        out_specs=VMEM,
        compiler_params=params(),
        name="strip",
    )(facets, jnp.asarray(np.ascontiguousarray(by_column.T)))
    strip = lax.all_to_all(strips, "col", split_axis=0, concat_axis=0, tiled=True)
    windows = pl.pallas_call(
        window_kernel,
        grid=(8,),
        out_shape=jax.ShapeDtypeStruct((SUBCOL, W, 128), BF),
        in_specs=[SMEM, pl.BlockSpec((2, 256, F), lambda i: (0, i, 0)), VMEM],
        out_specs=pl.BlockSpec((4, W, 128), lambda i: (i, 0, 0)),
        compiler_params=params(),
        name="window",
    )(units, row_tab, strip)
    windows = lax.all_to_all(windows, FACET, split_axis=0, concat_axis=0, tiled=True)
    returned = pl.pallas_call(
        subgrid_kernel,
        out_shape=jax.ShapeDtypeStruct((SUBCOL, W, 128), BF),
        in_specs=[SMEM, SMEM, VMEM, VMEM, VMEM, VMEM, VMEM],
        out_specs=VMEM,
        scratch_shapes=[pltpu.VMEM((S, VIS), BF), pltpu.VMEM((1024, VIS), BF)],
        compiler_params=params(),
        name="subgrid",
    )(units, counts, windows, observed, uv_cells, jnp.asarray(left_rows()), jnp.asarray(right_rows()))
    returned = lax.all_to_all(returned, FACET, split_axis=0, concat_axis=0, tiled=True)
    back = pl.pallas_call(
        back_kernel,
        grid=(4,),
        out_shape=jax.ShapeDtypeStruct((N_COL, 128, 256), BF),
        in_specs=[pl.BlockSpec((2, SUBCOL * W, 256), lambda i: (0, 0, i)), VMEM],
        out_specs=pl.BlockSpec((1, 128, 256), lambda i: (i, 0, 0)),
        scratch_shapes=[pltpu.VMEM((128, SUBCOL * W), BF)],
        compiler_params=params(),
        name="back",
    )(row_tab, returned)
    back = lax.all_to_all(back, "col", split_axis=0, concat_axis=0, tiled=True)
    return pl.pallas_call(
        image_kernel,
        out_shape=jax.ShapeDtypeStruct((2, 256, F), F32),
        in_specs=[VMEM, VMEM],
        out_specs=VMEM,
        compiler_params=params(),
        name="image",
    )(back, jnp.asarray(by_column))


def solution(mesh):
    finer = Mesh(
        mesh.devices.reshape(4, 4, 2, mesh.shape["col"]), ("facet_0", "facet_1", "facet_2", "col")
    )
    return jax.shard_map(
        on_device,
        mesh=finer,
        in_specs=(P(None, FACET_COL, None), P(None, "col", None), P(None, "col", None), P("col")),
        out_specs=P(None, FACET_COL, None),
        check_vma=False,
    )
```

profile of v0, /device:TPU:1, one launch (start us, length us, event | category | flops | bytes accessed | tf_op | source)
XLA Modules:
  0.0 81.4 jit_solution(10877115243072714021)
XLA Ops:
  0.0 0.0 copy-start
  0.0 1.2 %copy-done = bf16[2,256,1024]{2,1,0:T(8,128)(2,1)S(1)} copy-done((bf16[2,256,1024]{2,1,0:T(8,128)(2,1)S(1)}, bf16[2,256,1024]{2,1,0:T(8,128)(2,1)}, u32[]{:S(2)}) %copy-start) | copy-done | bytes 1048600
  1.2 0.0 copy-start.2
  1.2 1.2 %copy-done.2 = bf16[1024,512]{1,0:T(8,128)(2,1)S(1)} copy-done((bf16[1024,512]{1,0:T(8,128)(2,1)S(1)}, bf16[1024,512]{1,0:T(8,128)(2,1)}, u32[]{:S(2)}) %copy-start.2) | copy-done | bytes 1048600
  2.5 0.0 copy-start.3
  2.5 0.0 copy-start.4
  2.5 0.0 copy-start.5
  2.5 0.0 copy-start.6
  2.5 0.0 copy-start.8
  2.5 0.8 %strip.1 = bf16[4,256,128]{2,1,0:T(8,128)(2,1)S(1)} custom-call(bf16[2,256,1024]{2,1,0:T(8,128)(2,1)S(1)} %copy-done, bf16[1024,512]{1,0:T(8,128)(2,1)S(1)} %copy-done.2), custom_call_target="tpu_custom_call" | custom-call | tf_op jit(solution)/shard_map/strip/pallas_call | solution.py:220
  3.3 10.4 %all_to_all.20.strip = bf16[4,256,128]{2,1,0:T(8,128)(2,1)S(1)} all-to-all(bf16[4,256,128]{2,1,0:T(8,128)(2,1)S(1)} %strip.1), channel_id=1, replica_groups=mesh['facet_0'=4,'facet_1'=4,'facet_2'=2,'col'=4] {'col'}, dimensions={0} | all-to-all | bytes 524288 | tf_op jit(solution)/shard_map/all_to_all | solution.py:228
  13.7 0.0 copy-start.7
  13.7 0.7 copy-done.7
  14.4 8.1 %window.1 = bf16[32,64,128]{2,1,0:T(8,128)(2,1)S(1)} custom-call(f32[2,64]{1,0:T(2,128)S(1)} %copy-done.7, bf16[2,2048,1024]{2,1,0:T(8,128)(2,1)} %constant.13.clone.table, bf16[4,256,128]{2,1,0:T(8,128)(2,1)S(1)} %all_to_all.20.strip), custom_call_target="tpu_custom_call" | custom-call | tf_op jit(solution)/shard_map/window/pallas_call | solution.py:229
  22.5 0.0 copy-start.1
  22.5 21.6 %all_to_all.21.windows = bf16[32,64,128]{2,1,0:T(8,128)(2,1)S(1)} all-to-all(bf16[32,64,128]{2,1,0:T(8,128)(2,1)S(1)} %window.1), channel_id=1, replica_groups=mesh['facet_0'=4,'facet_1'=4,'facet_2'=2,'col'=4] {'facet_0','facet_1','..., dimensions={0} | all-to-all | bytes 1048576 | tf_op jit(solution)/shard_map/all_to_all | solution.py:238
  44.1 0.0 copy-done.3
  44.1 0.0 copy-done.4
  44.1 0.0 copy-done.5
  44.1 0.0 copy-done.6
  44.1 0.0 copy-done.8
  44.1 5.7 %subgrid.1 = bf16[32,64,128]{2,1,0:T(8,128)(2,1)S(1)} custom-call(f32[2,64]{1,0:T(2,128)S(1)} %copy-done.7, s32[32]{0:T(128)S(1)} %copy-done.8, bf16[32,64,128]{2,1,0:T(8,128)(2,1)S(1)} %all_to_all.21.windows, f32[2,32,1024]{2,1,0:T(8,128)S(1)} %copy-done.5, s32[2,32,1024]{2,1,0:T(8,128)S(1)} %copy-done.6, bf16[512,512]{1,0:T(8,128)(2,1)S(1)} %copy-done.3, ...), custom_call_target="tpu_custom_call" | custom-call | tf_op jit(solution)/shard_map/subgrid/pallas_call | solution.py:239
  49.8 15.1 %all_to_all.22.returned = bf16[32,64,128]{2,1,0:T(8,128)(2,1)S(1)} all-to-all(bf16[32,64,128]{2,1,0:T(8,128)(2,1)S(1)} %subgrid.1), channel_id=1, replica_groups=mesh['facet_0'=4,'facet_1'=4,'facet_2'=2,'col'=4] {'facet_0','facet_1','..., dimensions={0} | all-to-all | bytes 1048576 | tf_op jit(solution)/shard_map/all_to_all | solution.py:248
  64.9 5.1 %back.1 = bf16[4,128,256]{2,1,0:T(8,128)(2,1)S(1)} custom-call(bf16[2,2048,1024]{2,1,0:T(8,128)(2,1)} %constant.13.clone.table, bf16[32,64,128]{2,1,0:T(8,128)(2,1)S(1)} %all_to_all.22.returned), custom_call_target="tpu_custom_call" | custom-call | tf_op jit(solution)/shard_map/back/pallas_call | solution.py:249
  70.0 9.4 %all_to_all.23.strips = bf16[4,128,256]{2,1,0:T(8,128)(2,1)S(1)} all-to-all(bf16[4,128,256]{2,1,0:T(8,128)(2,1)S(1)} %back.1), channel_id=1, replica_groups=mesh['facet_0'=4,'facet_1'=4,'facet_2'=2,'col'=4] {'col'}, dimensions={0} | all-to-all | bytes 524288 | tf_op jit(solution)/shard_map/all_to_all | solution.py:259
  79.3 0.0 copy-done.1
  79.3 2.1 %image.1 = f32[2,256,1024]{2,1,0:T(8,128)} custom-call(bf16[4,128,256]{2,1,0:T(8,128)(2,1)S(1)} %all_to_all.23.strips, bf16[512,1024]{1,0:T(8,128)(2,1)S(1)} %copy-done.1), custom_call_target="tpu_custom_call" | custom-call | tf_op jit(solution)/shard_map/image/pallas_call | solution.py:260
Async XLA Ops:
  0.0 1.2 %copy-start = (bf16[2,256,1024]{2,1,0:T(8,128)(2,1)S(1)}, bf16[2,256,1024]{2,1,0:T(8,128)(2,1)}, u32[]{:S(2)}) copy-start(bf16[2,256,1024]{2,1,0:T(8,128)(2,1)} %pixels.1) | copy-start | bytes 3145732
  1.2 1.2 %copy-start.2 = (bf16[1024,512]{1,0:T(8,128)(2,1)S(1)}, bf16[1024,512]{1,0:T(8,128)(2,1)}, u32[]{:S(2)}) copy-start(bf16[1024,512]{1,0:T(8,128)(2,1)} %constant.14.clone.table) | copy-start | bytes 3145732
  2.5 41.6 %copy-start.3 = (bf16[512,512]{1,0:T(8,128)(2,1)S(1)}, bf16[512,512]{1,0:T(8,128)(2,1)}, u32[]{:S(2)}) copy-start(bf16[512,512]{1,0:T(8,128)(2,1)} %constant.15.clone.left_tab) | copy-start | bytes 1572868
  2.5 41.6 %copy-start.4 = (bf16[288,512]{1,0:T(8,128)(2,1)S(1)}, bf16[288,512]{1,0:T(8,128)(2,1)}, u32[]{:S(2)}) copy-start(bf16[288,512]{1,0:T(8,128)(2,1)} %constant.16.clone.right_tab) | copy-start | bytes 884740
  2.5 41.6 %copy-start.5 = (f32[2,32,1024]{2,1,0:T(8,128)S(1)}, f32[2,32,1024]{2,1,0:T(8,128)}, u32[]{:S(2)}) copy-start(f32[2,32,1024]{2,1,0:T(8,128)} %observed.1) | copy-start | bytes 786436
  2.5 41.6 %copy-start.6 = (s32[2,32,1024]{2,1,0:T(8,128)S(1)}, s32[2,32,1024]{2,1,0:T(8,128)}, u32[]{:S(2)}) copy-start(s32[2,32,1024]{2,1,0:T(8,128)} %cells.1) | copy-start | bytes 786436
  2.5 41.6 %copy-start.8 = (s32[32]{0:T(128)S(1)}, s32[32]{0:T(128)}, u32[]{:S(2)}) copy-start(s32[32]{0:T(128)} %counts.1) | copy-start | bytes 388
  13.7 0.7 copy-start.7
  22.5 56.8 %copy-start.1 = (bf16[512,1024]{1,0:T(8,128)(2,1)S(1)}, bf16[512,1024]{1,0:T(8,128)(2,1)}, u32[]{:S(2)}) copy-start(bf16[512,1024]{1,0:T(8,128)(2,1)} %constant.17.clone.table) | copy-start | bytes 3145732
where the time goes:
time: 81.9 us; the launch traced here: 81.4 us
  blocking collectives  56.3 us (69%)
  Pallas kernels  21.8 us (27%)
  local copies, waits for them, and re-layouts  3.15 us (4%)
    all_to_all x1, blocking collectives, on_device(): lax.all_to_all(windows, FACET, split_axis=0, concat_axis=0, tiled=True)  21.6 us
    all_to_all x1, blocking collectives, on_device(): lax.all_to_all(returned, FACET, split_axis=0, concat_axis=0, tiled=True)  15.1 us
    all_to_all x1, blocking collectives, on_device(): lax.all_to_all(strips, 'col', split_axis=0, concat_axis=0, tiled=True)  10.4 us
    all_to_all x1, blocking collectives, on_device(): back = lax.all_to_all(back, 'col', split_axis=0, concat_axis=0, tiled=True)  9.35 us
    pallas_call x1, Pallas kernels, on_device(): pl.pallas_call(window_kernel, grid=(8,), out_shape=jax.ShapeDtypeStruct((...  8.14 us
    pallas_call x1, Pallas kernels, on_device(): pl.pallas_call(subgrid_kernel, out_shape=jax.ShapeDtypeStruct((SUBCOL, W,...  5.7 us
    pallas_call x1, Pallas kernels, on_device(): pl.pallas_call(back_kernel, grid=(4,), out_shape=jax.ShapeDtypeStruct((N_...  5.06 us
    unnamed x18, local copies, waits for them, and re-layouts  3.15 us

commit v1 on v0

v1 whole, which is shorter than its diff:
```python
import math

import jax
import jax.numpy as jnp
import ml_dtypes
import numpy as np
from jax import lax
from jax.experimental import pallas as pl
from jax.experimental.pallas import tpu as pltpu
from jax.sharding import Mesh
from jax.sharding import PartitionSpec as P

F = 1024
S = 512
IMAGE = 65536
VIS = 1024
W = 64
SUBCOL = 32
N_COL = 4
FACET = ("facet_0", "facet_1", "facet_2")
FACET_COL = ("facet_0", "facet_1", "facet_2", "col")
BF = jnp.bfloat16
F32 = jnp.float32
PIECES = 4
CHUNK = 256
COST = pl.CostEstimate(flops=2 * 10**10, bytes_accessed=2**24, transcendentals=0)


def unit(ticks, modulus):
    angle = (ticks % modulus).astype(np.float64) * (-2.0 * math.pi / modulus)
    return np.cos(angle), np.sin(angle)


def taper():
    return 0.6 + 0.4 * np.sin(math.pi * (np.arange(F) + 0.5) / F) ** 2


def bf(values):
    return np.asarray(values, np.float32).astype(ml_dtypes.bfloat16)


def hi_lo(values):
    high = bf(values)
    return high, bf(values - high.astype(np.float64))


def column_rows():
    c, l, q = np.arange(N_COL), np.arange(W), np.arange(F)
    vc = c * (IMAGE // 4) + (29 * c + 3) % 64
    ticks = q[None, None, :] * (vc[:, None, None] + 64 * l[None, :, None])
    real, imag = unit(ticks, IMAGE)
    weights = taper() / math.sqrt(F)
    return bf(np.stack([real * weights, imag * weights], axis=1).reshape(N_COL * 2 * W, F))


def window_rows():
    j, k, p = np.arange(SUBCOL), np.arange(W), np.arange(F)
    freqs = 1024 * (k[None, :] + j[:, None]) + ((37 * j + 5) % 1024)[:, None]
    real, imag = unit(p[None, :] * freqs.reshape(-1, 1), IMAGE)
    weights = taper() / math.sqrt(F)
    return bf(np.stack([real * weights, imag * weights]))


def left_rows():
    real, imag = unit(np.arange(256)[:, None] * np.arange(S)[None, :], S)
    return bf(np.concatenate([real, imag]))


def right_rows():
    base = hi_lo(np.concatenate(unit(np.arange(W)[:, None] * np.arange(S)[None, :], S)))
    eighth = hi_lo(np.concatenate(unit(W * np.arange(8)[:, None] * np.arange(S)[None, :], S)))
    return np.concatenate([base[0], base[1], eighth[0], eighth[1]])


def facet_tables():
    return np.stack(unit(np.arange(W), W)).astype(np.float32)


def dot(a, b):
    return jnp.dot(a, b, preferred_element_type=F32)


def half_sign(shape):
    lane = lax.broadcasted_iota(jnp.int32, shape, len(shape) - 1)
    return jnp.where(lane % 128 < W, -1.0, 1.0).astype(F32)


def swap(values):
    return pltpu.roll(values, W, 1)


def scalar_phase(units, facet_row, facet_col, subgrid, column):
    shift = (37 * subgrid + 5) & 1023
    anchor = (29 * column + 3) & 63
    tick = (facet_row * shift + facet_col * anchor) & 63
    return units[0, tick], units[1, tick]


def column_of(shift):
    return (lax.axis_index("col") + shift) & (N_COL - 1)


def lanes(block, width):
    return pl.ds(pl.multiple_of(block * width, width), width)


def strip_kernel(pixels, table, *refs):
    outs = refs[:N_COL]
    pixels_in, table_in, held, arrived = refs[N_COL:]
    depth = F // PIECES
    copies = []
    for i in range(PIECES):
        at = slice(i * depth, (i + 1) * depth)
        copies.append(
            (
                pltpu.make_async_copy(table.at[at], table_in.at[at], arrived.at[i]),
                pltpu.make_async_copy(
                    pixels.at[:, :, at], pixels_in.at[:, :, at], arrived.at[PIECES + i]
                ),
            )
        )
    for pair in copies[:2]:
        pair[0].start()
        pair[1].start()
    both = jnp.zeros((512, 512), F32)
    for i in range(PIECES):
        copies[i][0].wait()
        copies[i][1].wait()
        if i + 2 < PIECES:
            copies[i + 2][0].start()
            copies[i + 2][1].start()
        at = slice(i * depth, (i + 1) * depth)
        both += dot(pixels_in[:, :, at].reshape(512, depth), table_in[at])
    held[...] = both
    sign = half_sign((256, 128))
    for shift, out in enumerate(outs):
        at = lanes(column_of(shift), 128)
        out[...] = (held[:256, at] + sign * swap(held[256:, at])).astype(BF)


def window_kernel(units, table, *refs):
    strips = refs[:N_COL]
    out, turned = refs[N_COL:]
    facet = lax.axis_index(FACET)
    column = lax.axis_index("col")
    for shift, strip in enumerate(strips):
        turned[:, lanes(column_of(-shift), 256)] = strip[...].astype(F32).T.astype(BF)
    sign = half_sign((W, 128))
    group = 4
    for step in range(SUBCOL // group):
        at = slice(step * group * W, (step + 1) * group * W)
        first, second = dot(turned[...], table[0, :, at]), dot(turned[...], table[1, :, at])
        both = jnp.concatenate([first[:W] - second[W:], first[W:] + second[:W]], axis=0).T
        for g in range(group):
            block = both[g * W : (g + 1) * W]
            real, imag = scalar_phase(units, facet // 8, facet % 8, step * group + g, column)
            out[step * group + g] = (block * real + sign * swap(block) * imag).astype(BF)


def wave_kernel(cells, left_tab, right_tab, left, base, eighth):
    subgrid = lax.axis_index(FACET)
    for begin in range(0, VIS, CHUNK):
        at = slice(begin, begin + CHUNK)
        first = cells[0, pl.ds(subgrid, 1), at]
        second = cells[1, pl.ds(subgrid, 1), at]
        cell = lax.broadcasted_iota(jnp.int32, (S, CHUNK), 0)
        left[:, at] = dot(left_tab[...], jnp.where(cell == first, 1.0, 0.0).astype(BF)).astype(BF)
        right = dot(right_tab[...], jnp.where(cell == second, 1.0, 0.0).astype(BF))
        base[:, at] = right[0:128] + right[128:256]
        eighth[:, at] = right[256:272] + right[272:288]


def subgrid_kernel(units, counts, windows, observed, left, base, eighth, out, weighted):
    subgrid = lax.axis_index(FACET)
    column = lax.axis_index("col")
    count = counts[subgrid]
    turned = []
    for y in range(8):
        block = jnp.concatenate([windows[x * 8 + y] for x in range(4)], axis=0)
        block = block.astype(F32).T
        other = jnp.concatenate([-block[W:], block[:W]], axis=0)
        turned.append(jnp.concatenate([block, other], axis=1).astype(BF))
    for begin in range(0, VIS, CHUNK):
        at = slice(begin, begin + CHUNK)
        left_part = left[:, at]
        base_real, base_imag = base[:W, at], base[W:, at]
        pred_real = jnp.zeros((1, CHUNK), F32)
        pred_imag = jnp.zeros((1, CHUNK), F32)
        for y in range(8):
            inner = dot(turned[y], left_part)
            inner_real, inner_imag = inner[:W], inner[W:]
            part_real = jnp.sum(inner_real * base_real - inner_imag * base_imag, axis=0, keepdims=True)
            part_imag = jnp.sum(inner_real * base_imag + inner_imag * base_real, axis=0, keepdims=True)
            er, ei = eighth[y : y + 1, at], eighth[8 + y : 9 + y, at]
            pred_real += part_real * er - part_imag * ei
            pred_imag += part_real * ei + part_imag * er
        slot = begin + lax.broadcasted_iota(jnp.int32, (1, CHUNK), 1)
        live = slot < count
        resid_real = jnp.where(live, observed[0, pl.ds(subgrid, 1), at] - pred_real / S, 0.0)
        resid_imag = jnp.where(live, observed[1, pl.ds(subgrid, 1), at] - pred_imag / S, 0.0)
        for y in range(8):
            er, ei = eighth[y : y + 1, at], eighth[8 + y : 9 + y, at]
            turned_real = resid_real * er + resid_imag * ei
            turned_imag = resid_imag * er - resid_real * ei
            weighted[y * 128 : y * 128 + W, at] = (
                turned_real * base_real + turned_imag * base_imag
            ).astype(BF)
            weighted[y * 128 + W : (y + 1) * 128, at] = (
                turned_imag * base_real - turned_real * base_imag
            ).astype(BF)
    sign = half_sign((W, 128))
    for y in range(8):
        both = lax.dot_general(
            left[...],
            weighted[y * 128 : (y + 1) * 128],
            (((1,), (1,)), ((), ())),
            preferred_element_type=F32,
        )
        for x in range(4):
            block = both[x * W : (x + 1) * W] - sign * swap(both[256 + x * W : 256 + (x + 1) * W])
            real, imag = scalar_phase(units, x, y, subgrid, column)
            scale = 1.0 / math.sqrt(VIS)
            out[x * 8 + y] = (
                block * (real * scale) - sign * swap(block) * (imag * scale)
            ).astype(BF)


def back_kernel(table, returned, *outs):
    turned = []
    for g in range(8):
        block = returned[g * 4 : (g + 1) * 4].reshape(256, 128)
        turned.append(block.astype(F32).T.astype(BF))
    turned = jnp.concatenate(turned, axis=1)
    for shift, out in enumerate(outs):
        at = lanes(column_of(shift), 256)
        real, imag = dot(turned, table[0, :, at]), dot(turned, table[1, :, at])
        out[:W] = (real[:W] + imag[W:]).astype(BF)
        out[W:] = (real[W:] - imag[:W]).astype(BF)


def image_kernel(table, *refs):
    strips = refs[:N_COL]
    out, held, wide, left = refs[N_COL:]
    for shift, strip in enumerate(strips):
        at = lanes(column_of(-shift), 128)
        block = strip[...].astype(F32)
        other = jnp.concatenate([block[W:], -block[:W]], axis=0)
        wide[:256, at] = block.T.astype(BF)
        wide[256:, at] = other.T.astype(BF)
    copies = []
    for i in range(PIECES):
        at = slice(i * 256, (i + 1) * 256)
        held[:, :, at] = dot(wide[...], table[:, at]).reshape(2, 256, 256)
        copy = pltpu.make_async_copy(held.at[:, :, at], out.at[:, :, at], left.at[i])
        copy.start()
        copies.append(copy)
    for copy in copies:
        copy.wait()


VMEM = pl.BlockSpec(memory_space=pltpu.VMEM)
SMEM = pl.BlockSpec(memory_space=pltpu.SMEM)
HBM = pl.BlockSpec(memory_space=pltpu.HBM)


def params(mebibytes=24):
    return pltpu.CompilerParams(vmem_limit_bytes=mebibytes * 1024 * 1024)


def along_columns(parts):
    arrived = list(parts)
    for shift in (2, 1, 3):
        route = [(i, (i + shift) % N_COL) for i in range(N_COL)]
        arrived[shift] = lax.ppermute(parts[shift], "col", route)
    return arrived


def shaped(*dims, dtype=BF):
    return jax.ShapeDtypeStruct(dims, dtype)


def on_device(facets, observed, uv_cells, counts):
    units = jnp.asarray(facet_tables())
    by_column = column_rows()
    by_window = window_rows()
    strips = pl.pallas_call(
        strip_kernel,
        out_shape=[shaped(256, 128)] * N_COL,
        in_specs=[HBM, HBM],
        out_specs=[VMEM] * N_COL,
        scratch_shapes=[
            pltpu.VMEM((2, 256, F), BF),
            pltpu.VMEM((F, 512), BF),
            pltpu.VMEM((512, 512), F32),
            pltpu.SemaphoreType.DMA((2 * PIECES,)),
        ],
        compiler_params=params(),
        cost_estimate=COST,
        name="strip",
    )(facets, jnp.asarray(np.ascontiguousarray(by_column.T)))
    left, base, eighth = pl.pallas_call(
        wave_kernel,
        out_shape=[shaped(S, VIS), shaped(128, VIS, dtype=F32), shaped(16, VIS, dtype=F32)],
        in_specs=[VMEM] * 3,
        out_specs=[VMEM] * 3,
        compiler_params=params(),
        cost_estimate=COST,
        name="wave",
    )(uv_cells, jnp.asarray(left_rows()), jnp.asarray(right_rows()))
    windows = pl.pallas_call(
        window_kernel,
        out_shape=shaped(SUBCOL, W, 128),
        in_specs=[SMEM, VMEM] + [VMEM] * N_COL,
        out_specs=VMEM,
        scratch_shapes=[pltpu.VMEM((128, F), BF)],
        compiler_params=params(),
        cost_estimate=COST,
        name="window",
    )(units, jnp.asarray(np.ascontiguousarray(by_window.transpose(0, 2, 1))), *along_columns(strips))
    windows = lax.all_to_all(windows, FACET, split_axis=0, concat_axis=0, tiled=True)
    returned = pl.pallas_call(
        subgrid_kernel,
        out_shape=shaped(SUBCOL, W, 128),
        in_specs=[SMEM, SMEM] + [VMEM] * 5,
        out_specs=VMEM,
        scratch_shapes=[pltpu.VMEM((1024, VIS), BF)],
        compiler_params=params(),
        cost_estimate=COST,
        name="subgrid",
    )(units, counts, windows, observed, left, base, eighth)
    returned = lax.all_to_all(returned, FACET, split_axis=0, concat_axis=0, tiled=True)
    back = pl.pallas_call(
        back_kernel,
        out_shape=[shaped(128, 256)] * N_COL,
        in_specs=[VMEM, VMEM],
        out_specs=[VMEM] * N_COL,
        compiler_params=params(),
        cost_estimate=COST,
        name="back",
    )(jnp.asarray(by_window), returned)
    return pl.pallas_call(
        image_kernel,
        out_shape=shaped(2, 256, F, dtype=F32),
        in_specs=[VMEM] * (1 + N_COL),
        out_specs=HBM,
        scratch_shapes=[
            pltpu.VMEM((2, 256, F), F32),
            pltpu.VMEM((512, 512), BF),
            pltpu.SemaphoreType.DMA((PIECES,)),
        ],
        compiler_params=params(),
        cost_estimate=COST,
        name="image",
    )(jnp.asarray(by_column), *along_columns(back))


def solution(mesh):
    finer = Mesh(
        mesh.devices.reshape(4, 4, 2, mesh.shape["col"]), ("facet_0", "facet_1", "facet_2", "col")
    )
    return jax.shard_map(
        on_device,
        mesh=finer,
        in_specs=(P(None, FACET_COL, None), P(None, "col", None), P(None, "col", None), P("col")),
        out_specs=P(None, FACET_COL, None),
        check_vma=False,
    )
```

time: 81.9 us -> 70.7 us (0.86)
  blocking collectives: 56.3 us -> 15.1 us
  starting transfers between devices: 0 us -> 19.5 us
  waiting for transfers between devices: 0 us -> 16.6 us
  Pallas kernels: 21.8 us -> 13.2 us
  local copies, waits for them, and re-layouts: 3.15 us -> 5.88 us
    all_to_all x3 -> x0, blocking collectives: 41.3 us -> none  [the longest x1 21.6 us: on_device(): lax.all_to_all(windows, FACET, split_axis=0, concat_axis=0, tiled=True)]
    all_to_all x0 -> x1, waiting for transfers between devices: none -> 10.5 us  [on_device(): lax.all_to_all(windows, FACET, split_axis=0, concat_axis=0, tiled=True)]
    all_to_all x0 -> x1, starting transfers between devices: none -> 10 us  [on_device(): lax.all_to_all(windows, FACET, split_axis=0, concat_axis=0, tiled=True)]
    ppermute x0 -> x6, starting transfers between devices: none -> 9.45 us  [along_columns(): arrived[shift] = lax.ppermute(parts[shift], 'col', route)]
    pallas_call x5 -> x6, Pallas kernels: 21.8 us -> 13.2 us  [the longest x1 4.59 us: on_device(): pl.pallas_call(subgrid_kernel, out_shape=shaped(SUBCOL, W, 128), in_specs...]
    ppermute x0 -> x6, waiting for transfers between devices: none -> 6.11 us  [along_columns(): arrived[shift] = lax.ppermute(parts[shift], 'col', route)]
    unnamed x18 -> x22, local copies, waits for them, and re-layouts: 3.15 us -> 5.88 us
  transfers between devices with their start and end apart: 0 -> 7, of which waited for: 0 -> 5; matrix products, arithmetic and copies ran while one was open for 0% -> 0% of each run, Pallas kernels for 0% -> 1%
where the time goes in v1:
time: 70.7 us; the launch traced here: 70.4 us
  starting transfers between devices  19.5 us (28%)
  waiting for transfers between devices  16.6 us (23%)
  blocking collectives  15.1 us (21%)
  Pallas kernels  13.2 us (19%)
  local copies, waits for them, and re-layouts  5.88 us (8%)
    all_to_all x1, blocking collectives, on_device(): lax.all_to_all(returned, FACET, split_axis=0, concat_axis=0, tiled=True)  15.1 us
    all_to_all x1, waiting for transfers between devices, on_device(): lax.all_to_all(windows, FACET, split_axis=0, concat_axis=0, tiled=True)  10.5 us
    all_to_all x1, starting transfers between devices, on_device(): lax.all_to_all(windows, FACET, split_axis=0, concat_axis=0, tiled=True)  10 us
    ppermute x6, starting transfers between devices, along_columns(): arrived[shift] = lax.ppermute(parts[shift], 'col', route)  9.45 us
    ppermute x6, waiting for transfers between devices, along_columns(): arrived[shift] = lax.ppermute(parts[shift], 'col', route)  6.11 us
    unnamed x22, local copies, waits for them, and re-layouts  5.88 us
    pallas_call x1, Pallas kernels, on_device(): pl.pallas_call(subgrid_kernel, out_shape=shaped(SUBCOL, W, 128), in_specs...  4.59 us
    pallas_call x1, Pallas kernels, on_device(): pl.pallas_call(window_kernel, out_shape=shaped(SUBCOL, W, 128), in_specs=...  3.02 us
  transfers between devices with their start and end apart: 7, of which 5 were waited for; matrix products, arithmetic and copies ran while one was open for 0% of the time, Pallas kernels for 1%

profile of v1, /device:TPU:1, one launch (start us, length us, event | category | flops | bytes accessed | tf_op | source)
XLA Modules:
  0.0 70.4 jit_solution(2274497908297139)
XLA Ops:
  0.0 0.0 copy-start.10
  0.0 0.0 copy-start
  0.0 1.2 %copy-done = bf16[2,256,1024]{2,1,0:T(8,128)(2,1)S(1)} copy-done((bf16[2,256,1024]{2,1,0:T(8,128)(2,1)S(1)}, bf16[2,256,1024]{2,1,0:T(8,128)(2,1)}, u32[]{:S(2)}) %copy-start) | copy-done | bytes 1048600
  1.2 0.0 copy-start.7
  1.2 1.2 %copy-done.7 = bf16[1024,512]{1,0:T(8,128)(2,1)S(1)} copy-done((bf16[1024,512]{1,0:T(8,128)(2,1)S(1)}, bf16[1024,512]{1,0:T(8,128)(2,1)}, u32[]{:S(2)}) %copy-start.7) | copy-done | bytes 1048600
  2.5 0.0 copy-start.5
  2.5 1.3 %strip.1 = (bf16[256,128]{1,0:T(8,128)(2,1)S(1)}, bf16[256,128]{1,0:T(8,128)(2,1)S(1)}, bf16[256,128]{1,0:T(8,128)(2,1)S(1)}, bf16[256,128]{1,0:T(8,128)(2,1)S(1)}) custom-call(bf16[2,256,1024]{2,1,0:T(8,128)(2,1)S(1)} %copy-done, bf16[1024,512]{1,0:T(8,128)(2,1)S(1)} %copy-done.7), custom_call_target="tpu_custom_call" | custom-call | flops 20000000000 | bytes 16777216 | tf_op jit(solution)/shard_map/strip/pallas_call | solution.py:286
  3.8 2.2 %collective-permute-start = (bf16[256,128]{1,0:T(8,128)(2,1)S(1)}, bf16[256,128]{1,0:T(8,128)(2,1)S(1)}, u32[]{:S(2)}, u32[]{:S(2)}) collective-permute-start(bf16[256,128]{1,0:T(8,128)(2,1)S(1)} %get-tuple-element.17), channel_id=1, source_target_pairs={{0,1},{1,2},{2,3},{3,0},{4,5},{5,6},{6,7},{7,4},{8,9},{9,10},{10,1... | collective-permute-start | bytes 196616 | tf_op jit(solution)/shard_map/ppermute | solution.py:274
  6.0 2.6 %collective-permute-start.1 = (bf16[256,128]{1,0:T(8,128)(2,1)S(1)}, bf16[256,128]{1,0:T(8,128)(2,1)S(1)}, u32[]{:S(2)}, u32[]{:S(2)}) collective-permute-start(bf16[256,128]{1,0:T(8,128)(2,1)S(1)} %get-tuple-element.18), channel_id=1, source_target_pairs={{0,2},{1,3},{2,0},{3,1},{4,6},{5,7},{6,4},{7,5},{8,10},{9,11},{10,... | collective-permute-start | bytes 196616 | tf_op jit(solution)/shard_map/ppermute | solution.py:274
  8.6 1.1 %collective-permute-start.2 = (bf16[256,128]{1,0:T(8,128)(2,1)S(1)}, bf16[256,128]{1,0:T(8,128)(2,1)S(1)}, u32[]{:S(2)}, u32[]{:S(2)}) collective-permute-start(bf16[256,128]{1,0:T(8,128)(2,1)S(1)} %get-tuple-element.19), channel_id=1, source_target_pairs={{0,3},{1,0},{2,1},{3,2},{4,7},{5,4},{6,5},{7,6},{8,11},{9,8},{10,9... | collective-permute-start | bytes 196616 | tf_op jit(solution)/shard_map/ppermute | solution.py:274
  9.7 0.0 collective-permute-done.refs_1_
  9.7 1.5 %collective-permute-done.1.refs_2_ = bf16[256,128]{1,0:T(8,128)(2,1)S(1)} collective-permute-done((bf16[256,128]{1,0:T(8,128)(2,1)S(1)}, bf16[256,128]{1,0:T(8,128)(2,1)S(1)}, u32[]{:S(2)}, u32[]{:S(2)}) %collective-permute-start.1) | collective-permute-done | bytes 65568 | tf_op jit(solution)/shard_map/ppermute | solution.py:274
  11.2 0.8 %collective-permute-done.2.refs_3_ = bf16[256,128]{1,0:T(8,128)(2,1)S(1)} collective-permute-done((bf16[256,128]{1,0:T(8,128)(2,1)S(1)}, bf16[256,128]{1,0:T(8,128)(2,1)S(1)}, u32[]{:S(2)}, u32[]{:S(2)}) %collective-permute-start.2) | collective-permute-done | bytes 65568 | tf_op jit(solution)/shard_map/ppermute | solution.py:274
  12.0 0.0 copy-done.10
  12.0 0.0 copy-done.5
  12.0 0.0 copy-start.1
  12.0 0.0 copy-start.8
  12.0 0.0 copy-start.9
  12.1 3.0 %window.1 = bf16[32,64,128]{2,1,0:T(8,128)(2,1)} custom-call(f32[2,64]{1,0:T(2,128)S(1)} %copy-done.10, bf16[2,1024,2048]{2,1,0:T(8,128)(2,1)S(1)} %copy-done.5, bf16[256,128]{1,0:T(8,128)(2,1)S(1)} %get-tuple-element.16.refs_0_, bf16[256,128]{1,0:T(8,128)(2,1)S(1)} %collective-permute-done.refs_1_, bf16[256,128]{1,0:T(8,128)(2,1)S(1)} %collective-permute-done.1.refs_2_, ...), custom_call_target="tpu_custom_call" | custom-call | flops 20000000000 | bytes 16777216 | tf_op jit(solution)/shard_map/window/pallas_call | solution.py:310
  15.1 10.0 %all-to-all-start = ((bf16[32,64,128]{2,1,0:T(8,128)(2,1)}), bf16[32,64,128]{2,1,0:T(8,128)(2,1)S(1)}, u32[]{:S(2)}, u32[]{:S(2)}) async-start(bf16[32,64,128]{2,1,0:T(8,128)(2,1)} %window.1), calls=%async_computation | async-start | bytes 1048576 | tf_op jit(solution)/shard_map/all_to_all | solution.py:320
  25.1 0.0 copy-done.1
  25.1 0.0 copy-done.8
  25.1 0.0 copy-done.9
  25.1 0.0 copy-start.2
  25.1 0.0 copy-start.3
  25.2 1.1 %wave.1 = (bf16[512,1024]{1,0:T(8,128)(2,1)S(1)}, f32[128,1024]{1,0:T(8,128)S(1)}, f32[16,1024]{1,0:T(8,128)S(1)}) custom-call(s32[2,32,1024]{2,1,0:T(8,128)S(1)} %copy-done.1, bf16[512,512]{1,0:T(8,128)(2,1)S(1)} %copy-done.8, bf16[288,512]{1,0:T(8,128)(2,1)S(1)} %copy-done.9), custom_call_target="tpu_custom_call" | custom-call | flops 20000000000 | bytes 16777216 | tf_op jit(solution)/shard_map/wave/pallas_call | solution.py:301
  26.2 10.5 %all-to-all-done.windows = bf16[32,64,128]{2,1,0:T(8,128)(2,1)S(1)} async-done(((bf16[32,64,128]{2,1,0:T(8,128)(2,1)}), bf16[32,64,128]{2,1,0:T(8,128)(2,1)S(1)}, u32[]{:S(2)}, u32[]{:S(2)}) %all-to-all-start) | async-done | bytes 524320 | tf_op jit(solution)/shard_map/all_to_all | solution.py:320
  36.7 0.0 copy-done.2
  36.7 0.0 copy-done.3
  36.7 4.6 %subgrid.1 = bf16[32,64,128]{2,1,0:T(8,128)(2,1)S(1)} custom-call(f32[2,64]{1,0:T(2,128)S(1)} %copy-done.10, s32[32]{0:T(128)S(1)} %copy-done.3, bf16[32,64,128]{2,1,0:T(8,128)(2,1)S(1)} %all-to-all-done.windows, f32[2,32,1024]{2,1,0:T(8,128)S(1)} %copy-done.2, bf16[512,1024]{1,0:T(8,128)(2,1)S(1)} %get-tuple-element.20.left, ...), custom_call_target="tpu_custom_call" | custom-call | flops 20000000000 | bytes 16777216 | tf_op jit(solution)/shard_map/subgrid/pallas_call | solution.py:321
  41.3 15.1 %all_to_all.10.returned = bf16[32,64,128]{2,1,0:T(8,128)(2,1)S(1)} all-to-all(bf16[32,64,128]{2,1,0:T(8,128)(2,1)S(1)} %subgrid.1), channel_id=1, replica_groups=mesh['facet_0'=4,'facet_1'=4,'facet_2'=2,'col'=4] {'facet_0','facet_1','..., dimensions={0} | all-to-all | bytes 1048576 | tf_op jit(solution)/shard_map/all_to_all | solution.py:331
  56.4 0.0 copy-start.4
  56.4 3.4 %copy-done.4 = bf16[2,2048,1024]{2,1,0:T(8,128)(2,1)S(1)} copy-done((bf16[2,2048,1024]{2,1,0:T(8,128)(2,1)S(1)}, bf16[2,2048,1024]{2,1,0:T(8,128)(2,1)}, u32[]{:S(2)}) %copy-start.4) | copy-done | bytes 8388632
  59.8 0.0 copy-start.6
  59.8 1.4 %back.1 = (bf16[128,256]{1,0:T(8,128)(2,1)S(1)}, bf16[128,256]{1,0:T(8,128)(2,1)S(1)}, bf16[128,256]{1,0:T(8,128)(2,1)S(1)}, bf16[128,256]{1,0:T(8,128)(2,1)S(1)}) custom-call(bf16[2,2048,1024]{2,1,0:T(8,128)(2,1)S(1)} %copy-done.4, bf16[32,64,128]{2,1,0:T(8,128)(2,1)S(1)} %all_to_all.10.returned), custom_call_target="tpu_custom_call" | custom-call | flops 20000000000 | bytes 16777216 | tf_op jit(solution)/shard_map/back/pallas_call | solution.py:332
  61.1 0.1 collective-permute-start.3
  61.2 3.4 %collective-permute-start.4 = (bf16[128,256]{1,0:T(8,128)(2,1)S(1)}, bf16[128,256]{1,0:T(8,128)(2,1)S(1)}, u32[]{:S(2)}, u32[]{:S(2)}) collective-permute-start(bf16[128,256]{1,0:T(8,128)(2,1)S(1)} %get-tuple-element.25), channel_id=1, source_target_pairs={{0,2},{1,3},{2,0},{3,1},{4,6},{5,7},{6,4},{7,5},{8,10},{9,11},{10,... | collective-permute-start | bytes 196616 | tf_op jit(solution)/shard_map/ppermute | solution.py:274
  64.7 0.0 collective-permute-start.5
  64.7 1.6 %collective-permute-done.3.refs_1_ = bf16[128,256]{1,0:T(8,128)(2,1)S(1)} collective-permute-done((bf16[128,256]{1,0:T(8,128)(2,1)S(1)}, bf16[128,256]{1,0:T(8,128)(2,1)S(1)}, u32[]{:S(2)}, u32[]{:S(2)}) %collective-permute-start.3) | collective-permute-done | bytes 65568 | tf_op jit(solution)/shard_map/ppermute | solution.py:274
  66.3 2.2 %collective-permute-done.4.refs_2_ = bf16[128,256]{1,0:T(8,128)(2,1)S(1)} collective-permute-done((bf16[128,256]{1,0:T(8,128)(2,1)S(1)}, bf16[128,256]{1,0:T(8,128)(2,1)S(1)}, u32[]{:S(2)}, u32[]{:S(2)}) %collective-permute-start.4) | collective-permute-done | bytes 65568 | tf_op jit(solution)/shard_map/ppermute | solution.py:274
  68.5 0.0 collective-permute-done.5.refs_3_
  68.5 0.0 copy-done.6
  68.5 1.9 %image.1 = f32[2,256,1024]{2,1,0:T(8,128)} custom-call(bf16[512,1024]{1,0:T(8,128)(2,1)S(1)} %copy-done.6, bf16[128,256]{1,0:T(8,128)(2,1)S(1)} %get-tuple-element.23.refs_0_, bf16[128,256]{1,0:T(8,128)(2,1)S(1)} %collective-permute-done.3.refs_1_, bf16[128,256]{1,0:T(8,128)(2,1)S(1)} %collective-permute-done.4.refs_2_, ...), custom_call_target="tpu_custom_call" | custom-call | flops 20000000000 | bytes 16777216 | tf_op jit(solution)/shard_map/image/pallas_call | solution.py:341
Async XLA Ops:
  0.0 12.0 %copy-start.10 = (f32[2,64]{1,0:T(2,128)S(1)}, f32[2,64]{1,0:T(2,128)}, u32[]{:S(2)}) copy-start(f32[2,64]{1,0:T(2,128)} %constant.14.clone.units) | copy-start | bytes 1540
  0.0 1.2 %copy-start = (bf16[2,256,1024]{2,1,0:T(8,128)(2,1)S(1)}, bf16[2,256,1024]{2,1,0:T(8,128)(2,1)}, u32[]{:S(2)}) copy-start(bf16[2,256,1024]{2,1,0:T(8,128)(2,1)} %pixels.1) | copy-start | bytes 3145732
  1.2 1.2 %copy-start.7 = (bf16[1024,512]{1,0:T(8,128)(2,1)S(1)}, bf16[1024,512]{1,0:T(8,128)(2,1)}, u32[]{:S(2)}) copy-start(bf16[1024,512]{1,0:T(8,128)(2,1)} %constant.15.clone.table) | copy-start | bytes 3145732
  2.5 9.6 %copy-start.5 = (bf16[2,1024,2048]{2,1,0:T(8,128)(2,1)S(1)}, bf16[2,1024,2048]{2,1,0:T(8,128)(2,1)}, u32[]{:S(2)}) copy-start(bf16[2,1024,2048]{2,1,0:T(8,128)(2,1)} %constant.18.clone.table) | copy-start | bytes 25165828
  3.8 5.9 %collective-permute-start = (bf16[256,128]{1,0:T(8,128)(2,1)S(1)}, bf16[256,128]{1,0:T(8,128)(2,1)S(1)}, u32[]{:S(2)}, u32[]{:S(2)}) collective-permute-start(bf16[256,128]{1,0:T(8,128)(2,1)S(1)} %get-tuple-element.17), channel_id=1, source_target_pairs={{0,1},{1,2},{2,3},{3,0},{4,5},{5,6},{6,7},{7,4},{8,9},{9,10},{10,1... | collective-permute-start | bytes 196616 | tf_op jit(solution)/shard_map/ppermute | solution.py:274
  6.0 5.2 %collective-permute-start.1 = (bf16[256,128]{1,0:T(8,128)(2,1)S(1)}, bf16[256,128]{1,0:T(8,128)(2,1)S(1)}, u32[]{:S(2)}, u32[]{:S(2)}) collective-permute-start(bf16[256,128]{1,0:T(8,128)(2,1)S(1)} %get-tuple-element.18), channel_id=1, source_target_pairs={{0,2},{1,3},{2,0},{3,1},{4,6},{5,7},{6,4},{7,5},{8,10},{9,11},{10,... | collective-permute-start | bytes 196616 | tf_op jit(solution)/shard_map/ppermute | solution.py:274
  8.6 3.4 %collective-permute-start.2 = (bf16[256,128]{1,0:T(8,128)(2,1)S(1)}, bf16[256,128]{1,0:T(8,128)(2,1)S(1)}, u32[]{:S(2)}, u32[]{:S(2)}) collective-permute-start(bf16[256,128]{1,0:T(8,128)(2,1)S(1)} %get-tuple-element.19), channel_id=1, source_target_pairs={{0,3},{1,0},{2,1},{3,2},{4,7},{5,4},{6,5},{7,6},{8,11},{9,8},{10,9... | collective-permute-start | bytes 196616 | tf_op jit(solution)/shard_map/ppermute | solution.py:274
  12.0 13.1 %copy-start.1 = (s32[2,32,1024]{2,1,0:T(8,128)S(1)}, s32[2,32,1024]{2,1,0:T(8,128)}, u32[]{:S(2)}) copy-start(s32[2,32,1024]{2,1,0:T(8,128)} %cells.1) | copy-start | bytes 786436
  12.0 13.1 %copy-start.8 = (bf16[512,512]{1,0:T(8,128)(2,1)S(1)}, bf16[512,512]{1,0:T(8,128)(2,1)}, u32[]{:S(2)}) copy-start(bf16[512,512]{1,0:T(8,128)(2,1)} %constant.16.clone.left_tab) | copy-start | bytes 1572868
  12.0 13.1 %copy-start.9 = (bf16[288,512]{1,0:T(8,128)(2,1)S(1)}, bf16[288,512]{1,0:T(8,128)(2,1)}, u32[]{:S(2)}) copy-start(bf16[288,512]{1,0:T(8,128)(2,1)} %constant.17.clone.right_tab) | copy-start | bytes 884740
  15.1 21.6 %all-to-all-start = ((bf16[32,64,128]{2,1,0:T(8,128)(2,1)}), bf16[32,64,128]{2,1,0:T(8,128)(2,1)S(1)}, u32[]{:S(2)}, u32[]{:S(2)}) async-start(bf16[32,64,128]{2,1,0:T(8,128)(2,1)} %window.1), calls=%async_computation | async-start | bytes 1048576 | tf_op jit(solution)/shard_map/all_to_all | solution.py:320
  25.1 11.6 %copy-start.2 = (f32[2,32,1024]{2,1,0:T(8,128)S(1)}, f32[2,32,1024]{2,1,0:T(8,128)}, u32[]{:S(2)}) copy-start(f32[2,32,1024]{2,1,0:T(8,128)} %observed.1) | copy-start | bytes 786436
  25.1 11.6 %copy-start.3 = (s32[32]{0:T(128)S(1)}, s32[32]{0:T(128)}, u32[]{:S(2)}) copy-start(s32[32]{0:T(128)} %counts.1) | copy-start | bytes 388
  56.4 3.4 %copy-start.4 = (bf16[2,2048,1024]{2,1,0:T(8,128)(2,1)S(1)}, bf16[2,2048,1024]{2,1,0:T(8,128)(2,1)}, u32[]{:S(2)}) copy-start(bf16[2,2048,1024]{2,1,0:T(8,128)(2,1)} %constant.19.clone.table) | copy-start | bytes 25165828
  59.8 8.7 %copy-start.6 = (bf16[512,1024]{1,0:T(8,128)(2,1)S(1)}, bf16[512,1024]{1,0:T(8,128)(2,1)}, u32[]{:S(2)}) copy-start(bf16[512,1024]{1,0:T(8,128)(2,1)} %constant.20.clone.table) | copy-start | bytes 3145732
  61.1 5.1 %collective-permute-start.3 = (bf16[128,256]{1,0:T(8,128)(2,1)S(1)}, bf16[128,256]{1,0:T(8,128)(2,1)S(1)}, u32[]{:S(2)}, u32[]{:S(2)}) collective-permute-start(bf16[128,256]{1,0:T(8,128)(2,1)S(1)} %get-tuple-element.24), channel_id=1, source_target_pairs={{0,1},{1,2},{2,3},{3,0},{4,5},{5,6},{6,7},{7,4},{8,9},{9,10},{10,1... | collective-permute-start | bytes 196616 | tf_op jit(solution)/shard_map/ppermute | solution.py:274
  61.2 7.2 %collective-permute-start.4 = (bf16[128,256]{1,0:T(8,128)(2,1)S(1)}, bf16[128,256]{1,0:T(8,128)(2,1)S(1)}, u32[]{:S(2)}, u32[]{:S(2)}) collective-permute-start(bf16[128,256]{1,0:T(8,128)(2,1)S(1)} %get-tuple-element.25), channel_id=1, source_target_pairs={{0,2},{1,3},{2,0},{3,1},{4,6},{5,7},{6,4},{7,5},{8,10},{9,11},{10,... | collective-permute-start | bytes 196616 | tf_op jit(solution)/shard_map/ppermute | solution.py:274
  64.7 3.8 %collective-permute-start.5 = (bf16[128,256]{1,0:T(8,128)(2,1)S(1)}, bf16[128,256]{1,0:T(8,128)(2,1)S(1)}, u32[]{:S(2)}, u32[]{:S(2)}) collective-permute-start(bf16[128,256]{1,0:T(8,128)(2,1)S(1)} %get-tuple-element.26), channel_id=1, source_target_pairs={{0,3},{1,0},{2,1},{3,2},{4,7},{5,4},{6,5},{7,6},{8,11},{9,8},{10,9... | collective-permute-start | bytes 196616 | tf_op jit(solution)/shard_map/ppermute | solution.py:274

commit v2 on v1

--- a/solution.py
+++ b/solution.py
@@ -56,14 +56,14 @@
 def window_rows():
     j, k, p = np.arange(SUBCOL), np.arange(W), np.arange(F)
     freqs = 1024 * (k[None, :] + j[:, None]) + ((37 * j + 5) % 1024)[:, None]
-    real, imag = unit(p[None, :] * freqs.reshape(-1, 1), IMAGE)
+    real, imag = unit(p[None, None, :] * freqs[:, :, None], IMAGE)
     weights = taper() / math.sqrt(F)
-    return bf(np.stack([real * weights, imag * weights]))
+    return bf(np.stack([real * weights, imag * weights], axis=1).reshape(SUBCOL * 128, F))
 
 
 def left_rows():
-    real, imag = unit(np.arange(256)[:, None] * np.arange(S)[None, :], S)
-    return bf(np.concatenate([real, imag]))
+    parts = unit(np.arange(256)[:, None] * np.arange(S)[None, :], S)
+    return bf(np.stack([part.reshape(4, W, S) for part in parts], axis=1).reshape(S, S))
 
 
 def right_rows():
@@ -104,55 +104,37 @@
     return pl.ds(pl.multiple_of(block * width, width), width)
 
 
+def rows(block, height):
+    return pl.ds(pl.multiple_of(block * height, height), height)
+
+
 def strip_kernel(pixels, table, *refs):
-    outs = refs[:N_COL]
-    pixels_in, table_in, held, arrived = refs[N_COL:]
-    depth = F // PIECES
-    copies = []
-    for i in range(PIECES):
-        at = slice(i * depth, (i + 1) * depth)
-        copies.append(
-            (
-                pltpu.make_async_copy(table.at[at], table_in.at[at], arrived.at[i]),
-                pltpu.make_async_copy(
-                    pixels.at[:, :, at], pixels_in.at[:, :, at], arrived.at[PIECES + i]
-                ),
-            )
+    outs, held = refs[:N_COL], refs[N_COL]
+    for part in range(2):
+        held[part] = lax.dot_general(
+            table[...], pixels[part], (((1,), (1,)), ((), ())), preferred_element_type=F32
         )
-    for pair in copies[:2]:
-        pair[0].start()
-        pair[1].start()
-    both = jnp.zeros((512, 512), F32)
-    for i in range(PIECES):
-        copies[i][0].wait()
-        copies[i][1].wait()
-        if i + 2 < PIECES:
-            copies[i + 2][0].start()
-            copies[i + 2][1].start()
-        at = slice(i * depth, (i + 1) * depth)
-        both += dot(pixels_in[:, :, at].reshape(512, depth), table_in[at])
-    held[...] = both
-    sign = half_sign((256, 128))
     for shift, out in enumerate(outs):
-        at = lanes(column_of(shift), 128)
-        out[...] = (held[:256, at] + sign * swap(held[256:, at])).astype(BF)
-
-
-def window_kernel(units, table, *refs):
+        at = rows(column_of(shift), 128)
+        real, imag = held[0, at], held[1, at]
+        out[:W] = (real[:W] - imag[W:]).astype(BF)
+        out[W:] = (real[W:] + imag[:W]).astype(BF)
+
+
+def window_kernel(units, table, after, *refs):
     strips = refs[:N_COL]
     out, turned = refs[N_COL:]
     facet = lax.axis_index(FACET)
     column = lax.axis_index("col")
     for shift, strip in enumerate(strips):
-        turned[:, lanes(column_of(-shift), 256)] = strip[...].astype(F32).T.astype(BF)
+        turned[:, lanes(column_of(-shift), 256)] = strip[...]
     sign = half_sign((W, 128))
-    group = 4
+    group = 2
     for step in range(SUBCOL // group):
-        at = slice(step * group * W, (step + 1) * group * W)
-        first, second = dot(turned[...], table[0, :, at]), dot(turned[...], table[1, :, at])
-        both = jnp.concatenate([first[:W] - second[W:], first[W:] + second[:W]], axis=0).T
+        both = dot(turned[...], table[:, step * group * 128 : (step + 1) * group * 128])
         for g in range(group):
-            block = both[g * W : (g + 1) * W]
+            at = slice(g * 128, (g + 1) * 128)
+            block = both[:W, at] + sign * swap(both[W:, at])
             real, imag = scalar_phase(units, facet // 8, facet % 8, step * group + g, column)
             out[step * group + g] = (block * real + sign * swap(block) * imag).astype(BF)
 
@@ -164,30 +146,36 @@
         first = cells[0, pl.ds(subgrid, 1), at]
         second = cells[1, pl.ds(subgrid, 1), at]
         cell = lax.broadcasted_iota(jnp.int32, (S, CHUNK), 0)
-        left[:, at] = dot(left_tab[...], jnp.where(cell == first, 1.0, 0.0).astype(BF)).astype(BF)
+        picked = dot(left_tab[...], jnp.where(cell == first, 1.0, 0.0).astype(BF))
+        left[:S, at] = picked.astype(BF)
+        half, slot = begin // S, begin % S
+        left[S + slot : S + slot + CHUNK, half * S : (half + 1) * S] = picked.T.astype(BF)
         right = dot(right_tab[...], jnp.where(cell == second, 1.0, 0.0).astype(BF))
         base[:, at] = right[0:128] + right[128:256]
         eighth[:, at] = right[256:272] + right[272:288]
 
 
-def subgrid_kernel(units, counts, windows, observed, left, base, eighth, out, weighted):
+def subgrid_kernel(
+    units, counts, windows, observed, left, base, eighth, out, turned, weighted
+):
     subgrid = lax.axis_index(FACET)
     column = lax.axis_index("col")
     count = counts[subgrid]
-    turned = []
-    for y in range(8):
-        block = jnp.concatenate([windows[x * 8 + y] for x in range(4)], axis=0)
-        block = block.astype(F32).T
-        other = jnp.concatenate([-block[W:], block[:W]], axis=0)
-        turned.append(jnp.concatenate([block, other], axis=1).astype(BF))
+    sign = half_sign((W, 128))
+    for x in range(4):
+        for y in range(8):
+            block = windows[x * 8 + y].astype(F32)
+            at = slice(x * 128, (x + 1) * 128)
+            turned[y * 128 : y * 128 + W, at] = (-sign * block).astype(BF)
+            turned[y * 128 + W : (y + 1) * 128, at] = swap(block).astype(BF)
     for begin in range(0, VIS, CHUNK):
         at = slice(begin, begin + CHUNK)
-        left_part = left[:, at]
+        left_part = left[:S, at]
         base_real, base_imag = base[:W, at], base[W:, at]
         pred_real = jnp.zeros((1, CHUNK), F32)
         pred_imag = jnp.zeros((1, CHUNK), F32)
         for y in range(8):
-            inner = dot(turned[y], left_part)
+            inner = dot(turned[y * 128 : (y + 1) * 128], left_part)
             inner_real, inner_imag = inner[:W], inner[W:]
             part_real = jnp.sum(inner_real * base_real - inner_imag * base_imag, axis=0, keepdims=True)
             part_imag = jnp.sum(inner_real * base_imag + inner_imag * base_real, axis=0, keepdims=True)
@@ -208,34 +196,38 @@
             weighted[y * 128 + W : (y + 1) * 128, at] = (
                 turned_imag * base_real - turned_real * base_imag
             ).astype(BF)
+    scale = 1.0 / math.sqrt(VIS)
+    for pair in range(4):
+        part = weighted[pair * 256 : (pair + 1) * 256]
+        both = dot(part[:, :S], left[S:, :S]) + dot(part[:, S:], left[S:, S:])
+        for half in range(2):
+            y = pair * 2 + half
+            for x in range(4):
+                at = slice(x * 128, (x + 1) * 128)
+                upper = both[half * 128 : half * 128 + W, at]
+                lower = both[half * 128 + W : (half + 1) * 128, at]
+                block = swap(lower) - sign * upper
+                real, imag = scalar_phase(units, x, y, subgrid, column)
+                out[x * 8 + y] = (
+                    block * (real * scale) - sign * swap(block) * (imag * scale)
+                ).astype(BF)
+
+
+def back_kernel(returned, *refs):
+    tables, outs, turned = refs[: -N_COL - 1], refs[-N_COL - 1 : -1], refs[-1]
     sign = half_sign((W, 128))
-    for y in range(8):
-        both = lax.dot_general(
-            left[...],
-            weighted[y * 128 : (y + 1) * 128],
-            (((1,), (1,)), ((), ())),
-            preferred_element_type=F32,
-        )
-        for x in range(4):
-            block = both[x * W : (x + 1) * W] - sign * swap(both[256 + x * W : 256 + (x + 1) * W])
-            real, imag = scalar_phase(units, x, y, subgrid, column)
-            scale = 1.0 / math.sqrt(VIS)
-            out[x * 8 + y] = (
-                block * (real * scale) - sign * swap(block) * (imag * scale)
-            ).astype(BF)
-
-
-def back_kernel(table, returned, *outs):
-    turned = []
-    for g in range(8):
-        block = returned[g * 4 : (g + 1) * 4].reshape(256, 128)
-        turned.append(block.astype(F32).T.astype(BF))
-    turned = jnp.concatenate(turned, axis=1)
+    for j in range(SUBCOL):
+        at = slice(j * 128, (j + 1) * 128)
+        block = returned[j]
+        turned[:W, at] = block
+        turned[W:, at] = (-sign * swap(block.astype(F32))).astype(BF)
+    depth = SUBCOL * 128 // len(tables)
     for shift, out in enumerate(outs):
         at = lanes(column_of(shift), 256)
-        real, imag = dot(turned, table[0, :, at]), dot(turned, table[1, :, at])
-        out[:W] = (real[:W] + imag[W:]).astype(BF)
-        out[W:] = (real[W:] - imag[:W]).astype(BF)
+        out[...] = sum(
+            dot(turned[:, g * depth : (g + 1) * depth], table[:, at])
+            for g, table in enumerate(tables)
+        ).astype(BF)
 
 
 def image_kernel(table, *refs):
@@ -281,26 +273,26 @@
 
 def on_device(facets, observed, uv_cells, counts):
     units = jnp.asarray(facet_tables())
-    by_column = column_rows()
+    by_column = jnp.asarray(column_rows())
     by_window = window_rows()
+    back_tabs = [jnp.asarray(part) for part in np.split(by_window, 2)]
     strips = pl.pallas_call(
         strip_kernel,
-        out_shape=[shaped(256, 128)] * N_COL,
-        in_specs=[HBM, HBM],
+        out_shape=[shaped(128, 256)] * N_COL,
+        in_specs=[VMEM, VMEM],
         out_specs=[VMEM] * N_COL,
-        scratch_shapes=[
-            pltpu.VMEM((2, 256, F), BF),
-            pltpu.VMEM((F, 512), BF),
-            pltpu.VMEM((512, 512), F32),
-            pltpu.SemaphoreType.DMA((2 * PIECES,)),
+        scratch_shapes=[pltpu.VMEM((2, 512, 256), F32)],
+        compiler_params=params(),
+        cost_estimate=COST,
+        name="strip",
+    )(facets, by_column)
+    waves = pl.pallas_call(
+        wave_kernel,
+        out_shape=[
+            shaped(2 * S, VIS),
+            shaped(128, VIS, dtype=F32),
+            shaped(16, VIS, dtype=F32),
         ],
-        compiler_params=params(),
-        cost_estimate=COST,
-        name="strip",
-    )(facets, jnp.asarray(np.ascontiguousarray(by_column.T)))
-    left, base, eighth = pl.pallas_call(
-        wave_kernel,
-        out_shape=[shaped(S, VIS), shaped(128, VIS, dtype=F32), shaped(16, VIS, dtype=F32)],
         in_specs=[VMEM] * 3,
         out_specs=[VMEM] * 3,
         compiler_params=params(),
@@ -310,34 +302,35 @@
     windows = pl.pallas_call(
         window_kernel,
         out_shape=shaped(SUBCOL, W, 128),
-        in_specs=[SMEM, VMEM] + [VMEM] * N_COL,
+        in_specs=[SMEM, VMEM, pl.BlockSpec(memory_space=pl.ANY)] + [VMEM] * N_COL,
         out_specs=VMEM,
         scratch_shapes=[pltpu.VMEM((128, F), BF)],
         compiler_params=params(),
         cost_estimate=COST,
         name="window",
-    )(units, jnp.asarray(np.ascontiguousarray(by_window.transpose(0, 2, 1))), *along_columns(strips))
+    )(units, jnp.asarray(np.ascontiguousarray(by_window.T)), waves[-1], *along_columns(strips))
     windows = lax.all_to_all(windows, FACET, split_axis=0, concat_axis=0, tiled=True)
     returned = pl.pallas_call(
         subgrid_kernel,
         out_shape=shaped(SUBCOL, W, 128),
         in_specs=[SMEM, SMEM] + [VMEM] * 5,
         out_specs=VMEM,
-        scratch_shapes=[pltpu.VMEM((1024, VIS), BF)],
+        scratch_shapes=[pltpu.VMEM((1024, S), BF), pltpu.VMEM((1024, VIS), BF)],
         compiler_params=params(),
         cost_estimate=COST,
         name="subgrid",
-    )(units, counts, windows, observed, left, base, eighth)
+    )(units, counts, windows, observed, *waves)
     returned = lax.all_to_all(returned, FACET, split_axis=0, concat_axis=0, tiled=True)
     back = pl.pallas_call(
         back_kernel,
         out_shape=[shaped(128, 256)] * N_COL,
-        in_specs=[VMEM, VMEM],
+        in_specs=[VMEM] * (1 + len(back_tabs)),
         out_specs=[VMEM] * N_COL,
+        scratch_shapes=[pltpu.VMEM((128, SUBCOL * 128), BF)],
         compiler_params=params(),
         cost_estimate=COST,
         name="back",
-    )(jnp.asarray(by_window), returned)
+    )(returned, *back_tabs)
     return pl.pallas_call(
         image_kernel,
         out_shape=shaped(2, 256, F, dtype=F32),
@@ -351,7 +344,7 @@
         compiler_params=params(),
         cost_estimate=COST,
         name="image",
-    )(jnp.asarray(by_column), *along_columns(back))
+    )(by_column, *along_columns(back))
 
 
 def solution(mesh):

time: 70.7 us -> 64.8 us (0.917)
  blocking collectives: 15.1 us -> 36.5 us
  waiting for transfers between devices: 16.6 us -> 4.97 us
  starting transfers between devices: 19.5 us -> 9.42 us
  local copies, waits for them, and re-layouts: 5.88 us -> 2.53 us
  Pallas kernels: 13.2 us -> 11.1 us
    all_to_all x0 -> x1, blocking collectives: none -> 21.4 us  [on_device(): lax.all_to_all(windows, FACET, split_axis=0, concat_axis=0, tiled=True)]
    all_to_all x1 -> x0, waiting for transfers between devices: 10.5 us -> none  [on_device(): lax.all_to_all(windows, FACET, split_axis=0, concat_axis=0, tiled=True)]
    all_to_all x1 -> x0, starting transfers between devices: 10 us -> none  [on_device(): lax.all_to_all(windows, FACET, split_axis=0, concat_axis=0, tiled=True)]
    unnamed x22 -> x26, local copies, waits for them, and re-layouts: 5.88 us -> 2.53 us
    ppermute x6, waiting for transfers between devices: 6.11 us -> 4.97 us  [along_columns(): arrived[shift] = lax.ppermute(parts[shift], 'col', route)]
    pallas_call x1, Pallas kernels: 3.02 us -> 2.09 us  [on_device(): pl.pallas_call(window_kernel, out_shape=shaped(SUBCOL, W, 128), in_specs=...]
    pallas_call x1, Pallas kernels: 4.59 us -> 3.72 us  [on_device(): pl.pallas_call(subgrid_kernel, out_shape=shaped(SUBCOL, W, 128), in_specs...]
  transfers between devices with their start and end apart: 7 -> 6, of which waited for: 5 -> 4; matrix products, arithmetic and copies ran while one was open for 0% -> 0% of each run, Pallas kernels for 1% -> 2%
where the time goes in v2:
time: 64.8 us; the launch traced here: 64.5 us
  blocking collectives  36.5 us (56%)
  Pallas kernels  11.1 us (17%)
  starting transfers between devices  9.42 us (15%)
  waiting for transfers between devices  4.97 us (8%)
  local copies, waits for them, and re-layouts  2.53 us (4%)
    all_to_all x1, blocking collectives, on_device(): lax.all_to_all(windows, FACET, split_axis=0, concat_axis=0, tiled=True)  21.4 us
    all_to_all x1, blocking collectives, on_device(): lax.all_to_all(returned, FACET, split_axis=0, concat_axis=0, tiled=True)  15 us
    ppermute x6, starting transfers between devices, along_columns(): arrived[shift] = lax.ppermute(parts[shift], 'col', route)  9.42 us
    ppermute x6, waiting for transfers between devices, along_columns(): arrived[shift] = lax.ppermute(parts[shift], 'col', route)  4.97 us
    pallas_call x1, Pallas kernels, on_device(): pl.pallas_call(subgrid_kernel, out_shape=shaped(SUBCOL, W, 128), in_specs...  3.72 us
    unnamed x26, local copies, waits for them, and re-layouts  2.53 us
    pallas_call x1, Pallas kernels, on_device(): pl.pallas_call(window_kernel, out_shape=shaped(SUBCOL, W, 128), in_specs=...  2.09 us
    pallas_call x1, Pallas kernels, on_device(): pl.pallas_call(image_kernel, out_shape=shaped(2, 256, F, dtype=F32), in_s...  1.9 us
  transfers between devices with their start and end apart: 6, of which 4 were waited for; matrix products, arithmetic and copies ran while one was open for 0% of the time, Pallas kernels for 2%

profile of v2, /device:TPU:1, one launch (start us, length us, event | category | flops | bytes accessed | tf_op | source)
XLA Modules:
  0.0 64.5 jit_solution(10198677093531822484)
XLA Ops:
  0.0 0.0 copy-start
  0.0 1.2 %copy-done = bf16[2,256,1024]{2,1,0:T(8,128)(2,1)S(1)} copy-done((bf16[2,256,1024]{2,1,0:T(8,128)(2,1)S(1)}, bf16[2,256,1024]{2,1,0:T(8,128)(2,1)}, u32[]{:S(2)}) %copy-start) | copy-done | bytes 1048600
  1.2 0.0 copy-start.6
  1.2 1.2 %copy-done.6 = bf16[512,1024]{1,0:T(8,128)(2,1)S(1)} copy-done((bf16[512,1024]{1,0:T(8,128)(2,1)S(1)}, bf16[512,1024]{1,0:T(8,128)(2,1)}, u32[]{:S(2)}) %copy-start.6) | copy-done | bytes 1048600
  2.5 0.0 copy-start.1
  2.5 0.0 copy-start.8
  2.5 0.0 copy-start.9
  2.5 0.8 %strip.1 = (bf16[128,256]{1,0:T(8,128)(2,1)S(1)}, bf16[128,256]{1,0:T(8,128)(2,1)S(1)}, bf16[128,256]{1,0:T(8,128)(2,1)S(1)}, bf16[128,256]{1,0:T(8,128)(2,1)S(1)}) custom-call(bf16[2,256,1024]{2,1,0:T(8,128)(2,1)S(1)} %copy-done, bf16[512,1024]{1,0:T(8,128)(2,1)S(1)} %copy-done.6), custom_call_target="tpu_custom_call" | custom-call | flops 20000000000 | bytes 16777216 | tf_op jit(solution)/shard_map/strip/pallas_call | solution.py:279
  3.3 2.2 %collective-permute-start = (bf16[128,256]{1,0:T(8,128)(2,1)S(1)}, bf16[128,256]{1,0:T(8,128)(2,1)S(1)}, u32[]{:S(2)}, u32[]{:S(2)}) collective-permute-start(bf16[128,256]{1,0:T(8,128)(2,1)S(1)} %get-tuple-element.18), channel_id=1, source_target_pairs={{0,1},{1,2},{2,3},{3,0},{4,5},{5,6},{6,7},{7,4},{8,9},{9,10},{10,1... | collective-permute-start | bytes 196616 | tf_op jit(solution)/shard_map/ppermute | solution.py:266
  5.5 2.6 %collective-permute-start.1 = (bf16[128,256]{1,0:T(8,128)(2,1)S(1)}, bf16[128,256]{1,0:T(8,128)(2,1)S(1)}, u32[]{:S(2)}, u32[]{:S(2)}) collective-permute-start(bf16[128,256]{1,0:T(8,128)(2,1)S(1)} %get-tuple-element.19), channel_id=1, source_target_pairs={{0,2},{1,3},{2,0},{3,1},{4,6},{5,7},{6,4},{7,5},{8,10},{9,11},{10,... | collective-permute-start | bytes 196616 | tf_op jit(solution)/shard_map/ppermute | solution.py:266
  8.1 0.0 slice-start
  8.1 0.0 slice-start.1
  8.1 0.0 copy-start.10
  8.1 1.1 %collective-permute-start.2 = (bf16[128,256]{1,0:T(8,128)(2,1)S(1)}, bf16[128,256]{1,0:T(8,128)(2,1)S(1)}, u32[]{:S(2)}, u32[]{:S(2)}) collective-permute-start(bf16[128,256]{1,0:T(8,128)(2,1)S(1)} %get-tuple-element.20), channel_id=1, source_target_pairs={{0,3},{1,0},{2,1},{3,2},{4,7},{5,4},{6,5},{7,6},{8,11},{9,8},{10,9... | collective-permute-start | bytes 196616 | tf_op jit(solution)/shard_map/ppermute | solution.py:266
  9.2 0.0 copy-done.1
  9.2 0.0 copy-done.8
  9.2 0.0 copy-done.9
  9.2 1.1 %wave.1 = (bf16[1024,1024]{1,0:T(8,128)(2,1)S(1)}, f32[128,1024]{1,0:T(8,128)S(1)}, f32[16,1024]{1,0:T(8,128)S(1)}) custom-call(s32[2,32,1024]{2,1,0:T(8,128)S(1)} %copy-done.1, bf16[512,512]{1,0:T(8,128)(2,1)S(1)} %copy-done.8, bf16[288,512]{1,0:T(8,128)(2,1)S(1)} %copy-done.9), custom_call_target="tpu_custom_call" | custom-call | flops 20000000000 | bytes 16777216 | tf_op jit(solution)/shard_map/wave/pallas_call | solution.py:289
  10.3 0.0 collective-permute-done.refs_1_
  10.3 0.4 collective-permute-done.1.refs_2_
  10.7 0.8 %collective-permute-done.2.refs_3_ = bf16[128,256]{1,0:T(8,128)(2,1)S(1)} collective-permute-done((bf16[128,256]{1,0:T(8,128)(2,1)S(1)}, bf16[128,256]{1,0:T(8,128)(2,1)S(1)}, u32[]{:S(2)}, u32[]{:S(2)}) %collective-permute-start.2) | collective-permute-done | bytes 65568 | tf_op jit(solution)/shard_map/ppermute | solution.py:266
  11.5 0.0 slice-done
  11.5 0.0 slice-done.1
  11.6 0.0 copy-done.10
  11.6 0.0 copy-start.2
  11.6 0.0 copy-start.3
  11.6 2.1 %window.1 = bf16[32,64,128]{2,1,0:T(8,128)(2,1)S(1)} custom-call(f32[2,64]{1,0:T(2,128)S(1)} %copy-done.10, bf16[1024,4096]{1,0:T(8,128)(2,1)S(1)} %bitcast.1, f32[16,1024]{1,0:T(8,128)S(1)} %get-tuple-element.16.after.eighth, bf16[128,256]{1,0:T(8,128)(2,1)S(1)} %get-tuple-element.17.refs_0_, bf16[128,256]{1,0:T(8,128)(2,1)S(1)} %collective-permute-done.refs_1_, ...), custom_call_target="tpu_custom_call" | custom-call | flops 20000000000 | bytes 16777216 | tf_op jit(solution)/shard_map/window/pallas_call | solution.py:302
  13.7 21.4 %all_to_all.10.windows = bf16[32,64,128]{2,1,0:T(8,128)(2,1)S(1)} all-to-all(bf16[32,64,128]{2,1,0:T(8,128)(2,1)S(1)} %window.1), channel_id=1, replica_groups=mesh['facet_0'=4,'facet_1'=4,'facet_2'=2,'col'=4] {'facet_0','facet_1','..., dimensions={0} | all-to-all | bytes 1048576 | tf_op jit(solution)/shard_map/all_to_all | solution.py:312
  35.1 0.0 copy-done.2
  35.1 0.0 copy-done.3
  35.1 0.0 copy-start.4
  35.1 0.0 copy-start.5
  35.1 3.7 %subgrid.1 = bf16[32,64,128]{2,1,0:T(8,128)(2,1)S(1)} custom-call(f32[2,64]{1,0:T(2,128)S(1)} %copy-done.10, s32[32]{0:T(128)S(1)} %copy-done.3, bf16[32,64,128]{2,1,0:T(8,128)(2,1)S(1)} %all_to_all.10.windows, f32[2,32,1024]{2,1,0:T(8,128)S(1)} %copy-done.2, bf16[1024,1024]{1,0:T(8,128)(2,1)S(1)} %get-tuple-element.21.left, ...), custom_call_target="tpu_custom_call" | custom-call | flops 20000000000 | bytes 16777216 | tf_op jit(solution)/shard_map/subgrid/pallas_call | solution.py:313
  38.8 15.0 %all_to_all.11.returned = bf16[32,64,128]{2,1,0:T(8,128)(2,1)S(1)} all-to-all(bf16[32,64,128]{2,1,0:T(8,128)(2,1)S(1)} %subgrid.1), channel_id=1, replica_groups=mesh['facet_0'=4,'facet_1'=4,'facet_2'=2,'col'=4] {'facet_0','facet_1','..., dimensions={0} | all-to-all | bytes 1048576 | tf_op jit(solution)/shard_map/all_to_all | solution.py:323
  53.9 0.0 copy-done.4
  53.9 0.0 copy-done.5
  53.9 0.0 copy-start.7
  53.9 1.4 %back.1 = (bf16[128,256]{1,0:T(8,128)(2,1)S(1)}, bf16[128,256]{1,0:T(8,128)(2,1)S(1)}, bf16[128,256]{1,0:T(8,128)(2,1)S(1)}, bf16[128,256]{1,0:T(8,128)(2,1)S(1)}) custom-call(bf16[32,64,128]{2,1,0:T(8,128)(2,1)S(1)} %all_to_all.11.returned, bf16[2048,1024]{1,0:T(8,128)(2,1)S(1)} %copy-done.5, bf16[2048,1024]{1,0:T(8,128)(2,1)S(1)} %copy-done.4), custom_call_target="tpu_custom_call" | custom-call | flops 20000000000 | bytes 16777216 | tf_op jit(solution)/shard_map/back/pallas_call | solution.py:324
  55.3 0.1 collective-permute-start.3
  55.4 3.4 %collective-permute-start.4 = (bf16[128,256]{1,0:T(8,128)(2,1)S(1)}, bf16[128,256]{1,0:T(8,128)(2,1)S(1)}, u32[]{:S(2)}, u32[]{:S(2)}) collective-permute-start(bf16[128,256]{1,0:T(8,128)(2,1)S(1)} %get-tuple-element.25), channel_id=1, source_target_pairs={{0,2},{1,3},{2,0},{3,1},{4,6},{5,7},{6,4},{7,5},{8,10},{9,11},{10,... | collective-permute-start | bytes 196616 | tf_op jit(solution)/shard_map/ppermute | solution.py:266
  58.9 0.0 collective-permute-start.5
  58.9 1.6 %collective-permute-done.3.refs_1_ = bf16[128,256]{1,0:T(8,128)(2,1)S(1)} collective-permute-done((bf16[128,256]{1,0:T(8,128)(2,1)S(1)}, bf16[128,256]{1,0:T(8,128)(2,1)S(1)}, u32[]{:S(2)}, u32[]{:S(2)}) %collective-permute-start.3) | collective-permute-done | bytes 65568 | tf_op jit(solution)/shard_map/ppermute | solution.py:266
  60.5 2.2 %collective-permute-done.4.refs_2_ = bf16[128,256]{1,0:T(8,128)(2,1)S(1)} collective-permute-done((bf16[128,256]{1,0:T(8,128)(2,1)S(1)}, bf16[128,256]{1,0:T(8,128)(2,1)S(1)}, u32[]{:S(2)}, u32[]{:S(2)}) %collective-permute-start.4) | collective-permute-done | bytes 65568 | tf_op jit(solution)/shard_map/ppermute | solution.py:266
  62.6 0.0 collective-permute-done.5.refs_3_
  62.6 0.0 copy-done.7
  62.6 1.9 %image.1 = f32[2,256,1024]{2,1,0:T(8,128)} custom-call(bf16[512,1024]{1,0:T(8,128)(2,1)S(1)} %copy-done.7, bf16[128,256]{1,0:T(8,128)(2,1)S(1)} %get-tuple-element.23.refs_0_, bf16[128,256]{1,0:T(8,128)(2,1)S(1)} %collective-permute-done.3.refs_1_, bf16[128,256]{1,0:T(8,128)(2,1)S(1)} %collective-permute-done.4.refs_2_, ...), custom_call_target="tpu_custom_call" | custom-call | flops 20000000000 | bytes 16777216 | tf_op jit(solution)/shard_map/image/pallas_call | solution.py:334
  (1 shorter events, 0.0 us)
Async XLA Ops:
  0.0 1.2 %copy-start = (bf16[2,256,1024]{2,1,0:T(8,128)(2,1)S(1)}, bf16[2,256,1024]{2,1,0:T(8,128)(2,1)}, u32[]{:S(2)}) copy-start(bf16[2,256,1024]{2,1,0:T(8,128)(2,1)} %pixels.1) | copy-start | bytes 3145732
  1.2 1.2 %copy-start.6 = (bf16[512,1024]{1,0:T(8,128)(2,1)S(1)}, bf16[512,1024]{1,0:T(8,128)(2,1)}, u32[]{:S(2)}) copy-start(bf16[512,1024]{1,0:T(8,128)(2,1)} %constant.15.clone.table) | copy-start | bytes 3145732
  2.5 6.7 %copy-start.1 = (s32[2,32,1024]{2,1,0:T(8,128)S(1)}, s32[2,32,1024]{2,1,0:T(8,128)}, u32[]{:S(2)}) copy-start(s32[2,32,1024]{2,1,0:T(8,128)} %cells.1) | copy-start | bytes 786436
  2.5 6.7 %copy-start.8 = (bf16[512,512]{1,0:T(8,128)(2,1)S(1)}, bf16[512,512]{1,0:T(8,128)(2,1)}, u32[]{:S(2)}) copy-start(bf16[512,512]{1,0:T(8,128)(2,1)} %constant.18.clone.left_tab) | copy-start | bytes 1572868
  2.5 6.7 %copy-start.9 = (bf16[288,512]{1,0:T(8,128)(2,1)S(1)}, bf16[288,512]{1,0:T(8,128)(2,1)}, u32[]{:S(2)}) copy-start(bf16[288,512]{1,0:T(8,128)(2,1)} %constant.19.clone.right_tab) | copy-start | bytes 884740
  3.3 7.0 %collective-permute-start = (bf16[128,256]{1,0:T(8,128)(2,1)S(1)}, bf16[128,256]{1,0:T(8,128)(2,1)S(1)}, u32[]{:S(2)}, u32[]{:S(2)}) collective-permute-start(bf16[128,256]{1,0:T(8,128)(2,1)S(1)} %get-tuple-element.18), channel_id=1, source_target_pairs={{0,1},{1,2},{2,3},{3,0},{4,5},{5,6},{6,7},{7,4},{8,9},{9,10},{10,1... | collective-permute-start | bytes 196616 | tf_op jit(solution)/shard_map/ppermute | solution.py:266
  5.5 5.2 %collective-permute-start.1 = (bf16[128,256]{1,0:T(8,128)(2,1)S(1)}, bf16[128,256]{1,0:T(8,128)(2,1)S(1)}, u32[]{:S(2)}, u32[]{:S(2)}) collective-permute-start(bf16[128,256]{1,0:T(8,128)(2,1)S(1)} %get-tuple-element.19), channel_id=1, source_target_pairs={{0,2},{1,3},{2,0},{3,1},{4,6},{5,7},{6,4},{7,5},{8,10},{9,11},{10,... | collective-permute-start | bytes 196616 | tf_op jit(solution)/shard_map/ppermute | solution.py:266
  8.1 3.4 %slice-start = ((s8[8388608]{0:T(1024)(128)(4,1)}), s8[4194304]{0:T(1024)(128)(4,1)S(1)}, s32[]{:S(2)}) async-start(s8[8388608]{0:T(1024)(128)(4,1)} %bitcast), calls=%async_computation.2 | async-start | bytes 8388608
  8.1 3.5 %slice-start.1 = ((s8[8388608]{0:T(1024)(128)(4,1)}), s8[4194304]{0:T(1024)(128)(4,1)S(1)}, s32[]{:S(2)}) async-start(s8[8388608]{0:T(1024)(128)(4,1)} %bitcast), calls=%async_computation.3 | async-start | bytes 8388608
  8.1 3.5 %copy-start.10 = (f32[2,64]{1,0:T(2,128)S(1)}, f32[2,64]{1,0:T(2,128)}, u32[]{:S(2)}) copy-start(f32[2,64]{1,0:T(2,128)} %constant.14.clone.units) | copy-start | bytes 1540
  8.1 3.4 %collective-permute-start.2 = (bf16[128,256]{1,0:T(8,128)(2,1)S(1)}, bf16[128,256]{1,0:T(8,128)(2,1)S(1)}, u32[]{:S(2)}, u32[]{:S(2)}) collective-permute-start(bf16[128,256]{1,0:T(8,128)(2,1)S(1)} %get-tuple-element.20), channel_id=1, source_target_pairs={{0,3},{1,0},{2,1},{3,2},{4,7},{5,4},{6,5},{7,6},{8,11},{9,8},{10,9... | collective-permute-start | bytes 196616 | tf_op jit(solution)/shard_map/ppermute | solution.py:266
  11.6 23.5 %copy-start.2 = (f32[2,32,1024]{2,1,0:T(8,128)S(1)}, f32[2,32,1024]{2,1,0:T(8,128)}, u32[]{:S(2)}) copy-start(f32[2,32,1024]{2,1,0:T(8,128)} %observed.1) | copy-start | bytes 786436
  11.6 23.5 %copy-start.3 = (s32[32]{0:T(128)S(1)}, s32[32]{0:T(128)}, u32[]{:S(2)}) copy-start(s32[32]{0:T(128)} %counts.1) | copy-start | bytes 388
  35.1 18.8 %copy-start.4 = (bf16[2048,1024]{1,0:T(8,128)(2,1)S(1)}, bf16[2048,1024]{1,0:T(8,128)(2,1)}, u32[]{:S(2)}) copy-start(bf16[2048,1024]{1,0:T(8,128)(2,1)} %constant.17.clone.refs_1_) | copy-start | bytes 12582916
  35.1 18.8 %copy-start.5 = (bf16[2048,1024]{1,0:T(8,128)(2,1)S(1)}, bf16[2048,1024]{1,0:T(8,128)(2,1)}, u32[]{:S(2)}) copy-start(bf16[2048,1024]{1,0:T(8,128)(2,1)} %constant.16.clone.refs_0_) | copy-start | bytes 12582916
  53.9 8.8 %copy-start.7 = (bf16[512,1024]{1,0:T(8,128)(2,1)S(1)}, bf16[512,1024]{1,0:T(8,128)(2,1)}, u32[]{:S(2)}) copy-start(bf16[512,1024]{1,0:T(8,128)(2,1)} %constant.15.clone.table) | copy-start | bytes 3145732
  55.3 5.1 %collective-permute-start.3 = (bf16[128,256]{1,0:T(8,128)(2,1)S(1)}, bf16[128,256]{1,0:T(8,128)(2,1)S(1)}, u32[]{:S(2)}, u32[]{:S(2)}) collective-permute-start(bf16[128,256]{1,0:T(8,128)(2,1)S(1)} %get-tuple-element.24), channel_id=1, source_target_pairs={{0,1},{1,2},{2,3},{3,0},{4,5},{5,6},{6,7},{7,4},{8,9},{9,10},{10,1... | collective-permute-start | bytes 196616 | tf_op jit(solution)/shard_map/ppermute | solution.py:266
  55.4 7.2 %collective-permute-start.4 = (bf16[128,256]{1,0:T(8,128)(2,1)S(1)}, bf16[128,256]{1,0:T(8,128)(2,1)S(1)}, u32[]{:S(2)}, u32[]{:S(2)}) collective-permute-start(bf16[128,256]{1,0:T(8,128)(2,1)S(1)} %get-tuple-element.25), channel_id=1, source_target_pairs={{0,2},{1,3},{2,0},{3,1},{4,6},{5,7},{6,4},{7,5},{8,10},{9,11},{10,... | collective-permute-start | bytes 196616 | tf_op jit(solution)/shard_map/ppermute | solution.py:266
  58.9 3.8 %collective-permute-start.5 = (bf16[128,256]{1,0:T(8,128)(2,1)S(1)}, bf16[128,256]{1,0:T(8,128)(2,1)S(1)}, u32[]{:S(2)}, u32[]{:S(2)}) collective-permute-start(bf16[128,256]{1,0:T(8,128)(2,1)S(1)} %get-tuple-element.26), channel_id=1, source_target_pairs={{0,3},{1,0},{2,1},{3,2},{4,7},{5,4},{6,5},{7,6},{8,11},{9,8},{10,9... | collective-permute-start | bytes 196616 | tf_op jit(solution)/shard_map/ppermute | solution.py:266

commit v3 on v2

--- a/solution.py
+++ b/solution.py
@@ -23,6 +23,7 @@
 F32 = jnp.float32
 PIECES = 4
 CHUNK = 256
+GROUP = 4
 COST = pl.CostEstimate(flops=2 * 10**10, bytes_accessed=2**24, transcendentals=0)
 
 
@@ -62,8 +63,8 @@
 
 
 def left_rows():
-    parts = unit(np.arange(256)[:, None] * np.arange(S)[None, :], S)
-    return bf(np.stack([part.reshape(4, W, S) for part in parts], axis=1).reshape(S, S))
+    real, imag = unit(np.arange(256)[:, None] * np.arange(S)[None, :], S)
+    return bf(np.stack([real.reshape(4, W, S), -imag.reshape(4, W, S)], axis=1).reshape(S, S))
 
 
 def right_rows():
@@ -109,11 +110,31 @@
 
 
 def strip_kernel(pixels, table, *refs):
-    outs, held = refs[:N_COL], refs[N_COL]
-    for part in range(2):
-        held[part] = lax.dot_general(
-            table[...], pixels[part], (((1,), (1,)), ((), ())), preferred_element_type=F32
+    outs = refs[:N_COL]
+    pixels_in, table_in, held, arrived = refs[N_COL:]
+    copies = []
+    for i in range(PIECES):
+        at = slice(i * F // PIECES, (i + 1) * F // PIECES)
+        copies.append(pltpu.make_async_copy(table.at[:, at], table_in.at[:, at], arrived.at[i]))
+        copies.append(
+            pltpu.make_async_copy(
+                pixels.at[:, :, at], pixels_in.at[:, :, at], arrived.at[PIECES + i]
+            )
         )
+    for copy in copies:
+        copy.start()
+    for i in range(PIECES):
+        at = slice(i * F // PIECES, (i + 1) * F // PIECES)
+        copies[2 * i].wait()
+        copies[2 * i + 1].wait()
+        for part in range(2):
+            product = lax.dot_general(
+                table_in[:, at],
+                pixels_in[part, :, at],
+                (((1,), (1,)), ((), ())),
+                preferred_element_type=F32,
+            )
+            held[part] = product if i == 0 else held[part] + product
     for shift, out in enumerate(outs):
         at = rows(column_of(shift), 128)
         real, imag = held[0, at], held[1, at]
@@ -139,7 +160,7 @@
             out[step * group + g] = (block * real + sign * swap(block) * imag).astype(BF)
 
 
-def wave_kernel(cells, left_tab, right_tab, left, base, eighth):
+def wave_kernel(cells, left_tab, right_tab, left, left_by_slot, base, eighth):
     subgrid = lax.axis_index(FACET)
     for begin in range(0, VIS, CHUNK):
         at = slice(begin, begin + CHUNK)
@@ -147,41 +168,52 @@
         second = cells[1, pl.ds(subgrid, 1), at]
         cell = lax.broadcasted_iota(jnp.int32, (S, CHUNK), 0)
         picked = dot(left_tab[...], jnp.where(cell == first, 1.0, 0.0).astype(BF))
+        other = jnp.concatenate(
+            [
+                part
+                for x in range(4)
+                for part in (-picked[x * 128 + W : (x + 1) * 128], picked[x * 128 : x * 128 + W])
+            ],
+            axis=0,
+        )
         left[:S, at] = picked.astype(BF)
-        half, slot = begin // S, begin % S
-        left[S + slot : S + slot + CHUNK, half * S : (half + 1) * S] = picked.T.astype(BF)
+        left[S:, at] = other.astype(BF)
+        left_by_slot[at] = picked.T.astype(BF)
+        left_by_slot[VIS + begin : VIS + begin + CHUNK] = other.T.astype(BF)
         right = dot(right_tab[...], jnp.where(cell == second, 1.0, 0.0).astype(BF))
         base[:, at] = right[0:128] + right[128:256]
         eighth[:, at] = right[256:272] + right[272:288]
 
 
 def subgrid_kernel(
-    units, counts, windows, observed, left, base, eighth, out, turned, weighted
+    units, counts, windows, observed, left, left_by_slot, base, eighth, out, held, weighted
 ):
     subgrid = lax.axis_index(FACET)
     column = lax.axis_index("col")
     count = counts[subgrid]
-    sign = half_sign((W, 128))
     for x in range(4):
         for y in range(8):
-            block = windows[x * 8 + y].astype(F32)
-            at = slice(x * 128, (x + 1) * 128)
-            turned[y * 128 : y * 128 + W, at] = (-sign * block).astype(BF)
-            turned[y * 128 + W : (y + 1) * 128, at] = swap(block).astype(BF)
+            held[y * W : (y + 1) * W, x * 128 : (x + 1) * 128] = windows[x * 8 + y]
     for begin in range(0, VIS, CHUNK):
         at = slice(begin, begin + CHUNK)
-        left_part = left[:S, at]
         base_real, base_imag = base[:W, at], base[W:, at]
         pred_real = jnp.zeros((1, CHUNK), F32)
         pred_imag = jnp.zeros((1, CHUNK), F32)
-        for y in range(8):
-            inner = dot(turned[y * 128 : (y + 1) * 128], left_part)
-            inner_real, inner_imag = inner[:W], inner[W:]
-            part_real = jnp.sum(inner_real * base_real - inner_imag * base_imag, axis=0, keepdims=True)
-            part_imag = jnp.sum(inner_real * base_imag + inner_imag * base_real, axis=0, keepdims=True)
-            er, ei = eighth[y : y + 1, at], eighth[8 + y : 9 + y, at]
-            pred_real += part_real * er - part_imag * ei
-            pred_imag += part_real * ei + part_imag * er
+        for y0 in range(0, 8, GROUP):
+            real = dot(held[y0 * W : (y0 + GROUP) * W], left[:S, at])
+            imag = dot(held[y0 * W : (y0 + GROUP) * W], left[S:, at])
+            for y in range(y0, y0 + GROUP):
+                inner_real = real[(y - y0) * W : (y - y0 + 1) * W]
+                inner_imag = imag[(y - y0) * W : (y - y0 + 1) * W]
+                part_real = jnp.sum(
+                    inner_real * base_real - inner_imag * base_imag, axis=0, keepdims=True
+                )
+                part_imag = jnp.sum(
+                    inner_real * base_imag + inner_imag * base_real, axis=0, keepdims=True
+                )
+                er, ei = eighth[y : y + 1, at], eighth[8 + y : 9 + y, at]
+                pred_real += part_real * er - part_imag * ei
+                pred_imag += part_real * ei + part_imag * er
         slot = begin + lax.broadcasted_iota(jnp.int32, (1, CHUNK), 1)
         live = slot < count
         resid_real = jnp.where(live, observed[0, pl.ds(subgrid, 1), at] - pred_real / S, 0.0)
@@ -190,23 +222,18 @@
             er, ei = eighth[y : y + 1, at], eighth[8 + y : 9 + y, at]
             turned_real = resid_real * er + resid_imag * ei
             turned_imag = resid_imag * er - resid_real * ei
-            weighted[y * 128 : y * 128 + W, at] = (
-                turned_real * base_real + turned_imag * base_imag
-            ).astype(BF)
-            weighted[y * 128 + W : (y + 1) * 128, at] = (
+            here = slice(y * W, (y + 1) * W)
+            weighted[here, at] = (turned_real * base_real + turned_imag * base_imag).astype(BF)
+            weighted[here, VIS + begin : VIS + begin + CHUNK] = (
                 turned_imag * base_real - turned_real * base_imag
             ).astype(BF)
+    sign = half_sign((W, 128))
     scale = 1.0 / math.sqrt(VIS)
-    for pair in range(4):
-        part = weighted[pair * 256 : (pair + 1) * 256]
-        both = dot(part[:, :S], left[S:, :S]) + dot(part[:, S:], left[S:, S:])
-        for half in range(2):
-            y = pair * 2 + half
+    for y0 in range(0, 8, GROUP):
+        both = dot(weighted[y0 * W : (y0 + GROUP) * W], left_by_slot[...])
+        for y in range(y0, y0 + GROUP):
             for x in range(4):
-                at = slice(x * 128, (x + 1) * 128)
-                upper = both[half * 128 : half * 128 + W, at]
-                lower = both[half * 128 + W : (half + 1) * 128, at]
-                block = swap(lower) - sign * upper
+                block = both[(y - y0) * W : (y - y0 + 1) * W, x * 128 : (x + 1) * 128]
                 real, imag = scalar_phase(units, x, y, subgrid, column)
                 out[x * 8 + y] = (
                     block * (real * scale) - sign * swap(block) * (imag * scale)
@@ -233,19 +260,21 @@
 def image_kernel(table, *refs):
     strips = refs[:N_COL]
     out, held, wide, left = refs[N_COL:]
-    for shift, strip in enumerate(strips):
-        at = lanes(column_of(-shift), 128)
-        block = strip[...].astype(F32)
-        other = jnp.concatenate([block[W:], -block[:W]], axis=0)
-        wide[:256, at] = block.T.astype(BF)
-        wide[256:, at] = other.T.astype(BF)
     copies = []
-    for i in range(PIECES):
-        at = slice(i * 256, (i + 1) * 256)
-        held[:, :, at] = dot(wide[...], table[:, at]).reshape(2, 256, 256)
-        copy = pltpu.make_async_copy(held.at[:, :, at], out.at[:, :, at], left.at[i])
-        copy.start()
-        copies.append(copy)
+    for part in range(2):
+        for shift, strip in enumerate(strips):
+            block = strip[...].astype(F32)
+            if part == 1:
+                block = jnp.concatenate([block[W:], -block[:W]], axis=0)
+            wide[part * 256 : (part + 1) * 256, lanes(column_of(-shift), 128)] = block.T.astype(BF)
+        for i in range(2):
+            at = slice(i * 128, (i + 1) * 128)
+            held[part, at] = dot(wide[part * 256 + i * 128 : part * 256 + (i + 1) * 128], table[...])
+            copy = pltpu.make_async_copy(
+                held.at[part, at], out.at[part, at], left.at[part * 2 + i]
+            )
+            copy.start(priority=i)
+            copies.append(copy)
     for copy in copies:
         copy.wait()
 
@@ -279,22 +308,31 @@
     strips = pl.pallas_call(
         strip_kernel,
         out_shape=[shaped(128, 256)] * N_COL,
-        in_specs=[VMEM, VMEM],
+        in_specs=[HBM, HBM],
         out_specs=[VMEM] * N_COL,
-        scratch_shapes=[pltpu.VMEM((2, 512, 256), F32)],
+        scratch_shapes=[
+            pltpu.VMEM((2, 256, F), BF),
+            pltpu.VMEM((512, F), BF),
+            pltpu.VMEM((2, 512, 256), F32),
+            pltpu.SemaphoreType.DMA((2 * PIECES,)),
+        ],
         compiler_params=params(),
         cost_estimate=COST,
         name="strip",
-    )(facets, by_column)
+    )(
+        pltpu.with_memory_space_constraint(facets, pltpu.HBM),
+        pltpu.with_memory_space_constraint(by_column, pltpu.HBM),
+    )
     waves = pl.pallas_call(
         wave_kernel,
         out_shape=[
             shaped(2 * S, VIS),
+            shaped(2 * VIS, S),
             shaped(128, VIS, dtype=F32),
             shaped(16, VIS, dtype=F32),
         ],
         in_specs=[VMEM] * 3,
-        out_specs=[VMEM] * 3,
+        out_specs=[VMEM] * 4,
         compiler_params=params(),
         cost_estimate=COST,
         name="wave",
@@ -313,9 +351,9 @@
     returned = pl.pallas_call(
         subgrid_kernel,
         out_shape=shaped(SUBCOL, W, 128),
-        in_specs=[SMEM, SMEM] + [VMEM] * 5,
+        in_specs=[SMEM, SMEM] + [VMEM] * 6,
         out_specs=VMEM,
-        scratch_shapes=[pltpu.VMEM((1024, S), BF), pltpu.VMEM((1024, VIS), BF)],
+        scratch_shapes=[pltpu.VMEM((S, S), BF), pltpu.VMEM((S, 2 * VIS), BF)],
         compiler_params=params(),
         cost_estimate=COST,
         name="subgrid",

time: 64.8 us -> 63.1 us (0.974)
  local copies, waits for them, and re-layouts: 2.53 us -> 0.08 us
  Pallas kernels: 11.1 us -> 11.9 us
    unnamed x26 -> x22, local copies, waits for them, and re-layouts: 2.53 us -> 0.08 us
    pallas_call x1, Pallas kernels: 0.81 us -> 2.27 us  [on_device(): pl.pallas_call(strip_kernel, out_shape=[shaped(128, 256)] * N_COL, in_spe...]
where the time goes in v3:
time: 63.1 us; the launch traced here: 62.9 us
  blocking collectives  36.5 us (58%)
  Pallas kernels  11.9 us (19%)
  starting transfers between devices  9.4 us (15%)
  waiting for transfers between devices  4.91 us (8%)
    all_to_all x1, blocking collectives, on_device(): lax.all_to_all(windows, FACET, split_axis=0, concat_axis=0, tiled=True)  21.4 us
    all_to_all x1, blocking collectives, on_device(): lax.all_to_all(returned, FACET, split_axis=0, concat_axis=0, tiled=True)  15.1 us
    ppermute x6, starting transfers between devices, along_columns(): arrived[shift] = lax.ppermute(parts[shift], 'col', route)  9.4 us
    ppermute x6, waiting for transfers between devices, along_columns(): arrived[shift] = lax.ppermute(parts[shift], 'col', route)  4.91 us
    pallas_call x1, Pallas kernels, on_device(): pl.pallas_call(subgrid_kernel, out_shape=shaped(SUBCOL, W, 128), in_specs...  3.15 us
    pallas_call x1, Pallas kernels, on_device(): pl.pallas_call(strip_kernel, out_shape=[shaped(128, 256)] * N_COL, in_spe...  2.27 us
    pallas_call x1, Pallas kernels, on_device(): pl.pallas_call(window_kernel, out_shape=shaped(SUBCOL, W, 128), in_specs=...  2.08 us
    pallas_call x1, Pallas kernels, on_device(): pl.pallas_call(image_kernel, out_shape=shaped(2, 256, F, dtype=F32), in_s...  1.82 us
  transfers between devices with their start and end apart: 6, of which 4 were waited for; matrix products, arithmetic and copies ran while one was open for 0% of the time, Pallas kernels for 2%

profile of v3, /device:TPU:1, one launch (start us, length us, event | category | flops | bytes accessed | tf_op | source)
XLA Modules:
  0.0 62.9 jit_solution(13879543549939663575)
XLA Ops:
  0.0 0.0 copy-start.6
  0.0 0.0 copy-start.7
  0.0 0.0 copy-start
  0.0 2.3 %strip.1 = (bf16[128,256]{1,0:T(8,128)(2,1)S(1)}, bf16[128,256]{1,0:T(8,128)(2,1)S(1)}, bf16[128,256]{1,0:T(8,128)(2,1)S(1)}, bf16[128,256]{1,0:T(8,128)(2,1)S(1)}) custom-call(bf16[2,256,1024]{2,1,0:T(8,128)(2,1)} %pixels.1, bf16[512,1024]{1,0:T(8,128)(2,1)} %constant.15.clone.table), custom_call_target="tpu_custom_call" | custom-call | flops 20000000000 | bytes 16777216 | tf_op jit(solution)/shard_map/strip/pallas_call | solution.py:308
  2.3 2.2 %collective-permute-start = (bf16[128,256]{1,0:T(8,128)(2,1)S(1)}, bf16[128,256]{1,0:T(8,128)(2,1)S(1)}, u32[]{:S(2)}, u32[]{:S(2)}) collective-permute-start(bf16[128,256]{1,0:T(8,128)(2,1)S(1)} %get-tuple-element.19), channel_id=1, source_target_pairs={{0,1},{1,2},{2,3},{3,0},{4,5},{5,6},{6,7},{7,4},{8,9},{9,10},{10,1... | collective-permute-start | bytes 196616 | tf_op jit(solution)/shard_map/ppermute | solution.py:295
  4.5 2.6 %collective-permute-start.1 = (bf16[128,256]{1,0:T(8,128)(2,1)S(1)}, bf16[128,256]{1,0:T(8,128)(2,1)S(1)}, u32[]{:S(2)}, u32[]{:S(2)}) collective-permute-start(bf16[128,256]{1,0:T(8,128)(2,1)S(1)} %get-tuple-element.20), channel_id=1, source_target_pairs={{0,2},{1,3},{2,0},{3,1},{4,6},{5,7},{6,4},{7,5},{8,10},{9,11},{10,... | collective-permute-start | bytes 196616 | tf_op jit(solution)/shard_map/ppermute | solution.py:295
  7.1 0.0 slice-start
  7.1 0.0 slice-start.1
  7.1 0.0 copy-start.8
  7.1 1.1 %collective-permute-start.2 = (bf16[128,256]{1,0:T(8,128)(2,1)S(1)}, bf16[128,256]{1,0:T(8,128)(2,1)S(1)}, u32[]{:S(2)}, u32[]{:S(2)}) collective-permute-start(bf16[128,256]{1,0:T(8,128)(2,1)S(1)} %get-tuple-element.21), channel_id=1, source_target_pairs={{0,3},{1,0},{2,1},{3,2},{4,7},{5,4},{6,5},{7,6},{8,11},{9,8},{10,9... | collective-permute-start | bytes 196616 | tf_op jit(solution)/shard_map/ppermute | solution.py:295
  8.2 0.0 copy-done.6
  8.2 0.0 copy-done.7
  8.2 0.0 copy-done
  8.2 1.2 %wave.1 = (bf16[1024,1024]{1,0:T(8,128)(2,1)S(1)}, bf16[2048,512]{1,0:T(8,128)(2,1)S(1)}, f32[128,1024]{1,0:T(8,128)S(1)}, f32[16,1024]{1,0:T(8,128)S(1)}) custom-call(s32[2,32,1024]{2,1,0:T(8,128)S(1)} %copy-done, bf16[512,512]{1,0:T(8,128)(2,1)S(1)} %copy-done.6, bf16[288,512]{1,0:T(8,128)(2,1)S(1)} %copy-done.7), custom_call_target="tpu_custom_call" | custom-call | flops 20000000000 | bytes 16777216 | tf_op jit(solution)/shard_map/wave/pallas_call | solution.py:326
  9.4 0.0 collective-permute-done.refs_1_
  9.4 0.3 collective-permute-done.1.refs_2_
  9.7 0.8 %collective-permute-done.2.refs_3_ = bf16[128,256]{1,0:T(8,128)(2,1)S(1)} collective-permute-done((bf16[128,256]{1,0:T(8,128)(2,1)S(1)}, bf16[128,256]{1,0:T(8,128)(2,1)S(1)}, u32[]{:S(2)}, u32[]{:S(2)}) %collective-permute-start.2) | collective-permute-done | bytes 65568 | tf_op jit(solution)/shard_map/ppermute | solution.py:295
  10.5 0.0 slice-done
  10.5 0.0 slice-done.1
  10.6 0.0 copy-done.8
  10.6 0.0 copy-start.1
  10.6 0.0 copy-start.2
  10.6 2.1 %window.1 = bf16[32,64,128]{2,1,0:T(8,128)(2,1)S(1)} custom-call(f32[2,64]{1,0:T(2,128)S(1)} %copy-done.8, bf16[1024,4096]{1,0:T(8,128)(2,1)S(1)} %bitcast.1, f32[16,1024]{1,0:T(8,128)S(1)} %get-tuple-element.17.after.eighth, bf16[128,256]{1,0:T(8,128)(2,1)S(1)} %get-tuple-element.18.refs_0_, bf16[128,256]{1,0:T(8,128)(2,1)S(1)} %collective-permute-done.refs_1_, ...), custom_call_target="tpu_custom_call" | custom-call | flops 20000000000 | bytes 16777216 | tf_op jit(solution)/shard_map/window/pallas_call | solution.py:340
  12.7 21.4 %all_to_all.10.windows = bf16[32,64,128]{2,1,0:T(8,128)(2,1)S(1)} all-to-all(bf16[32,64,128]{2,1,0:T(8,128)(2,1)S(1)} %window.1), channel_id=1, replica_groups=mesh['facet_0'=4,'facet_1'=4,'facet_2'=2,'col'=4] {'facet_0','facet_1','..., dimensions={0} | all-to-all | bytes 1048576 | tf_op jit(solution)/shard_map/all_to_all | solution.py:350
  34.1 0.0 copy-done.1
  34.1 0.0 copy-done.2
  34.1 0.0 copy-start.3
  34.1 0.0 copy-start.4
  34.1 3.1 %subgrid.1 = bf16[32,64,128]{2,1,0:T(8,128)(2,1)S(1)} custom-call(f32[2,64]{1,0:T(2,128)S(1)} %copy-done.8, s32[32]{0:T(128)S(1)} %copy-done.2, bf16[32,64,128]{2,1,0:T(8,128)(2,1)S(1)} %all_to_all.10.windows, f32[2,32,1024]{2,1,0:T(8,128)S(1)} %copy-done.1, bf16[1024,1024]{1,0:T(8,128)(2,1)S(1)} %get-tuple-element.22.left, ...), custom_call_target="tpu_custom_call" | custom-call | flops 20000000000 | bytes 16777216 | tf_op jit(solution)/shard_map/subgrid/pallas_call | solution.py:351
  37.3 15.1 %all_to_all.11.returned = bf16[32,64,128]{2,1,0:T(8,128)(2,1)S(1)} all-to-all(bf16[32,64,128]{2,1,0:T(8,128)(2,1)S(1)} %subgrid.1), channel_id=1, replica_groups=mesh['facet_0'=4,'facet_1'=4,'facet_2'=2,'col'=4] {'facet_0','facet_1','..., dimensions={0} | all-to-all | bytes 1048576 | tf_op jit(solution)/shard_map/all_to_all | solution.py:361
  52.3 0.0 copy-done.3
  52.3 0.0 copy-done.4
  52.3 0.0 copy-start.5
  52.3 1.4 %back.1 = (bf16[128,256]{1,0:T(8,128)(2,1)S(1)}, bf16[128,256]{1,0:T(8,128)(2,1)S(1)}, bf16[128,256]{1,0:T(8,128)(2,1)S(1)}, bf16[128,256]{1,0:T(8,128)(2,1)S(1)}) custom-call(bf16[32,64,128]{2,1,0:T(8,128)(2,1)S(1)} %all_to_all.11.returned, bf16[2048,1024]{1,0:T(8,128)(2,1)S(1)} %copy-done.4, bf16[2048,1024]{1,0:T(8,128)(2,1)S(1)} %copy-done.3), custom_call_target="tpu_custom_call" | custom-call | flops 20000000000 | bytes 16777216 | tf_op jit(solution)/shard_map/back/pallas_call | solution.py:362
  53.8 0.1 collective-permute-start.3
  53.9 3.4 %collective-permute-start.4 = (bf16[128,256]{1,0:T(8,128)(2,1)S(1)}, bf16[128,256]{1,0:T(8,128)(2,1)S(1)}, u32[]{:S(2)}, u32[]{:S(2)}) collective-permute-start(bf16[128,256]{1,0:T(8,128)(2,1)S(1)} %get-tuple-element.27), channel_id=1, source_target_pairs={{0,2},{1,3},{2,0},{3,1},{4,6},{5,7},{6,4},{7,5},{8,10},{9,11},{10,... | collective-permute-start | bytes 196616 | tf_op jit(solution)/shard_map/ppermute | solution.py:295
  57.3 0.0 collective-permute-start.5
  57.3 1.6 %collective-permute-done.3.refs_1_ = bf16[128,256]{1,0:T(8,128)(2,1)S(1)} collective-permute-done((bf16[128,256]{1,0:T(8,128)(2,1)S(1)}, bf16[128,256]{1,0:T(8,128)(2,1)S(1)}, u32[]{:S(2)}, u32[]{:S(2)}) %collective-permute-start.3) | collective-permute-done | bytes 65568 | tf_op jit(solution)/shard_map/ppermute | solution.py:295
  58.9 2.2 %collective-permute-done.4.refs_2_ = bf16[128,256]{1,0:T(8,128)(2,1)S(1)} collective-permute-done((bf16[128,256]{1,0:T(8,128)(2,1)S(1)}, bf16[128,256]{1,0:T(8,128)(2,1)S(1)}, u32[]{:S(2)}, u32[]{:S(2)}) %collective-permute-start.4) | collective-permute-done | bytes 65568 | tf_op jit(solution)/shard_map/ppermute | solution.py:295
  61.1 0.0 collective-permute-done.5.refs_3_
  61.1 0.0 copy-done.5
  61.1 1.8 %image.1 = f32[2,256,1024]{2,1,0:T(8,128)} custom-call(bf16[512,1024]{1,0:T(8,128)(2,1)S(1)} %copy-done.5, bf16[128,256]{1,0:T(8,128)(2,1)S(1)} %get-tuple-element.25.refs_0_, bf16[128,256]{1,0:T(8,128)(2,1)S(1)} %collective-permute-done.3.refs_1_, bf16[128,256]{1,0:T(8,128)(2,1)S(1)} %collective-permute-done.4.refs_2_, ...), custom_call_target="tpu_custom_call" | custom-call | flops 20000000000 | bytes 16777216 | tf_op jit(solution)/shard_map/image/pallas_call | solution.py:372
  (1 shorter events, 0.0 us)
Async XLA Ops:
  0.0 8.2 %copy-start.6 = (bf16[512,512]{1,0:T(8,128)(2,1)S(1)}, bf16[512,512]{1,0:T(8,128)(2,1)}, u32[]{:S(2)}) copy-start(bf16[512,512]{1,0:T(8,128)(2,1)} %constant.18.clone.left_tab) | copy-start | bytes 1572868
  0.0 8.2 %copy-start.7 = (bf16[288,512]{1,0:T(8,128)(2,1)S(1)}, bf16[288,512]{1,0:T(8,128)(2,1)}, u32[]{:S(2)}) copy-start(bf16[288,512]{1,0:T(8,128)(2,1)} %constant.19.clone.right_tab) | copy-start | bytes 884740
  0.0 8.2 %copy-start = (s32[2,32,1024]{2,1,0:T(8,128)S(1)}, s32[2,32,1024]{2,1,0:T(8,128)}, u32[]{:S(2)}) copy-start(s32[2,32,1024]{2,1,0:T(8,128)} %cells.1) | copy-start | bytes 786436
  2.3 7.1 %collective-permute-start = (bf16[128,256]{1,0:T(8,128)(2,1)S(1)}, bf16[128,256]{1,0:T(8,128)(2,1)S(1)}, u32[]{:S(2)}, u32[]{:S(2)}) collective-permute-start(bf16[128,256]{1,0:T(8,128)(2,1)S(1)} %get-tuple-element.19), channel_id=1, source_target_pairs={{0,1},{1,2},{2,3},{3,0},{4,5},{5,6},{6,7},{7,4},{8,9},{9,10},{10,1... | collective-permute-start | bytes 196616 | tf_op jit(solution)/shard_map/ppermute | solution.py:295
  4.5 5.2 %collective-permute-start.1 = (bf16[128,256]{1,0:T(8,128)(2,1)S(1)}, bf16[128,256]{1,0:T(8,128)(2,1)S(1)}, u32[]{:S(2)}, u32[]{:S(2)}) collective-permute-start(bf16[128,256]{1,0:T(8,128)(2,1)S(1)} %get-tuple-element.20), channel_id=1, source_target_pairs={{0,2},{1,3},{2,0},{3,1},{4,6},{5,7},{6,4},{7,5},{8,10},{9,11},{10,... | collective-permute-start | bytes 196616 | tf_op jit(solution)/shard_map/ppermute | solution.py:295
  7.1 3.4 %slice-start = ((s8[8388608]{0:T(1024)(128)(4,1)}), s8[4194304]{0:T(1024)(128)(4,1)S(1)}, s32[]{:S(2)}) async-start(s8[8388608]{0:T(1024)(128)(4,1)} %bitcast), calls=%async_computation.2 | async-start | bytes 8388608
  7.1 3.5 %slice-start.1 = ((s8[8388608]{0:T(1024)(128)(4,1)}), s8[4194304]{0:T(1024)(128)(4,1)S(1)}, s32[]{:S(2)}) async-start(s8[8388608]{0:T(1024)(128)(4,1)} %bitcast), calls=%async_computation.3 | async-start | bytes 8388608
  7.1 3.5 %copy-start.8 = (f32[2,64]{1,0:T(2,128)S(1)}, f32[2,64]{1,0:T(2,128)}, u32[]{:S(2)}) copy-start(f32[2,64]{1,0:T(2,128)} %constant.14.clone.units) | copy-start | bytes 1540
  7.1 3.4 %collective-permute-start.2 = (bf16[128,256]{1,0:T(8,128)(2,1)S(1)}, bf16[128,256]{1,0:T(8,128)(2,1)S(1)}, u32[]{:S(2)}, u32[]{:S(2)}) collective-permute-start(bf16[128,256]{1,0:T(8,128)(2,1)S(1)} %get-tuple-element.21), channel_id=1, source_target_pairs={{0,3},{1,0},{2,1},{3,2},{4,7},{5,4},{6,5},{7,6},{8,11},{9,8},{10,9... | collective-permute-start | bytes 196616 | tf_op jit(solution)/shard_map/ppermute | solution.py:295
  10.6 23.5 %copy-start.1 = (f32[2,32,1024]{2,1,0:T(8,128)S(1)}, f32[2,32,1024]{2,1,0:T(8,128)}, u32[]{:S(2)}) copy-start(f32[2,32,1024]{2,1,0:T(8,128)} %observed.1) | copy-start | bytes 786436
  10.6 23.5 %copy-start.2 = (s32[32]{0:T(128)S(1)}, s32[32]{0:T(128)}, u32[]{:S(2)}) copy-start(s32[32]{0:T(128)} %counts.1) | copy-start | bytes 388
  34.1 18.2 %copy-start.3 = (bf16[2048,1024]{1,0:T(8,128)(2,1)S(1)}, bf16[2048,1024]{1,0:T(8,128)(2,1)}, u32[]{:S(2)}) copy-start(bf16[2048,1024]{1,0:T(8,128)(2,1)} %constant.17.clone.refs_1_) | copy-start | bytes 12582916
  34.1 18.2 %copy-start.4 = (bf16[2048,1024]{1,0:T(8,128)(2,1)S(1)}, bf16[2048,1024]{1,0:T(8,128)(2,1)}, u32[]{:S(2)}) copy-start(bf16[2048,1024]{1,0:T(8,128)(2,1)} %constant.16.clone.refs_0_) | copy-start | bytes 12582916
  52.3 8.7 %copy-start.5 = (bf16[512,1024]{1,0:T(8,128)(2,1)S(1)}, bf16[512,1024]{1,0:T(8,128)(2,1)}, u32[]{:S(2)}) copy-start(bf16[512,1024]{1,0:T(8,128)(2,1)} %constant.15.clone.table) | copy-start | bytes 3145732
  53.8 5.1 %collective-permute-start.3 = (bf16[128,256]{1,0:T(8,128)(2,1)S(1)}, bf16[128,256]{1,0:T(8,128)(2,1)S(1)}, u32[]{:S(2)}, u32[]{:S(2)}) collective-permute-start(bf16[128,256]{1,0:T(8,128)(2,1)S(1)} %get-tuple-element.26), channel_id=1, source_target_pairs={{0,1},{1,2},{2,3},{3,0},{4,5},{5,6},{6,7},{7,4},{8,9},{9,10},{10,1... | collective-permute-start | bytes 196616 | tf_op jit(solution)/shard_map/ppermute | solution.py:295
  53.9 7.2 %collective-permute-start.4 = (bf16[128,256]{1,0:T(8,128)(2,1)S(1)}, bf16[128,256]{1,0:T(8,128)(2,1)S(1)}, u32[]{:S(2)}, u32[]{:S(2)}) collective-permute-start(bf16[128,256]{1,0:T(8,128)(2,1)S(1)} %get-tuple-element.27), channel_id=1, source_target_pairs={{0,2},{1,3},{2,0},{3,1},{4,6},{5,7},{6,4},{7,5},{8,10},{9,11},{10,... | collective-permute-start | bytes 196616 | tf_op jit(solution)/shard_map/ppermute | solution.py:295
  57.3 3.8 %collective-permute-start.5 = (bf16[128,256]{1,0:T(8,128)(2,1)S(1)}, bf16[128,256]{1,0:T(8,128)(2,1)S(1)}, u32[]{:S(2)}, u32[]{:S(2)}) collective-permute-start(bf16[128,256]{1,0:T(8,128)(2,1)S(1)} %get-tuple-element.28), channel_id=1, source_target_pairs={{0,3},{1,0},{2,1},{3,2},{4,7},{5,4},{6,5},{7,6},{8,11},{9,8},{10,9... | collective-permute-start | bytes 196616 | tf_op jit(solution)/shard_map/ppermute | solution.py:295

commit v4 on v3

--- a/solution.py
+++ b/solution.py
@@ -64,7 +64,8 @@
 
 def left_rows():
     real, imag = unit(np.arange(256)[:, None] * np.arange(S)[None, :], S)
-    return bf(np.stack([real.reshape(4, W, S), -imag.reshape(4, W, S)], axis=1).reshape(S, S))
+    both = np.stack([real.reshape(4, W, S), -imag.reshape(4, W, S)], axis=1)
+    return np.concatenate(hi_lo(both.reshape(S, S)))
 
 
 def right_rows():
@@ -90,11 +91,8 @@
     return pltpu.roll(values, W, 1)
 
 
-def scalar_phase(units, facet_row, facet_col, subgrid, column):
-    shift = (37 * subgrid + 5) & 1023
-    anchor = (29 * column + 3) & 63
-    tick = (facet_row * shift + facet_col * anchor) & 63
-    return units[0, tick], units[1, tick]
+def scalar_phase(units, tick):
+    return units[0, tick & 63], units[1, tick & 63]
 
 
 def column_of(shift):
@@ -142,11 +140,9 @@
         out[W:] = (real[W:] + imag[:W]).astype(BF)
 
 
-def window_kernel(units, table, after, *refs):
+def window_kernel(table, after, *refs):
     strips = refs[:N_COL]
     out, turned = refs[N_COL:]
-    facet = lax.axis_index(FACET)
-    column = lax.axis_index("col")
     for shift, strip in enumerate(strips):
         turned[:, lanes(column_of(-shift), 256)] = strip[...]
     sign = half_sign((W, 128))
@@ -155,41 +151,49 @@
         both = dot(turned[...], table[:, step * group * 128 : (step + 1) * group * 128])
         for g in range(group):
             at = slice(g * 128, (g + 1) * 128)
-            block = both[:W, at] + sign * swap(both[W:, at])
-            real, imag = scalar_phase(units, facet // 8, facet % 8, step * group + g, column)
-            out[step * group + g] = (block * real + sign * swap(block) * imag).astype(BF)
-
-
-def wave_kernel(cells, left_tab, right_tab, left, left_by_slot, base, eighth):
+            out[step * group + g] = (both[:W, at] + sign * swap(both[W:, at])).astype(BF)
+
+
+def wave_kernel(units, cells, left_tab, right_tab, left, left_by_slot, base, eighth):
     subgrid = lax.axis_index(FACET)
+    shift = (37 * subgrid + 5) & 1023
+    anchor = (29 * lax.axis_index("col") + 3) & 63
     for begin in range(0, VIS, CHUNK):
         at = slice(begin, begin + CHUNK)
         first = cells[0, pl.ds(subgrid, 1), at]
         second = cells[1, pl.ds(subgrid, 1), at]
         cell = lax.broadcasted_iota(jnp.int32, (S, CHUNK), 0)
         picked = dot(left_tab[...], jnp.where(cell == first, 1.0, 0.0).astype(BF))
-        other = jnp.concatenate(
-            [
-                part
-                for x in range(4)
-                for part in (-picked[x * 128 + W : (x + 1) * 128], picked[x * 128 : x * 128 + W])
-            ],
-            axis=0,
-        )
+        picked = picked[:S] + picked[S:]
+        first_rows, second_rows = [], []
+        for x in range(4):
+            real, imag = scalar_phase(units, x * shift)
+            upper = picked[x * 128 : x * 128 + W]
+            lower = picked[x * 128 + W : (x + 1) * 128]
+            turned_real = upper * real + lower * imag
+            turned_imag = upper * imag - lower * real
+            first_rows += [turned_real, -turned_imag]
+            second_rows += [turned_imag, turned_real]
+        picked = jnp.concatenate(first_rows, axis=0)
+        other = jnp.concatenate(second_rows, axis=0)
         left[:S, at] = picked.astype(BF)
         left[S:, at] = other.astype(BF)
         left_by_slot[at] = picked.T.astype(BF)
         left_by_slot[VIS + begin : VIS + begin + CHUNK] = other.T.astype(BF)
         right = dot(right_tab[...], jnp.where(cell == second, 1.0, 0.0).astype(BF))
         base[:, at] = right[0:128] + right[128:256]
-        eighth[:, at] = right[256:272] + right[272:288]
+        for y in range(8):
+            real, imag = scalar_phase(units, y * anchor)
+            upper = right[256 + y : 257 + y] + right[272 + y : 273 + y]
+            lower = right[264 + y : 265 + y] + right[280 + y : 281 + y]
+            eighth[y : y + 1, at] = upper * real - lower * imag
+            eighth[8 + y : 9 + y, at] = upper * imag + lower * real
 
 
 def subgrid_kernel(
-    units, counts, windows, observed, left, left_by_slot, base, eighth, out, held, weighted
+    counts, windows, observed, left, left_by_slot, base, eighth, out, held, weighted
 ):
     subgrid = lax.axis_index(FACET)
-    column = lax.axis_index("col")
     count = counts[subgrid]
     for x in range(4):
         for y in range(8):
@@ -227,17 +231,13 @@
             weighted[here, VIS + begin : VIS + begin + CHUNK] = (
                 turned_imag * base_real - turned_real * base_imag
             ).astype(BF)
-    sign = half_sign((W, 128))
     scale = 1.0 / math.sqrt(VIS)
     for y0 in range(0, 8, GROUP):
         both = dot(weighted[y0 * W : (y0 + GROUP) * W], left_by_slot[...])
         for y in range(y0, y0 + GROUP):
             for x in range(4):
                 block = both[(y - y0) * W : (y - y0 + 1) * W, x * 128 : (x + 1) * 128]
-                real, imag = scalar_phase(units, x, y, subgrid, column)
-                out[x * 8 + y] = (
-                    block * (real * scale) - sign * swap(block) * (imag * scale)
-                ).astype(BF)
+                out[x * 8 + y] = (block * scale).astype(BF)
 
 
 def back_kernel(returned, *refs):
@@ -331,33 +331,33 @@
             shaped(128, VIS, dtype=F32),
             shaped(16, VIS, dtype=F32),
         ],
-        in_specs=[VMEM] * 3,
+        in_specs=[SMEM] + [VMEM] * 3,
         out_specs=[VMEM] * 4,
         compiler_params=params(),
         cost_estimate=COST,
         name="wave",
-    )(uv_cells, jnp.asarray(left_rows()), jnp.asarray(right_rows()))
+    )(units, uv_cells, jnp.asarray(left_rows()), jnp.asarray(right_rows()))
     windows = pl.pallas_call(
         window_kernel,
         out_shape=shaped(SUBCOL, W, 128),
-        in_specs=[SMEM, VMEM, pl.BlockSpec(memory_space=pl.ANY)] + [VMEM] * N_COL,
+        in_specs=[VMEM, pl.BlockSpec(memory_space=pl.ANY)] + [VMEM] * N_COL,
         out_specs=VMEM,
         scratch_shapes=[pltpu.VMEM((128, F), BF)],
         compiler_params=params(),
         cost_estimate=COST,
         name="window",
-    )(units, jnp.asarray(np.ascontiguousarray(by_window.T)), waves[-1], *along_columns(strips))
+    )(jnp.asarray(np.ascontiguousarray(by_window.T)), waves[-1], *along_columns(strips))
     windows = lax.all_to_all(windows, FACET, split_axis=0, concat_axis=0, tiled=True)
     returned = pl.pallas_call(
         subgrid_kernel,
         out_shape=shaped(SUBCOL, W, 128),
-        in_specs=[SMEM, SMEM] + [VMEM] * 6,
+        in_specs=[SMEM] + [VMEM] * 6,
         out_specs=VMEM,
         scratch_shapes=[pltpu.VMEM((S, S), BF), pltpu.VMEM((S, 2 * VIS), BF)],
         compiler_params=params(),
         cost_estimate=COST,
         name="subgrid",
-    )(units, counts, windows, observed, *waves)
+    )(counts, windows, observed, *waves)
     returned = lax.all_to_all(returned, FACET, split_axis=0, concat_axis=0, tiled=True)
     back = pl.pallas_call(
         back_kernel,

time: 63.1 us -> 62.3 us (0.987)
  waiting for transfers between devices: 4.91 us -> 3.78 us
    pallas_call x1, Pallas kernels: 1.18 us -> 2.4 us  [on_device(): pl.pallas_call(wave_kernel, out_shape=[shaped(2 * S, VIS), shaped(2 * VIS...]
    ppermute x6, waiting for transfers between devices: 4.91 us -> 3.78 us  [along_columns(): arrived[shift] = lax.ppermute(parts[shift], 'col', route)]
    pallas_call x1, Pallas kernels: 2.08 us -> 1.37 us  [on_device(): pl.pallas_call(window_kernel, out_shape=shaped(SUBCOL, W, 128), in_specs=...]
  transfers between devices with their start and end apart: 6 -> 6, of which waited for: 4 -> 2; matrix products, arithmetic and copies ran while one was open for 0% -> 0% of each run, Pallas kernels for 2% -> 4%
where the time goes in v4:
time: 62.3 us; the launch traced here: 62.2 us
  blocking collectives  36.3 us (58%)
  Pallas kernels  12.4 us (20%)
  starting transfers between devices  9.46 us (15%)
  waiting for transfers between devices  3.78 us (6%)
    all_to_all x1, blocking collectives, on_device(): lax.all_to_all(windows, FACET, split_axis=0, concat_axis=0, tiled=True)  21.3 us
    all_to_all x1, blocking collectives, on_device(): lax.all_to_all(returned, FACET, split_axis=0, concat_axis=0, tiled=True)  15 us
    ppermute x6, starting transfers between devices, along_columns(): arrived[shift] = lax.ppermute(parts[shift], 'col', route)  9.46 us
    ppermute x6, waiting for transfers between devices, along_columns(): arrived[shift] = lax.ppermute(parts[shift], 'col', route)  3.78 us
    pallas_call x1, Pallas kernels, on_device(): pl.pallas_call(subgrid_kernel, out_shape=shaped(SUBCOL, W, 128), in_specs...  3.1 us
    pallas_call x1, Pallas kernels, on_device(): pl.pallas_call(wave_kernel, out_shape=[shaped(2 * S, VIS), shaped(2 * VIS...  2.4 us
    pallas_call x1, Pallas kernels, on_device(): pl.pallas_call(strip_kernel, out_shape=[shaped(128, 256)] * N_COL, in_spe...  2.3 us
    pallas_call x1, Pallas kernels, on_device(): pl.pallas_call(image_kernel, out_shape=shaped(2, 256, F, dtype=F32), in_s...  1.82 us
  transfers between devices with their start and end apart: 6, of which 2 were waited for; matrix products, arithmetic and copies ran while one was open for 0% of the time, Pallas kernels for 4%

profile of v4, /device:TPU:1, one launch (start us, length us, event | category | flops | bytes accessed | tf_op | source)
XLA Modules:
  0.0 62.2 jit_solution(17870238192289261157)
XLA Ops:
  0.0 0.0 copy-start.6
  0.0 0.0 copy-start.7
  0.0 0.0 copy-start.8
  0.0 0.0 copy-start
  0.0 2.3 %strip.1 = (bf16[128,256]{1,0:T(8,128)(2,1)S(1)}, bf16[128,256]{1,0:T(8,128)(2,1)S(1)}, bf16[128,256]{1,0:T(8,128)(2,1)S(1)}, bf16[128,256]{1,0:T(8,128)(2,1)S(1)}) custom-call(bf16[2,256,1024]{2,1,0:T(8,128)(2,1)} %pixels.1, bf16[512,1024]{1,0:T(8,128)(2,1)} %constant.15.clone.table), custom_call_target="tpu_custom_call" | custom-call | flops 20000000000 | bytes 16777216 | tf_op jit(solution)/shard_map/strip/pallas_call | solution.py:308
  2.3 2.2 %collective-permute-start = (bf16[128,256]{1,0:T(8,128)(2,1)S(1)}, bf16[128,256]{1,0:T(8,128)(2,1)S(1)}, u32[]{:S(2)}, u32[]{:S(2)}) collective-permute-start(bf16[128,256]{1,0:T(8,128)(2,1)S(1)} %get-tuple-element.19), channel_id=1, source_target_pairs={{0,1},{1,2},{2,3},{3,0},{4,5},{5,6},{6,7},{7,4},{8,9},{9,10},{10,1... | collective-permute-start | bytes 196616 | tf_op jit(solution)/shard_map/ppermute | solution.py:295
  4.5 2.6 %collective-permute-start.1 = (bf16[128,256]{1,0:T(8,128)(2,1)S(1)}, bf16[128,256]{1,0:T(8,128)(2,1)S(1)}, u32[]{:S(2)}, u32[]{:S(2)}) collective-permute-start(bf16[128,256]{1,0:T(8,128)(2,1)S(1)} %get-tuple-element.20), channel_id=1, source_target_pairs={{0,2},{1,3},{2,0},{3,1},{4,6},{5,7},{6,4},{7,5},{8,10},{9,11},{10,... | collective-permute-start | bytes 196616 | tf_op jit(solution)/shard_map/ppermute | solution.py:295
  7.1 0.0 slice-start
  7.1 0.0 slice-start.1
  7.1 1.1 %collective-permute-start.2 = (bf16[128,256]{1,0:T(8,128)(2,1)S(1)}, bf16[128,256]{1,0:T(8,128)(2,1)S(1)}, u32[]{:S(2)}, u32[]{:S(2)}) collective-permute-start(bf16[128,256]{1,0:T(8,128)(2,1)S(1)} %get-tuple-element.21), channel_id=1, source_target_pairs={{0,3},{1,0},{2,1},{3,2},{4,7},{5,4},{6,5},{7,6},{8,11},{9,8},{10,9... | collective-permute-start | bytes 196616 | tf_op jit(solution)/shard_map/ppermute | solution.py:295
  8.2 0.0 copy-done.6
  8.2 0.0 copy-done.7
  8.2 0.0 copy-done.8
  8.2 0.0 copy-done
  8.2 2.4 %wave.1 = (bf16[1024,1024]{1,0:T(8,128)(2,1)S(1)}, bf16[2048,512]{1,0:T(8,128)(2,1)S(1)}, f32[128,1024]{1,0:T(8,128)S(1)}, f32[16,1024]{1,0:T(8,128)S(1)}) custom-call(f32[2,64]{1,0:T(2,128)S(1)} %copy-done.8, s32[2,32,1024]{2,1,0:T(8,128)S(1)} %copy-done, bf16[1024,512]{1,0:T(8,128)(2,1)S(1)} %copy-done.6, bf16[288,512]{1,0:T(8,128)(2,1)S(1)} %copy-done.7), custom_call_target="tpu_custom_call" | custom-call | flops 20000000000 | bytes 16777216 | tf_op jit(solution)/shard_map/wave/pallas_call | solution.py:326
  10.6 0.0 collective-permute-done.refs_1_
  10.6 0.0 collective-permute-done.1.refs_2_
  10.7 0.0 collective-permute-done.2.refs_3_
  10.7 0.0 slice-done
  10.7 0.0 slice-done.1
  10.7 0.0 copy-start.1
  10.7 0.0 copy-start.2
  10.7 1.4 %window.1 = bf16[32,64,128]{2,1,0:T(8,128)(2,1)S(1)} custom-call(bf16[1024,4096]{1,0:T(8,128)(2,1)S(1)} %bitcast.1, f32[16,1024]{1,0:T(8,128)S(1)} %get-tuple-element.17.after.eighth, bf16[128,256]{1,0:T(8,128)(2,1)S(1)} %get-tuple-element.18.refs_0_, bf16[128,256]{1,0:T(8,128)(2,1)S(1)} %collective-permute-done.refs_1_, ...), custom_call_target="tpu_custom_call" | custom-call | flops 20000000000 | bytes 16777216 | tf_op jit(solution)/shard_map/window/pallas_call | solution.py:340
  12.1 21.3 %all_to_all.10.windows = bf16[32,64,128]{2,1,0:T(8,128)(2,1)S(1)} all-to-all(bf16[32,64,128]{2,1,0:T(8,128)(2,1)S(1)} %window.1), channel_id=1, replica_groups=mesh['facet_0'=4,'facet_1'=4,'facet_2'=2,'col'=4] {'facet_0','facet_1','..., dimensions={0} | all-to-all | bytes 1048576 | tf_op jit(solution)/shard_map/all_to_all | solution.py:350
  33.4 0.0 copy-done.1
  33.4 0.0 copy-done.2
  33.4 0.0 copy-start.3
  33.4 0.0 copy-start.4
  33.4 3.1 %subgrid.1 = bf16[32,64,128]{2,1,0:T(8,128)(2,1)S(1)} custom-call(s32[32]{0:T(128)S(1)} %copy-done.2, bf16[32,64,128]{2,1,0:T(8,128)(2,1)S(1)} %all_to_all.10.windows, f32[2,32,1024]{2,1,0:T(8,128)S(1)} %copy-done.1, bf16[1024,1024]{1,0:T(8,128)(2,1)S(1)} %get-tuple-element.22.left, bf16[2048,512]{1,0:T(8,128)(2,1)S(1)} %get-tuple-element.23.left_by_slot, ...), custom_call_target="tpu_custom_call" | custom-call | flops 20000000000 | bytes 16777216 | tf_op jit(solution)/shard_map/subgrid/pallas_call | solution.py:351
  36.5 15.0 %all_to_all.11.returned = bf16[32,64,128]{2,1,0:T(8,128)(2,1)S(1)} all-to-all(bf16[32,64,128]{2,1,0:T(8,128)(2,1)S(1)} %subgrid.1), channel_id=1, replica_groups=mesh['facet_0'=4,'facet_1'=4,'facet_2'=2,'col'=4] {'facet_0','facet_1','..., dimensions={0} | all-to-all | bytes 1048576 | tf_op jit(solution)/shard_map/all_to_all | solution.py:361
  51.6 0.0 copy-done.3
  51.6 0.0 copy-done.4
  51.6 0.0 copy-start.5
  51.6 1.4 %back.1 = (bf16[128,256]{1,0:T(8,128)(2,1)S(1)}, bf16[128,256]{1,0:T(8,128)(2,1)S(1)}, bf16[128,256]{1,0:T(8,128)(2,1)S(1)}, bf16[128,256]{1,0:T(8,128)(2,1)S(1)}) custom-call(bf16[32,64,128]{2,1,0:T(8,128)(2,1)S(1)} %all_to_all.11.returned, bf16[2048,1024]{1,0:T(8,128)(2,1)S(1)} %copy-done.4, bf16[2048,1024]{1,0:T(8,128)(2,1)S(1)} %copy-done.3), custom_call_target="tpu_custom_call" | custom-call | flops 20000000000 | bytes 16777216 | tf_op jit(solution)/shard_map/back/pallas_call | solution.py:362
  53.0 0.1 collective-permute-start.3
  53.1 3.4 %collective-permute-start.4 = (bf16[128,256]{1,0:T(8,128)(2,1)S(1)}, bf16[128,256]{1,0:T(8,128)(2,1)S(1)}, u32[]{:S(2)}, u32[]{:S(2)}) collective-permute-start(bf16[128,256]{1,0:T(8,128)(2,1)S(1)} %get-tuple-element.27), channel_id=1, source_target_pairs={{0,2},{1,3},{2,0},{3,1},{4,6},{5,7},{6,4},{7,5},{8,10},{9,11},{10,... | collective-permute-start | bytes 196616 | tf_op jit(solution)/shard_map/ppermute | solution.py:295
  56.6 0.0 collective-permute-start.5
  56.6 1.5 %collective-permute-done.3.refs_1_ = bf16[128,256]{1,0:T(8,128)(2,1)S(1)} collective-permute-done((bf16[128,256]{1,0:T(8,128)(2,1)S(1)}, bf16[128,256]{1,0:T(8,128)(2,1)S(1)}, u32[]{:S(2)}, u32[]{:S(2)}) %collective-permute-start.3) | collective-permute-done | bytes 65568 | tf_op jit(solution)/shard_map/ppermute | solution.py:295
  58.1 2.2 %collective-permute-done.4.refs_2_ = bf16[128,256]{1,0:T(8,128)(2,1)S(1)} collective-permute-done((bf16[128,256]{1,0:T(8,128)(2,1)S(1)}, bf16[128,256]{1,0:T(8,128)(2,1)S(1)}, u32[]{:S(2)}, u32[]{:S(2)}) %collective-permute-start.4) | collective-permute-done | bytes 65568 | tf_op jit(solution)/shard_map/ppermute | solution.py:295
  60.3 0.0 collective-permute-done.5.refs_3_
  60.3 0.0 copy-done.5
  60.3 1.8 %image.1 = f32[2,256,1024]{2,1,0:T(8,128)} custom-call(bf16[512,1024]{1,0:T(8,128)(2,1)S(1)} %copy-done.5, bf16[128,256]{1,0:T(8,128)(2,1)S(1)} %get-tuple-element.25.refs_0_, bf16[128,256]{1,0:T(8,128)(2,1)S(1)} %collective-permute-done.3.refs_1_, bf16[128,256]{1,0:T(8,128)(2,1)S(1)} %collective-permute-done.4.refs_2_, ...), custom_call_target="tpu_custom_call" | custom-call | flops 20000000000 | bytes 16777216 | tf_op jit(solution)/shard_map/image/pallas_call | solution.py:372
  (1 shorter events, 0.0 us)
Async XLA Ops:
  0.0 8.2 %copy-start.6 = (bf16[1024,512]{1,0:T(8,128)(2,1)S(1)}, bf16[1024,512]{1,0:T(8,128)(2,1)}, u32[]{:S(2)}) copy-start(bf16[1024,512]{1,0:T(8,128)(2,1)} %constant.18.clone.left_tab) | copy-start | bytes 3145732
  0.0 8.2 %copy-start.7 = (bf16[288,512]{1,0:T(8,128)(2,1)S(1)}, bf16[288,512]{1,0:T(8,128)(2,1)}, u32[]{:S(2)}) copy-start(bf16[288,512]{1,0:T(8,128)(2,1)} %constant.19.clone.right_tab) | copy-start | bytes 884740
  0.0 8.2 %copy-start.8 = (f32[2,64]{1,0:T(2,128)S(1)}, f32[2,64]{1,0:T(2,128)}, u32[]{:S(2)}) copy-start(f32[2,64]{1,0:T(2,128)} %constant.14.clone.units) | copy-start | bytes 1540
  0.0 8.2 %copy-start = (s32[2,32,1024]{2,1,0:T(8,128)S(1)}, s32[2,32,1024]{2,1,0:T(8,128)}, u32[]{:S(2)}) copy-start(s32[2,32,1024]{2,1,0:T(8,128)} %cells.1) | copy-start | bytes 786436
  2.3 8.3 %collective-permute-start = (bf16[128,256]{1,0:T(8,128)(2,1)S(1)}, bf16[128,256]{1,0:T(8,128)(2,1)S(1)}, u32[]{:S(2)}, u32[]{:S(2)}) collective-permute-start(bf16[128,256]{1,0:T(8,128)(2,1)S(1)} %get-tuple-element.19), channel_id=1, source_target_pairs={{0,1},{1,2},{2,3},{3,0},{4,5},{5,6},{6,7},{7,4},{8,9},{9,10},{10,1... | collective-permute-start | bytes 196616 | tf_op jit(solution)/shard_map/ppermute | solution.py:295
  4.5 6.1 %collective-permute-start.1 = (bf16[128,256]{1,0:T(8,128)(2,1)S(1)}, bf16[128,256]{1,0:T(8,128)(2,1)S(1)}, u32[]{:S(2)}, u32[]{:S(2)}) collective-permute-start(bf16[128,256]{1,0:T(8,128)(2,1)S(1)} %get-tuple-element.20), channel_id=1, source_target_pairs={{0,2},{1,3},{2,0},{3,1},{4,6},{5,7},{6,4},{7,5},{8,10},{9,11},{10,... | collective-permute-start | bytes 196616 | tf_op jit(solution)/shard_map/ppermute | solution.py:295
  7.1 3.5 %slice-start = ((s8[8388608]{0:T(1024)(128)(4,1)}), s8[4194304]{0:T(1024)(128)(4,1)S(1)}, s32[]{:S(2)}) async-start(s8[8388608]{0:T(1024)(128)(4,1)} %bitcast), calls=%async_computation.2 | async-start | bytes 8388608
  7.1 3.5 %slice-start.1 = ((s8[8388608]{0:T(1024)(128)(4,1)}), s8[4194304]{0:T(1024)(128)(4,1)S(1)}, s32[]{:S(2)}) async-start(s8[8388608]{0:T(1024)(128)(4,1)} %bitcast), calls=%async_computation.3 | async-start | bytes 8388608
  7.1 3.5 %collective-permute-start.2 = (bf16[128,256]{1,0:T(8,128)(2,1)S(1)}, bf16[128,256]{1,0:T(8,128)(2,1)S(1)}, u32[]{:S(2)}, u32[]{:S(2)}) collective-permute-start(bf16[128,256]{1,0:T(8,128)(2,1)S(1)} %get-tuple-element.21), channel_id=1, source_target_pairs={{0,3},{1,0},{2,1},{3,2},{4,7},{5,4},{6,5},{7,6},{8,11},{9,8},{10,9... | collective-permute-start | bytes 196616 | tf_op jit(solution)/shard_map/ppermute | solution.py:295
  10.7 22.7 %copy-start.1 = (f32[2,32,1024]{2,1,0:T(8,128)S(1)}, f32[2,32,1024]{2,1,0:T(8,128)}, u32[]{:S(2)}) copy-start(f32[2,32,1024]{2,1,0:T(8,128)} %observed.1) | copy-start | bytes 786436
  10.7 22.7 %copy-start.2 = (s32[32]{0:T(128)S(1)}, s32[32]{0:T(128)}, u32[]{:S(2)}) copy-start(s32[32]{0:T(128)} %counts.1) | copy-start | bytes 388
  33.4 18.2 %copy-start.3 = (bf16[2048,1024]{1,0:T(8,128)(2,1)S(1)}, bf16[2048,1024]{1,0:T(8,128)(2,1)}, u32[]{:S(2)}) copy-start(bf16[2048,1024]{1,0:T(8,128)(2,1)} %constant.17.clone.refs_1_) | copy-start | bytes 12582916
  33.4 18.2 %copy-start.4 = (bf16[2048,1024]{1,0:T(8,128)(2,1)S(1)}, bf16[2048,1024]{1,0:T(8,128)(2,1)}, u32[]{:S(2)}) copy-start(bf16[2048,1024]{1,0:T(8,128)(2,1)} %constant.16.clone.refs_0_) | copy-start | bytes 12582916
  51.6 8.8 %copy-start.5 = (bf16[512,1024]{1,0:T(8,128)(2,1)S(1)}, bf16[512,1024]{1,0:T(8,128)(2,1)}, u32[]{:S(2)}) copy-start(bf16[512,1024]{1,0:T(8,128)(2,1)} %constant.15.clone.table) | copy-start | bytes 3145732
  53.0 5.1 %collective-permute-start.3 = (bf16[128,256]{1,0:T(8,128)(2,1)S(1)}, bf16[128,256]{1,0:T(8,128)(2,1)S(1)}, u32[]{:S(2)}, u32[]{:S(2)}) collective-permute-start(bf16[128,256]{1,0:T(8,128)(2,1)S(1)} %get-tuple-element.26), channel_id=1, source_target_pairs={{0,1},{1,2},{2,3},{3,0},{4,5},{5,6},{6,7},{7,4},{8,9},{9,10},{10,1... | collective-permute-start | bytes 196616 | tf_op jit(solution)/shard_map/ppermute | solution.py:295
  53.1 7.2 %collective-permute-start.4 = (bf16[128,256]{1,0:T(8,128)(2,1)S(1)}, bf16[128,256]{1,0:T(8,128)(2,1)S(1)}, u32[]{:S(2)}, u32[]{:S(2)}) collective-permute-start(bf16[128,256]{1,0:T(8,128)(2,1)S(1)} %get-tuple-element.27), channel_id=1, source_target_pairs={{0,2},{1,3},{2,0},{3,1},{4,6},{5,7},{6,4},{7,5},{8,10},{9,11},{10,... | collective-permute-start | bytes 196616 | tf_op jit(solution)/shard_map/ppermute | solution.py:295
  56.6 3.8 %collective-permute-start.5 = (bf16[128,256]{1,0:T(8,128)(2,1)S(1)}, bf16[128,256]{1,0:T(8,128)(2,1)S(1)}, u32[]{:S(2)}, u32[]{:S(2)}) collective-permute-start(bf16[128,256]{1,0:T(8,128)(2,1)S(1)} %get-tuple-element.28), channel_id=1, source_target_pairs={{0,3},{1,0},{2,1},{3,2},{4,7},{5,4},{6,5},{7,6},{8,11},{9,8},{10,9... | collective-permute-start | bytes 196616 | tf_op jit(solution)/shard_map/ppermute | solution.py:295

commit v5 on v4

--- a/solution.py
+++ b/solution.py
@@ -24,6 +24,7 @@
 PIECES = 4
 CHUNK = 256
 GROUP = 4
+ORDER = (0, 2, 1, 3)
 COST = pl.CostEstimate(flops=2 * 10**10, bytes_accessed=2**24, transcendentals=0)
 
 
@@ -178,8 +179,8 @@
         other = jnp.concatenate(second_rows, axis=0)
         left[:S, at] = picked.astype(BF)
         left[S:, at] = other.astype(BF)
-        left_by_slot[at] = picked.T.astype(BF)
-        left_by_slot[VIS + begin : VIS + begin + CHUNK] = other.T.astype(BF)
+        left_by_slot[2 * begin : 2 * begin + CHUNK] = picked.T.astype(BF)
+        left_by_slot[2 * begin + CHUNK : 2 * begin + 2 * CHUNK] = other.T.astype(BF)
         right = dot(right_tab[...], jnp.where(cell == second, 1.0, 0.0).astype(BF))
         base[:, at] = right[0:128] + right[128:256]
         for y in range(8):
@@ -227,17 +228,17 @@
             turned_real = resid_real * er + resid_imag * ei
             turned_imag = resid_imag * er - resid_real * ei
             here = slice(y * W, (y + 1) * W)
-            weighted[here, at] = (turned_real * base_real + turned_imag * base_imag).astype(BF)
-            weighted[here, VIS + begin : VIS + begin + CHUNK] = (
+            weighted[here, 2 * begin : 2 * begin + CHUNK] = (
+                turned_real * base_real + turned_imag * base_imag
+            ).astype(BF)
+            weighted[here, 2 * begin + CHUNK : 2 * begin + 2 * CHUNK] = (
                 turned_imag * base_real - turned_real * base_imag
             ).astype(BF)
     scale = 1.0 / math.sqrt(VIS)
-    for y0 in range(0, 8, GROUP):
-        both = dot(weighted[y0 * W : (y0 + GROUP) * W], left_by_slot[...])
-        for y in range(y0, y0 + GROUP):
-            for x in range(4):
-                block = both[(y - y0) * W : (y - y0 + 1) * W, x * 128 : (x + 1) * 128]
-                out[x * 8 + y] = (block * scale).astype(BF)
+    both = dot(weighted[...], left_by_slot[...]) * scale
+    for y in range(8):
+        for x in range(4):
+            out[x * 8 + y] = both[y * W : (y + 1) * W, x * 128 : (x + 1) * 128].astype(BF)
 
 
 def back_kernel(returned, *refs):
@@ -262,7 +263,7 @@
     out, held, wide, left = refs[N_COL:]
     copies = []
     for part in range(2):
-        for shift, strip in enumerate(strips):
+        for shift, strip in zip(ORDER, strips):
             block = strip[...].astype(F32)
             if part == 1:
                 block = jnp.concatenate([block[W:], -block[:W]], axis=0)
@@ -294,6 +295,10 @@
         route = [(i, (i + shift) % N_COL) for i in range(N_COL)]
         arrived[shift] = lax.ppermute(parts[shift], "col", route)
     return arrived
+
+
+def in_order(parts):
+    return [parts[shift] for shift in ORDER]
 
 
 def shaped(*dims, dtype=BF):
@@ -382,7 +387,7 @@
         compiler_params=params(),
         cost_estimate=COST,
         name="image",
-    )(by_column, *along_columns(back))
+    )(by_column, *in_order(along_columns(back)))
 
 
 def solution(mesh):

time: 62.3 us -> 61.9 us (level)
  waiting for transfers between devices: 3.78 us -> 2.9 us
    ppermute x6, waiting for transfers between devices: 3.78 us -> 2.9 us  [along_columns(): arrived[shift] = lax.ppermute(parts[shift], 'col', route)]
where the time goes in v5:
time: 61.9 us; the launch traced here: 61.7 us
  blocking collectives  36.3 us (59%)
  Pallas kernels  12.4 us (20%)
  starting transfers between devices  9.92 us (16%)
  waiting for transfers between devices  2.9 us (5%)
    all_to_all x1, blocking collectives, on_device(): lax.all_to_all(windows, FACET, split_axis=0, concat_axis=0, tiled=True)  21.3 us
    all_to_all x1, blocking collectives, on_device(): lax.all_to_all(returned, FACET, split_axis=0, concat_axis=0, tiled=True)  15 us
    ppermute x6, starting transfers between devices, along_columns(): arrived[shift] = lax.ppermute(parts[shift], 'col', route)  9.92 us
    pallas_call x1, Pallas kernels, on_device(): pl.pallas_call(subgrid_kernel, out_shape=shaped(SUBCOL, W, 128), in_specs...  3.06 us
    ppermute x6, waiting for transfers between devices, along_columns(): arrived[shift] = lax.ppermute(parts[shift], 'col', route)  2.9 us
    pallas_call x1, Pallas kernels, on_device(): pl.pallas_call(wave_kernel, out_shape=[shaped(2 * S, VIS), shaped(2 * VIS...  2.4 us
    pallas_call x1, Pallas kernels, on_device(): pl.pallas_call(strip_kernel, out_shape=[shaped(128, 256)] * N_COL, in_spe...  2.3 us
    pallas_call x1, Pallas kernels, on_device(): pl.pallas_call(image_kernel, out_shape=shaped(2, 256, F, dtype=F32), in_s...  1.82 us
  transfers between devices with their start and end apart: 6, of which 2 were waited for; matrix products, arithmetic and copies ran while one was open for 0% of the time, Pallas kernels for 4%

profile of v5, /device:TPU:1, one launch (start us, length us, event | category | flops | bytes accessed | tf_op | source)
XLA Modules:
  0.0 61.7 jit_solution(11725011187331059974)
XLA Ops:
  0.0 0.0 copy-start.6
  0.0 0.0 copy-start.7
  0.0 0.0 copy-start.8
  0.0 0.0 copy-start
  0.0 2.3 %strip.1 = (bf16[128,256]{1,0:T(8,128)(2,1)S(1)}, bf16[128,256]{1,0:T(8,128)(2,1)S(1)}, bf16[128,256]{1,0:T(8,128)(2,1)S(1)}, bf16[128,256]{1,0:T(8,128)(2,1)S(1)}) custom-call(bf16[2,256,1024]{2,1,0:T(8,128)(2,1)} %pixels.1, bf16[512,1024]{1,0:T(8,128)(2,1)} %constant.15.clone.table), custom_call_target="tpu_custom_call" | custom-call | flops 20000000000 | bytes 16777216 | tf_op jit(solution)/shard_map/strip/pallas_call | solution.py:313
  2.3 2.2 %collective-permute-start = (bf16[128,256]{1,0:T(8,128)(2,1)S(1)}, bf16[128,256]{1,0:T(8,128)(2,1)S(1)}, u32[]{:S(2)}, u32[]{:S(2)}) collective-permute-start(bf16[128,256]{1,0:T(8,128)(2,1)S(1)} %get-tuple-element.19), channel_id=1, source_target_pairs={{0,1},{1,2},{2,3},{3,0},{4,5},{5,6},{6,7},{7,4},{8,9},{9,10},{10,1... | collective-permute-start | bytes 196616 | tf_op jit(solution)/shard_map/ppermute | solution.py:296
  4.5 2.6 %collective-permute-start.1 = (bf16[128,256]{1,0:T(8,128)(2,1)S(1)}, bf16[128,256]{1,0:T(8,128)(2,1)S(1)}, u32[]{:S(2)}, u32[]{:S(2)}) collective-permute-start(bf16[128,256]{1,0:T(8,128)(2,1)S(1)} %get-tuple-element.20), channel_id=1, source_target_pairs={{0,2},{1,3},{2,0},{3,1},{4,6},{5,7},{6,4},{7,5},{8,10},{9,11},{10,... | collective-permute-start | bytes 196616 | tf_op jit(solution)/shard_map/ppermute | solution.py:296
  7.1 0.0 slice-start
  7.1 0.0 slice-start.1
  7.1 1.1 %collective-permute-start.2 = (bf16[128,256]{1,0:T(8,128)(2,1)S(1)}, bf16[128,256]{1,0:T(8,128)(2,1)S(1)}, u32[]{:S(2)}, u32[]{:S(2)}) collective-permute-start(bf16[128,256]{1,0:T(8,128)(2,1)S(1)} %get-tuple-element.21), channel_id=1, source_target_pairs={{0,3},{1,0},{2,1},{3,2},{4,7},{5,4},{6,5},{7,6},{8,11},{9,8},{10,9... | collective-permute-start | bytes 196616 | tf_op jit(solution)/shard_map/ppermute | solution.py:296
  8.2 0.0 copy-done.6
  8.2 0.0 copy-done.7
  8.2 0.0 copy-done.8
  8.2 0.0 copy-done
  8.2 2.4 %wave.1 = (bf16[1024,1024]{1,0:T(8,128)(2,1)S(1)}, bf16[2048,512]{1,0:T(8,128)(2,1)S(1)}, f32[128,1024]{1,0:T(8,128)S(1)}, f32[16,1024]{1,0:T(8,128)S(1)}) custom-call(f32[2,64]{1,0:T(2,128)S(1)} %copy-done.8, s32[2,32,1024]{2,1,0:T(8,128)S(1)} %copy-done, bf16[1024,512]{1,0:T(8,128)(2,1)S(1)} %copy-done.6, bf16[288,512]{1,0:T(8,128)(2,1)S(1)} %copy-done.7), custom_call_target="tpu_custom_call" | custom-call | flops 20000000000 | bytes 16777216 | tf_op jit(solution)/shard_map/wave/pallas_call | solution.py:331
  10.6 0.0 collective-permute-done.refs_1_
  10.6 0.0 collective-permute-done.1.refs_2_
  10.7 0.0 collective-permute-done.2.refs_3_
  10.7 0.0 slice-done
  10.7 0.0 slice-done.1
  10.7 0.0 copy-start.1
  10.7 0.0 copy-start.2
  10.7 1.4 %window.1 = bf16[32,64,128]{2,1,0:T(8,128)(2,1)S(1)} custom-call(bf16[1024,4096]{1,0:T(8,128)(2,1)S(1)} %bitcast.1, f32[16,1024]{1,0:T(8,128)S(1)} %get-tuple-element.17.after.eighth, bf16[128,256]{1,0:T(8,128)(2,1)S(1)} %get-tuple-element.18.refs_0_, bf16[128,256]{1,0:T(8,128)(2,1)S(1)} %collective-permute-done.refs_1_, ...), custom_call_target="tpu_custom_call" | custom-call | flops 20000000000 | bytes 16777216 | tf_op jit(solution)/shard_map/window/pallas_call | solution.py:345
  12.1 21.3 %all_to_all.10.windows = bf16[32,64,128]{2,1,0:T(8,128)(2,1)S(1)} all-to-all(bf16[32,64,128]{2,1,0:T(8,128)(2,1)S(1)} %window.1), channel_id=1, replica_groups=mesh['facet_0'=4,'facet_1'=4,'facet_2'=2,'col'=4] {'facet_0','facet_1','..., dimensions={0} | all-to-all | bytes 1048576 | tf_op jit(solution)/shard_map/all_to_all | solution.py:355
  33.4 0.0 copy-done.1
  33.4 0.0 copy-done.2
  33.4 0.0 copy-start.3
  33.4 0.0 copy-start.4
  33.4 3.1 %subgrid.1 = bf16[32,64,128]{2,1,0:T(8,128)(2,1)S(1)} custom-call(s32[32]{0:T(128)S(1)} %copy-done.2, bf16[32,64,128]{2,1,0:T(8,128)(2,1)S(1)} %all_to_all.10.windows, f32[2,32,1024]{2,1,0:T(8,128)S(1)} %copy-done.1, bf16[1024,1024]{1,0:T(8,128)(2,1)S(1)} %get-tuple-element.22.left, bf16[2048,512]{1,0:T(8,128)(2,1)S(1)} %get-tuple-element.23.left_by_slot, ...), custom_call_target="tpu_custom_call" | custom-call | flops 20000000000 | bytes 16777216 | tf_op jit(solution)/shard_map/subgrid/pallas_call | solution.py:356
  36.5 15.0 %all_to_all.11.returned = bf16[32,64,128]{2,1,0:T(8,128)(2,1)S(1)} all-to-all(bf16[32,64,128]{2,1,0:T(8,128)(2,1)S(1)} %subgrid.1), channel_id=1, replica_groups=mesh['facet_0'=4,'facet_1'=4,'facet_2'=2,'col'=4] {'facet_0','facet_1','..., dimensions={0} | all-to-all | bytes 1048576 | tf_op jit(solution)/shard_map/all_to_all | solution.py:366
  51.5 0.0 copy-done.3
  51.5 0.0 copy-done.4
  51.5 0.0 copy-start.5
  51.5 1.4 %back.1 = (bf16[128,256]{1,0:T(8,128)(2,1)S(1)}, bf16[128,256]{1,0:T(8,128)(2,1)S(1)}, bf16[128,256]{1,0:T(8,128)(2,1)S(1)}, bf16[128,256]{1,0:T(8,128)(2,1)S(1)}) custom-call(bf16[32,64,128]{2,1,0:T(8,128)(2,1)S(1)} %all_to_all.11.returned, bf16[2048,1024]{1,0:T(8,128)(2,1)S(1)} %copy-done.4, bf16[2048,1024]{1,0:T(8,128)(2,1)S(1)} %copy-done.3), custom_call_target="tpu_custom_call" | custom-call | flops 20000000000 | bytes 16777216 | tf_op jit(solution)/shard_map/back/pallas_call | solution.py:367
  53.0 1.3 %collective-permute-start.3 = (bf16[128,256]{1,0:T(8,128)(2,1)S(1)}, bf16[128,256]{1,0:T(8,128)(2,1)S(1)}, u32[]{:S(2)}, u32[]{:S(2)}) collective-permute-start(bf16[128,256]{1,0:T(8,128)(2,1)S(1)} %get-tuple-element.26), channel_id=1, source_target_pairs={{0,2},{1,3},{2,0},{3,1},{4,6},{5,7},{6,4},{7,5},{8,10},{9,11},{10,... | collective-permute-start | bytes 196616 | tf_op jit(solution)/shard_map/ppermute | solution.py:296
  54.3 1.6 %collective-permute-start.4 = (bf16[128,256]{1,0:T(8,128)(2,1)S(1)}, bf16[128,256]{1,0:T(8,128)(2,1)S(1)}, u32[]{:S(2)}, u32[]{:S(2)}) collective-permute-start(bf16[128,256]{1,0:T(8,128)(2,1)S(1)} %get-tuple-element.27), channel_id=1, source_target_pairs={{0,1},{1,2},{2,3},{3,0},{4,5},{5,6},{6,7},{7,4},{8,9},{9,10},{10,1... | collective-permute-start | bytes 196616 | tf_op jit(solution)/shard_map/ppermute | solution.py:296
  55.9 1.1 %collective-permute-start.5 = (bf16[128,256]{1,0:T(8,128)(2,1)S(1)}, bf16[128,256]{1,0:T(8,128)(2,1)S(1)}, u32[]{:S(2)}, u32[]{:S(2)}) collective-permute-start(bf16[128,256]{1,0:T(8,128)(2,1)S(1)} %get-tuple-element.28), channel_id=1, source_target_pairs={{0,3},{1,0},{2,1},{3,2},{4,7},{5,4},{6,5},{7,6},{8,11},{9,8},{10,9... | collective-permute-start | bytes 196616 | tf_op jit(solution)/shard_map/ppermute | solution.py:296
  57.0 1.4 %collective-permute-done.3.refs_1_ = bf16[128,256]{1,0:T(8,128)(2,1)S(1)} collective-permute-done((bf16[128,256]{1,0:T(8,128)(2,1)S(1)}, bf16[128,256]{1,0:T(8,128)(2,1)S(1)}, u32[]{:S(2)}, u32[]{:S(2)}) %collective-permute-start.3) | collective-permute-done | bytes 65568 | tf_op jit(solution)/shard_map/ppermute | solution.py:296
  58.4 1.5 %collective-permute-done.4.refs_2_ = bf16[128,256]{1,0:T(8,128)(2,1)S(1)} collective-permute-done((bf16[128,256]{1,0:T(8,128)(2,1)S(1)}, bf16[128,256]{1,0:T(8,128)(2,1)S(1)}, u32[]{:S(2)}, u32[]{:S(2)}) %collective-permute-start.4) | collective-permute-done | bytes 65568 | tf_op jit(solution)/shard_map/ppermute | solution.py:296
  59.9 0.0 collective-permute-done.5.refs_3_
  59.9 0.0 copy-done.5
  59.9 1.8 %image.1 = f32[2,256,1024]{2,1,0:T(8,128)} custom-call(bf16[512,1024]{1,0:T(8,128)(2,1)S(1)} %copy-done.5, bf16[128,256]{1,0:T(8,128)(2,1)S(1)} %get-tuple-element.25.refs_0_, bf16[128,256]{1,0:T(8,128)(2,1)S(1)} %collective-permute-done.3.refs_1_, bf16[128,256]{1,0:T(8,128)(2,1)S(1)} %collective-permute-done.4.refs_2_, ...), custom_call_target="tpu_custom_call" | custom-call | flops 20000000000 | bytes 16777216 | tf_op jit(solution)/shard_map/image/pallas_call | solution.py:377
  (1 shorter events, 0.0 us)
Async XLA Ops:
  0.0 8.2 %copy-start.6 = (bf16[1024,512]{1,0:T(8,128)(2,1)S(1)}, bf16[1024,512]{1,0:T(8,128)(2,1)}, u32[]{:S(2)}) copy-start(bf16[1024,512]{1,0:T(8,128)(2,1)} %constant.18.clone.left_tab) | copy-start | bytes 3145732
  0.0 8.2 %copy-start.7 = (bf16[288,512]{1,0:T(8,128)(2,1)S(1)}, bf16[288,512]{1,0:T(8,128)(2,1)}, u32[]{:S(2)}) copy-start(bf16[288,512]{1,0:T(8,128)(2,1)} %constant.19.clone.right_tab) | copy-start | bytes 884740
  0.0 8.2 %copy-start.8 = (f32[2,64]{1,0:T(2,128)S(1)}, f32[2,64]{1,0:T(2,128)}, u32[]{:S(2)}) copy-start(f32[2,64]{1,0:T(2,128)} %constant.14.clone.units) | copy-start | bytes 1540
  0.0 8.2 %copy-start = (s32[2,32,1024]{2,1,0:T(8,128)S(1)}, s32[2,32,1024]{2,1,0:T(8,128)}, u32[]{:S(2)}) copy-start(s32[2,32,1024]{2,1,0:T(8,128)} %cells.1) | copy-start | bytes 786436
  2.3 8.3 %collective-permute-start = (bf16[128,256]{1,0:T(8,128)(2,1)S(1)}, bf16[128,256]{1,0:T(8,128)(2,1)S(1)}, u32[]{:S(2)}, u32[]{:S(2)}) collective-permute-start(bf16[128,256]{1,0:T(8,128)(2,1)S(1)} %get-tuple-element.19), channel_id=1, source_target_pairs={{0,1},{1,2},{2,3},{3,0},{4,5},{5,6},{6,7},{7,4},{8,9},{9,10},{10,1... | collective-permute-start | bytes 196616 | tf_op jit(solution)/shard_map/ppermute | solution.py:296
  4.5 6.1 %collective-permute-start.1 = (bf16[128,256]{1,0:T(8,128)(2,1)S(1)}, bf16[128,256]{1,0:T(8,128)(2,1)S(1)}, u32[]{:S(2)}, u32[]{:S(2)}) collective-permute-start(bf16[128,256]{1,0:T(8,128)(2,1)S(1)} %get-tuple-element.20), channel_id=1, source_target_pairs={{0,2},{1,3},{2,0},{3,1},{4,6},{5,7},{6,4},{7,5},{8,10},{9,11},{10,... | collective-permute-start | bytes 196616 | tf_op jit(solution)/shard_map/ppermute | solution.py:296
  7.1 3.5 %slice-start = ((s8[8388608]{0:T(1024)(128)(4,1)}), s8[4194304]{0:T(1024)(128)(4,1)S(1)}, s32[]{:S(2)}) async-start(s8[8388608]{0:T(1024)(128)(4,1)} %bitcast), calls=%async_computation.2 | async-start | bytes 8388608
  7.1 3.5 %slice-start.1 = ((s8[8388608]{0:T(1024)(128)(4,1)}), s8[4194304]{0:T(1024)(128)(4,1)S(1)}, s32[]{:S(2)}) async-start(s8[8388608]{0:T(1024)(128)(4,1)} %bitcast), calls=%async_computation.3 | async-start | bytes 8388608
  7.1 3.5 %collective-permute-start.2 = (bf16[128,256]{1,0:T(8,128)(2,1)S(1)}, bf16[128,256]{1,0:T(8,128)(2,1)S(1)}, u32[]{:S(2)}, u32[]{:S(2)}) collective-permute-start(bf16[128,256]{1,0:T(8,128)(2,1)S(1)} %get-tuple-element.21), channel_id=1, source_target_pairs={{0,3},{1,0},{2,1},{3,2},{4,7},{5,4},{6,5},{7,6},{8,11},{9,8},{10,9... | collective-permute-start | bytes 196616 | tf_op jit(solution)/shard_map/ppermute | solution.py:296
  10.7 22.7 %copy-start.1 = (f32[2,32,1024]{2,1,0:T(8,128)S(1)}, f32[2,32,1024]{2,1,0:T(8,128)}, u32[]{:S(2)}) copy-start(f32[2,32,1024]{2,1,0:T(8,128)} %observed.1) | copy-start | bytes 786436
  10.7 22.7 %copy-start.2 = (s32[32]{0:T(128)S(1)}, s32[32]{0:T(128)}, u32[]{:S(2)}) copy-start(s32[32]{0:T(128)} %counts.1) | copy-start | bytes 388
  33.4 18.1 %copy-start.3 = (bf16[2048,1024]{1,0:T(8,128)(2,1)S(1)}, bf16[2048,1024]{1,0:T(8,128)(2,1)}, u32[]{:S(2)}) copy-start(bf16[2048,1024]{1,0:T(8,128)(2,1)} %constant.17.clone.refs_1_) | copy-start | bytes 12582916
  33.4 18.1 %copy-start.4 = (bf16[2048,1024]{1,0:T(8,128)(2,1)S(1)}, bf16[2048,1024]{1,0:T(8,128)(2,1)}, u32[]{:S(2)}) copy-start(bf16[2048,1024]{1,0:T(8,128)(2,1)} %constant.16.clone.refs_0_) | copy-start | bytes 12582916
  51.5 8.4 %copy-start.5 = (bf16[512,1024]{1,0:T(8,128)(2,1)S(1)}, bf16[512,1024]{1,0:T(8,128)(2,1)}, u32[]{:S(2)}) copy-start(bf16[512,1024]{1,0:T(8,128)(2,1)} %constant.15.clone.table) | copy-start | bytes 3145732
  53.0 5.4 %collective-permute-start.3 = (bf16[128,256]{1,0:T(8,128)(2,1)S(1)}, bf16[128,256]{1,0:T(8,128)(2,1)S(1)}, u32[]{:S(2)}, u32[]{:S(2)}) collective-permute-start(bf16[128,256]{1,0:T(8,128)(2,1)S(1)} %get-tuple-element.26), channel_id=1, source_target_pairs={{0,2},{1,3},{2,0},{3,1},{4,6},{5,7},{6,4},{7,5},{8,10},{9,11},{10,... | collective-permute-start | bytes 196616 | tf_op jit(solution)/shard_map/ppermute | solution.py:296
  54.3 5.6 %collective-permute-start.4 = (bf16[128,256]{1,0:T(8,128)(2,1)S(1)}, bf16[128,256]{1,0:T(8,128)(2,1)S(1)}, u32[]{:S(2)}, u32[]{:S(2)}) collective-permute-start(bf16[128,256]{1,0:T(8,128)(2,1)S(1)} %get-tuple-element.27), channel_id=1, source_target_pairs={{0,1},{1,2},{2,3},{3,0},{4,5},{5,6},{6,7},{7,4},{8,9},{9,10},{10,1... | collective-permute-start | bytes 196616 | tf_op jit(solution)/shard_map/ppermute | solution.py:296
  55.9 3.9 %collective-permute-start.5 = (bf16[128,256]{1,0:T(8,128)(2,1)S(1)}, bf16[128,256]{1,0:T(8,128)(2,1)S(1)}, u32[]{:S(2)}, u32[]{:S(2)}) collective-permute-start(bf16[128,256]{1,0:T(8,128)(2,1)S(1)} %get-tuple-element.28), channel_id=1, source_target_pairs={{0,3},{1,0},{2,1},{3,2},{4,7},{5,4},{6,5},{7,6},{8,11},{9,8},{10,9... | collective-permute-start | bytes 196616 | tf_op jit(solution)/shard_map/ppermute | solution.py:296

commit v6 on v5

--- a/solution.py
+++ b/solution.py
@@ -159,6 +159,7 @@
     subgrid = lax.axis_index(FACET)
     shift = (37 * subgrid + 5) & 1023
     anchor = (29 * lax.axis_index("col") + 3) & 63
+    scale = 1.0 / math.sqrt(VIS)
     for begin in range(0, VIS, CHUNK):
         at = slice(begin, begin + CHUNK)
         first = cells[0, pl.ds(subgrid, 1), at]
@@ -179,8 +180,8 @@
         other = jnp.concatenate(second_rows, axis=0)
         left[:S, at] = picked.astype(BF)
         left[S:, at] = other.astype(BF)
-        left_by_slot[2 * begin : 2 * begin + CHUNK] = picked.T.astype(BF)
-        left_by_slot[2 * begin + CHUNK : 2 * begin + 2 * CHUNK] = other.T.astype(BF)
+        left_by_slot[2 * begin : 2 * begin + CHUNK] = (picked * scale).T.astype(BF)
+        left_by_slot[2 * begin + CHUNK : 2 * begin + 2 * CHUNK] = (other * scale).T.astype(BF)
         right = dot(right_tab[...], jnp.where(cell == second, 1.0, 0.0).astype(BF))
         base[:, at] = right[0:128] + right[128:256]
         for y in range(8):
@@ -234,8 +235,7 @@
             weighted[here, 2 * begin + CHUNK : 2 * begin + 2 * CHUNK] = (
                 turned_imag * base_real - turned_real * base_imag
             ).astype(BF)
-    scale = 1.0 / math.sqrt(VIS)
-    both = dot(weighted[...], left_by_slot[...]) * scale
+    both = dot(weighted[...], left_by_slot[...])
     for y in range(8):
         for x in range(4):
             out[x * 8 + y] = both[y * W : (y + 1) * W, x * 128 : (x + 1) * 128].astype(BF)

time: 61.9 us -> 61.9 us (level)
  no operation moved by 1% of the time
where the time goes in v6:
time: 61.9 us; the launch traced here: 61.7 us
  blocking collectives  36.3 us (59%)
  Pallas kernels  12.4 us (20%)
  starting transfers between devices  9.92 us (16%)
  waiting for transfers between devices  2.89 us (5%)
    all_to_all x1, blocking collectives, on_device(): lax.all_to_all(windows, FACET, split_axis=0, concat_axis=0, tiled=True)  21.2 us
    all_to_all x1, blocking collectives, on_device(): lax.all_to_all(returned, FACET, split_axis=0, concat_axis=0, tiled=True)  15 us
    ppermute x6, starting transfers between devices, along_columns(): arrived[shift] = lax.ppermute(parts[shift], 'col', route)  9.92 us
    pallas_call x1, Pallas kernels, on_device(): pl.pallas_call(subgrid_kernel, out_shape=shaped(SUBCOL, W, 128), in_specs...  3.05 us
    ppermute x6, waiting for transfers between devices, along_columns(): arrived[shift] = lax.ppermute(parts[shift], 'col', route)  2.89 us
    pallas_call x1, Pallas kernels, on_device(): pl.pallas_call(wave_kernel, out_shape=[shaped(2 * S, VIS), shaped(2 * VIS...  2.47 us
    pallas_call x1, Pallas kernels, on_device(): pl.pallas_call(strip_kernel, out_shape=[shaped(128, 256)] * N_COL, in_spe...  2.3 us
    pallas_call x1, Pallas kernels, on_device(): pl.pallas_call(image_kernel, out_shape=shaped(2, 256, F, dtype=F32), in_s...  1.82 us
  transfers between devices with their start and end apart: 6, of which 2 were waited for; matrix products, arithmetic and copies ran while one was open for 0% of the time, Pallas kernels for 4%

profile of v6, /device:TPU:1, one launch (start us, length us, event | category | flops | bytes accessed | tf_op | source)
XLA Modules:
  0.0 61.7 jit_solution(13390924689683643504)
XLA Ops:
  0.0 0.0 copy-start.6
  0.0 0.0 copy-start.7
  0.0 0.0 copy-start.8
  0.0 0.0 copy-start
  0.0 2.3 %strip.1 = (bf16[128,256]{1,0:T(8,128)(2,1)S(1)}, bf16[128,256]{1,0:T(8,128)(2,1)S(1)}, bf16[128,256]{1,0:T(8,128)(2,1)S(1)}, bf16[128,256]{1,0:T(8,128)(2,1)S(1)}) custom-call(bf16[2,256,1024]{2,1,0:T(8,128)(2,1)} %pixels.1, bf16[512,1024]{1,0:T(8,128)(2,1)} %constant.15.clone.table), custom_call_target="tpu_custom_call" | custom-call | flops 20000000000 | bytes 16777216 | tf_op jit(solution)/shard_map/strip/pallas_call | solution.py:313
  2.3 2.2 %collective-permute-start = (bf16[128,256]{1,0:T(8,128)(2,1)S(1)}, bf16[128,256]{1,0:T(8,128)(2,1)S(1)}, u32[]{:S(2)}, u32[]{:S(2)}) collective-permute-start(bf16[128,256]{1,0:T(8,128)(2,1)S(1)} %get-tuple-element.19), channel_id=1, source_target_pairs={{0,1},{1,2},{2,3},{3,0},{4,5},{5,6},{6,7},{7,4},{8,9},{9,10},{10,1... | collective-permute-start | bytes 196616 | tf_op jit(solution)/shard_map/ppermute | solution.py:296
  4.5 2.6 %collective-permute-start.1 = (bf16[128,256]{1,0:T(8,128)(2,1)S(1)}, bf16[128,256]{1,0:T(8,128)(2,1)S(1)}, u32[]{:S(2)}, u32[]{:S(2)}) collective-permute-start(bf16[128,256]{1,0:T(8,128)(2,1)S(1)} %get-tuple-element.20), channel_id=1, source_target_pairs={{0,2},{1,3},{2,0},{3,1},{4,6},{5,7},{6,4},{7,5},{8,10},{9,11},{10,... | collective-permute-start | bytes 196616 | tf_op jit(solution)/shard_map/ppermute | solution.py:296
  7.1 0.0 slice-start
  7.1 0.0 slice-start.1
  7.1 1.1 %collective-permute-start.2 = (bf16[128,256]{1,0:T(8,128)(2,1)S(1)}, bf16[128,256]{1,0:T(8,128)(2,1)S(1)}, u32[]{:S(2)}, u32[]{:S(2)}) collective-permute-start(bf16[128,256]{1,0:T(8,128)(2,1)S(1)} %get-tuple-element.21), channel_id=1, source_target_pairs={{0,3},{1,0},{2,1},{3,2},{4,7},{5,4},{6,5},{7,6},{8,11},{9,8},{10,9... | collective-permute-start | bytes 196616 | tf_op jit(solution)/shard_map/ppermute | solution.py:296
  8.2 0.0 copy-done.6
  8.2 0.0 copy-done.7
  8.2 0.0 copy-done.8
  8.2 0.0 copy-done
  8.2 2.5 %wave.1 = (bf16[1024,1024]{1,0:T(8,128)(2,1)S(1)}, bf16[2048,512]{1,0:T(8,128)(2,1)S(1)}, f32[128,1024]{1,0:T(8,128)S(1)}, f32[16,1024]{1,0:T(8,128)S(1)}) custom-call(f32[2,64]{1,0:T(2,128)S(1)} %copy-done.8, s32[2,32,1024]{2,1,0:T(8,128)S(1)} %copy-done, bf16[1024,512]{1,0:T(8,128)(2,1)S(1)} %copy-done.6, bf16[288,512]{1,0:T(8,128)(2,1)S(1)} %copy-done.7), custom_call_target="tpu_custom_call" | custom-call | flops 20000000000 | bytes 16777216 | tf_op jit(solution)/shard_map/wave/pallas_call | solution.py:331
  10.7 0.0 collective-permute-done.refs_1_
  10.7 0.0 collective-permute-done.1.refs_2_
  10.7 0.0 collective-permute-done.2.refs_3_
  10.7 0.0 slice-done
  10.7 0.0 slice-done.1
  10.8 0.0 copy-start.1
  10.8 0.0 copy-start.2
  10.8 1.4 %window.1 = bf16[32,64,128]{2,1,0:T(8,128)(2,1)S(1)} custom-call(bf16[1024,4096]{1,0:T(8,128)(2,1)S(1)} %bitcast.1, f32[16,1024]{1,0:T(8,128)S(1)} %get-tuple-element.17.after.eighth, bf16[128,256]{1,0:T(8,128)(2,1)S(1)} %get-tuple-element.18.refs_0_, bf16[128,256]{1,0:T(8,128)(2,1)S(1)} %collective-permute-done.refs_1_, ...), custom_call_target="tpu_custom_call" | custom-call | flops 20000000000 | bytes 16777216 | tf_op jit(solution)/shard_map/window/pallas_call | solution.py:345
  12.2 21.2 %all_to_all.10.windows = bf16[32,64,128]{2,1,0:T(8,128)(2,1)S(1)} all-to-all(bf16[32,64,128]{2,1,0:T(8,128)(2,1)S(1)} %window.1), channel_id=1, replica_groups=mesh['facet_0'=4,'facet_1'=4,'facet_2'=2,'col'=4] {'facet_0','facet_1','..., dimensions={0} | all-to-all | bytes 1048576 | tf_op jit(solution)/shard_map/all_to_all | solution.py:355
  33.4 0.0 copy-done.1
  33.4 0.0 copy-done.2
  33.4 0.0 copy-start.3
  33.4 0.0 copy-start.4
  33.4 3.1 %subgrid.1 = bf16[32,64,128]{2,1,0:T(8,128)(2,1)S(1)} custom-call(s32[32]{0:T(128)S(1)} %copy-done.2, bf16[32,64,128]{2,1,0:T(8,128)(2,1)S(1)} %all_to_all.10.windows, f32[2,32,1024]{2,1,0:T(8,128)S(1)} %copy-done.1, bf16[1024,1024]{1,0:T(8,128)(2,1)S(1)} %get-tuple-element.22.left, bf16[2048,512]{1,0:T(8,128)(2,1)S(1)} %get-tuple-element.23.left_by_slot, ...), custom_call_target="tpu_custom_call" | custom-call | flops 20000000000 | bytes 16777216 | tf_op jit(solution)/shard_map/subgrid/pallas_call | solution.py:356
  36.5 15.0 %all_to_all.11.returned = bf16[32,64,128]{2,1,0:T(8,128)(2,1)S(1)} all-to-all(bf16[32,64,128]{2,1,0:T(8,128)(2,1)S(1)} %subgrid.1), channel_id=1, replica_groups=mesh['facet_0'=4,'facet_1'=4,'facet_2'=2,'col'=4] {'facet_0','facet_1','..., dimensions={0} | all-to-all | bytes 1048576 | tf_op jit(solution)/shard_map/all_to_all | solution.py:366
  51.5 0.0 copy-done.3
  51.5 0.0 copy-done.4
  51.5 0.0 copy-start.5
  51.5 1.4 %back.1 = (bf16[128,256]{1,0:T(8,128)(2,1)S(1)}, bf16[128,256]{1,0:T(8,128)(2,1)S(1)}, bf16[128,256]{1,0:T(8,128)(2,1)S(1)}, bf16[128,256]{1,0:T(8,128)(2,1)S(1)}) custom-call(bf16[32,64,128]{2,1,0:T(8,128)(2,1)S(1)} %all_to_all.11.returned, bf16[2048,1024]{1,0:T(8,128)(2,1)S(1)} %copy-done.4, bf16[2048,1024]{1,0:T(8,128)(2,1)S(1)} %copy-done.3), custom_call_target="tpu_custom_call" | custom-call | flops 20000000000 | bytes 16777216 | tf_op jit(solution)/shard_map/back/pallas_call | solution.py:367
  53.0 1.3 %collective-permute-start.3 = (bf16[128,256]{1,0:T(8,128)(2,1)S(1)}, bf16[128,256]{1,0:T(8,128)(2,1)S(1)}, u32[]{:S(2)}, u32[]{:S(2)}) collective-permute-start(bf16[128,256]{1,0:T(8,128)(2,1)S(1)} %get-tuple-element.26), channel_id=1, source_target_pairs={{0,2},{1,3},{2,0},{3,1},{4,6},{5,7},{6,4},{7,5},{8,10},{9,11},{10,... | collective-permute-start | bytes 196616 | tf_op jit(solution)/shard_map/ppermute | solution.py:296
  54.3 1.6 %collective-permute-start.4 = (bf16[128,256]{1,0:T(8,128)(2,1)S(1)}, bf16[128,256]{1,0:T(8,128)(2,1)S(1)}, u32[]{:S(2)}, u32[]{:S(2)}) collective-permute-start(bf16[128,256]{1,0:T(8,128)(2,1)S(1)} %get-tuple-element.27), channel_id=1, source_target_pairs={{0,1},{1,2},{2,3},{3,0},{4,5},{5,6},{6,7},{7,4},{8,9},{9,10},{10,1... | collective-permute-start | bytes 196616 | tf_op jit(solution)/shard_map/ppermute | solution.py:296
  55.9 1.1 %collective-permute-start.5 = (bf16[128,256]{1,0:T(8,128)(2,1)S(1)}, bf16[128,256]{1,0:T(8,128)(2,1)S(1)}, u32[]{:S(2)}, u32[]{:S(2)}) collective-permute-start(bf16[128,256]{1,0:T(8,128)(2,1)S(1)} %get-tuple-element.28), channel_id=1, source_target_pairs={{0,3},{1,0},{2,1},{3,2},{4,7},{5,4},{6,5},{7,6},{8,11},{9,8},{10,9... | collective-permute-start | bytes 196616 | tf_op jit(solution)/shard_map/ppermute | solution.py:296
  57.0 1.4 %collective-permute-done.3.refs_1_ = bf16[128,256]{1,0:T(8,128)(2,1)S(1)} collective-permute-done((bf16[128,256]{1,0:T(8,128)(2,1)S(1)}, bf16[128,256]{1,0:T(8,128)(2,1)S(1)}, u32[]{:S(2)}, u32[]{:S(2)}) %collective-permute-start.3) | collective-permute-done | bytes 65568 | tf_op jit(solution)/shard_map/ppermute | solution.py:296
  58.4 1.5 %collective-permute-done.4.refs_2_ = bf16[128,256]{1,0:T(8,128)(2,1)S(1)} collective-permute-done((bf16[128,256]{1,0:T(8,128)(2,1)S(1)}, bf16[128,256]{1,0:T(8,128)(2,1)S(1)}, u32[]{:S(2)}, u32[]{:S(2)}) %collective-permute-start.4) | collective-permute-done | bytes 65568 | tf_op jit(solution)/shard_map/ppermute | solution.py:296
  59.9 0.0 collective-permute-done.5.refs_3_
  59.9 0.0 copy-done.5
  59.9 1.8 %image.1 = f32[2,256,1024]{2,1,0:T(8,128)} custom-call(bf16[512,1024]{1,0:T(8,128)(2,1)S(1)} %copy-done.5, bf16[128,256]{1,0:T(8,128)(2,1)S(1)} %get-tuple-element.25.refs_0_, bf16[128,256]{1,0:T(8,128)(2,1)S(1)} %collective-permute-done.3.refs_1_, bf16[128,256]{1,0:T(8,128)(2,1)S(1)} %collective-permute-done.4.refs_2_, ...), custom_call_target="tpu_custom_call" | custom-call | flops 20000000000 | bytes 16777216 | tf_op jit(solution)/shard_map/image/pallas_call | solution.py:377
  (1 shorter events, 0.0 us)
Async XLA Ops:
  0.0 8.2 %copy-start.6 = (bf16[1024,512]{1,0:T(8,128)(2,1)S(1)}, bf16[1024,512]{1,0:T(8,128)(2,1)}, u32[]{:S(2)}) copy-start(bf16[1024,512]{1,0:T(8,128)(2,1)} %constant.18.clone.left_tab) | copy-start | bytes 3145732
  0.0 8.2 %copy-start.7 = (bf16[288,512]{1,0:T(8,128)(2,1)S(1)}, bf16[288,512]{1,0:T(8,128)(2,1)}, u32[]{:S(2)}) copy-start(bf16[288,512]{1,0:T(8,128)(2,1)} %constant.19.clone.right_tab) | copy-start | bytes 884740
  0.0 8.2 %copy-start.8 = (f32[2,64]{1,0:T(2,128)S(1)}, f32[2,64]{1,0:T(2,128)}, u32[]{:S(2)}) copy-start(f32[2,64]{1,0:T(2,128)} %constant.14.clone.units) | copy-start | bytes 1540
  0.0 8.2 %copy-start = (s32[2,32,1024]{2,1,0:T(8,128)S(1)}, s32[2,32,1024]{2,1,0:T(8,128)}, u32[]{:S(2)}) copy-start(s32[2,32,1024]{2,1,0:T(8,128)} %cells.1) | copy-start | bytes 786436
  2.3 8.4 %collective-permute-start = (bf16[128,256]{1,0:T(8,128)(2,1)S(1)}, bf16[128,256]{1,0:T(8,128)(2,1)S(1)}, u32[]{:S(2)}, u32[]{:S(2)}) collective-permute-start(bf16[128,256]{1,0:T(8,128)(2,1)S(1)} %get-tuple-element.19), channel_id=1, source_target_pairs={{0,1},{1,2},{2,3},{3,0},{4,5},{5,6},{6,7},{7,4},{8,9},{9,10},{10,1... | collective-permute-start | bytes 196616 | tf_op jit(solution)/shard_map/ppermute | solution.py:296
  4.5 6.2 %collective-permute-start.1 = (bf16[128,256]{1,0:T(8,128)(2,1)S(1)}, bf16[128,256]{1,0:T(8,128)(2,1)S(1)}, u32[]{:S(2)}, u32[]{:S(2)}) collective-permute-start(bf16[128,256]{1,0:T(8,128)(2,1)S(1)} %get-tuple-element.20), channel_id=1, source_target_pairs={{0,2},{1,3},{2,0},{3,1},{4,6},{5,7},{6,4},{7,5},{8,10},{9,11},{10,... | collective-permute-start | bytes 196616 | tf_op jit(solution)/shard_map/ppermute | solution.py:296
  7.1 3.6 %slice-start = ((s8[8388608]{0:T(1024)(128)(4,1)}), s8[4194304]{0:T(1024)(128)(4,1)S(1)}, s32[]{:S(2)}) async-start(s8[8388608]{0:T(1024)(128)(4,1)} %bitcast), calls=%async_computation.2 | async-start | bytes 8388608
  7.1 3.6 %slice-start.1 = ((s8[8388608]{0:T(1024)(128)(4,1)}), s8[4194304]{0:T(1024)(128)(4,1)S(1)}, s32[]{:S(2)}) async-start(s8[8388608]{0:T(1024)(128)(4,1)} %bitcast), calls=%async_computation.3 | async-start | bytes 8388608
  7.1 3.6 %collective-permute-start.2 = (bf16[128,256]{1,0:T(8,128)(2,1)S(1)}, bf16[128,256]{1,0:T(8,128)(2,1)S(1)}, u32[]{:S(2)}, u32[]{:S(2)}) collective-permute-start(bf16[128,256]{1,0:T(8,128)(2,1)S(1)} %get-tuple-element.21), channel_id=1, source_target_pairs={{0,3},{1,0},{2,1},{3,2},{4,7},{5,4},{6,5},{7,6},{8,11},{9,8},{10,9... | collective-permute-start | bytes 196616 | tf_op jit(solution)/shard_map/ppermute | solution.py:296
  10.8 22.6 %copy-start.1 = (f32[2,32,1024]{2,1,0:T(8,128)S(1)}, f32[2,32,1024]{2,1,0:T(8,128)}, u32[]{:S(2)}) copy-start(f32[2,32,1024]{2,1,0:T(8,128)} %observed.1) | copy-start | bytes 786436
  10.8 22.6 %copy-start.2 = (s32[32]{0:T(128)S(1)}, s32[32]{0:T(128)}, u32[]{:S(2)}) copy-start(s32[32]{0:T(128)} %counts.1) | copy-start | bytes 388
  33.4 18.1 %copy-start.3 = (bf16[2048,1024]{1,0:T(8,128)(2,1)S(1)}, bf16[2048,1024]{1,0:T(8,128)(2,1)}, u32[]{:S(2)}) copy-start(bf16[2048,1024]{1,0:T(8,128)(2,1)} %constant.17.clone.refs_1_) | copy-start | bytes 12582916
  33.4 18.1 %copy-start.4 = (bf16[2048,1024]{1,0:T(8,128)(2,1)S(1)}, bf16[2048,1024]{1,0:T(8,128)(2,1)}, u32[]{:S(2)}) copy-start(bf16[2048,1024]{1,0:T(8,128)(2,1)} %constant.16.clone.refs_0_) | copy-start | bytes 12582916
  51.5 8.4 %copy-start.5 = (bf16[512,1024]{1,0:T(8,128)(2,1)S(1)}, bf16[512,1024]{1,0:T(8,128)(2,1)}, u32[]{:S(2)}) copy-start(bf16[512,1024]{1,0:T(8,128)(2,1)} %constant.15.clone.table) | copy-start | bytes 3145732
  53.0 5.4 %collective-permute-start.3 = (bf16[128,256]{1,0:T(8,128)(2,1)S(1)}, bf16[128,256]{1,0:T(8,128)(2,1)S(1)}, u32[]{:S(2)}, u32[]{:S(2)}) collective-permute-start(bf16[128,256]{1,0:T(8,128)(2,1)S(1)} %get-tuple-element.26), channel_id=1, source_target_pairs={{0,2},{1,3},{2,0},{3,1},{4,6},{5,7},{6,4},{7,5},{8,10},{9,11},{10,... | collective-permute-start | bytes 196616 | tf_op jit(solution)/shard_map/ppermute | solution.py:296
  54.3 5.6 %collective-permute-start.4 = (bf16[128,256]{1,0:T(8,128)(2,1)S(1)}, bf16[128,256]{1,0:T(8,128)(2,1)S(1)}, u32[]{:S(2)}, u32[]{:S(2)}) collective-permute-start(bf16[128,256]{1,0:T(8,128)(2,1)S(1)} %get-tuple-element.27), channel_id=1, source_target_pairs={{0,1},{1,2},{2,3},{3,0},{4,5},{5,6},{6,7},{7,4},{8,9},{9,10},{10,1... | collective-permute-start | bytes 196616 | tf_op jit(solution)/shard_map/ppermute | solution.py:296
  55.9 3.9 %collective-permute-start.5 = (bf16[128,256]{1,0:T(8,128)(2,1)S(1)}, bf16[128,256]{1,0:T(8,128)(2,1)S(1)}, u32[]{:S(2)}, u32[]{:S(2)}) collective-permute-start(bf16[128,256]{1,0:T(8,128)(2,1)S(1)} %get-tuple-element.28), channel_id=1, source_target_pairs={{0,3},{1,0},{2,1},{3,2},{4,7},{5,4},{6,5},{7,6},{8,11},{9,8},{10,9... | collective-permute-start | bytes 196616 | tf_op jit(solution)/shard_map/ppermute | solution.py:296
